TPU v7x, 32 devices: a whole 2x2x4 slice. The times are simulated.
32 devices in a mesh: ctx: 8 (over y, x, core), fsdp: 4 (over z).
Axes of the slice: x: 2, y: 2, z: 4, core: 2. Of those that a mesh axis runs over, the one named last changes fastest.
Arguments:
- tokens: bfloat16 [4, 2048, 1600], P('fsdp', 'ctx'), may hold values from -6 to 6
- cotangent: bfloat16 [4, 2048, 1600], P('fsdp', 'ctx'), may hold values from -6 to 6
- unit_order: int32 [4, 16], P('fsdp'), may hold values from 0 to 15, as said below
- block_seq: int32 [4, 8], P('fsdp'), may hold values from 0 to 1, as said below
- meta_tokens: bfloat16 [128, 1600], P('fsdp', 'ctx'), may hold values from -6 to 6
- input_gain: bfloat16 [1600], P('ctx'), may hold values from 0.5 to 1.5
- query_key_value_weight: bfloat16 [1600, 2240], P('fsdp', 'ctx'), may hold values from -0.15625 to 0.15625
- w_xz: bfloat16 [1600, 6400], P('fsdp', 'ctx'), may hold values from -0.15625 to 0.15625
- conv_kernel: bfloat16 [4, 3200], P('fsdp', 'ctx'), may hold values from -3 to 3
- state_proj: bfloat16 [132, 3200], P('fsdp', 'ctx'), may hold values from -0.109375 to 0.109375
- step_proj: bfloat16 [100, 3200], P('fsdp', 'ctx'), may hold values from -0.625 to 0.625
- step_bias: bfloat16 [3200], P('ctx'), may hold values from -9 to -2.5
- decay_log: bfloat16 [16, 3200], P('fsdp', 'ctx'), may hold values from -2 to 2
- skip_gain: bfloat16 [3200], P('ctx'), may hold values from 0.5 to 1.5
- attn_gain: bfloat16 [1600], P('ctx'), may hold values from 0.5 to 1.5
- ssm_gain: bfloat16 [3200], P('ctx'), may hold values from 0.5 to 1.5
- out_proj: bfloat16 [4800, 1600], P('fsdp', 'ctx'), may hold values from -0.1875 to 0.1875
- ffn_gain: bfloat16 [1600], P('ctx'), may hold values from 0.5 to 1.5
- w_gate: bfloat16 [1600, 5504], P('fsdp', 'ctx'), may hold values from -0.15625 to 0.15625
- w_up: bfloat16 [1600, 5504], P('fsdp', 'ctx'), may hold values from -0.15625 to 0.15625
- w_down: bfloat16 [5504, 1600], P('fsdp', 'ctx'), may hold values from -0.15625 to 0.15625
Outputs:
- layer_out: bfloat16 [4, 2048, 1600], P('fsdp', 'ctx')
- tokens_grad: bfloat16 [4, 2048, 1600], P('fsdp', 'ctx')
- meta_grad: float32 [128, 1600], P('fsdp', 'ctx')
- input_gain_grad: float32 [1600], P('ctx')
- qkv_grad: float32 [1600, 2240], P('fsdp', 'ctx')
- xz_grad: float32 [1600, 6400], P('fsdp', 'ctx')
- conv_grad: float32 [4, 3200], P('fsdp', 'ctx')
- state_proj_grad: float32 [132, 3200], P('fsdp', 'ctx')
- step_proj_grad: float32 [100, 3200], P('fsdp', 'ctx')
- step_bias_grad: float32 [3200], P('ctx')
- decay_log_grad: float32 [16, 3200], P('fsdp', 'ctx')
- skip_gain_grad: float32 [3200], P('ctx')
- attn_gain_grad: float32 [1600], P('ctx')
- ssm_gain_grad: float32 [3200], P('ctx')
- out_proj_grad: float32 [4800, 1600], P('fsdp', 'ctx')
- ffn_gain_grad: float32 [1600], P('ctx')
- gate_grad: float32 [1600, 5504], P('fsdp', 'ctx')
- up_grad: float32 [1600, 5504], P('fsdp', 'ctx')
- down_grad: float32 [5504, 1600], P('fsdp', 'ctx')
Inputs may be any that keep to these rules, and one draw needn't show every extreme that they name: `unit_order`: each row is a permutation of 0 to 15; slots 2c and 2c + 1 hold units u and 15 - u for some u. `block_seq`: each row is 0 on its first blocks and 1 on the rest; each value covers 2 or more blocks.
All inputs are finite; a program needn't handle non-finite values.
Results may differ from a plain program's by a relative error of at most 0.02.
Values may be sent and summed in bfloat16 or wider, within the bound.
No kernel may reach another device: no remote copies, remote signals or barrier semaphores. Data moves between devices by JAX's collectives and lax.ppermute only.
A program may use at most 576 MiB of HBM per device.

v0:
```python
import jax
import jax.numpy as jnp
from jax import lax
from jax.sharding import PartitionSpec as P

QUERY_HEADS = 25
KEY_VALUE_HEADS = 5
HEAD_SIZE = 64
INNER = 3200
STATE = 16
CONV = 4
DT_RANK = 100
BLOCK_ROWS = 256
KEYS_BLK = 512


EPS = 1e-06
NEGATIVE_FILL = -1e30
NAMES = (
    "meta",
    "qkv",
    "xz",
    "conv",
    "select",
    "step",
    "decay",
    "out",
    "gate",
    "up",
    "down",
    "gain_in",
    "step_bias",
    "skip",
    "gain_attn",
    "gain_ssm",
    "gain_ffn",
)


def silu(value):
    return value * jax.nn.sigmoid(value)


def silu_slope(value):
    sigma = jax.nn.sigmoid(value)
    return sigma * (1.0 + value * (1.0 - sigma))


def norm_fwd(value, gain):
    factor = lax.rsqrt(jnp.mean(value * value, axis=-1, keepdims=True) + EPS)
    return (value * factor * gain, factor)


def norm_back(value, factor, gain, grad):
    weighted = grad * gain
    d_value = factor * weighted - value * factor * factor * factor * jnp.mean(
        value * weighted, axis=-1, keepdims=True
    )
    return (d_value, jnp.sum(grad * value * factor, axis=0))


def product(left, right):
    return jnp.dot(left, right, preferred_element_type=jnp.float32)


def product_tn(left, right):
    return lax.dot_general(
        left, right, (((0,), (0,)), ((), ())), preferred_element_type=jnp.float32
    )


def product_nt(left, right):
    return lax.dot_general(
        left, right, (((1,), (1,)), ((), ())), preferred_element_type=jnp.float32
    )


def unit_scan(inputs, step_rows, b_rows, c_rows, decay_log, start):
    decay = -jnp.exp(decay_log)

    def advance(state, row):
        x_row, step_row, b_row, c_row = row
        state = (
            jnp.exp(step_row[None, :] * decay) * state
            + (step_row * x_row)[None, :] * b_row[:, None]
        )
        return (state, jnp.sum(c_row[:, None] * state, axis=0))

    final_state, outputs = lax.scan(advance, start, (inputs, step_rows, b_rows, c_rows), unroll=16)
    return (outputs, final_state)


def scan_back(inputs, step_rows, b_rows, c_rows, decay_log, start, d_outputs, d_final):
    _, pullback = jax.vjp(unit_scan, inputs, step_rows, b_rows, c_rows, decay_log, start)
    return pullback((d_outputs, d_final))


def link(first_pair, second_pair):
    return (first_pair[0] * second_pair[0], second_pair[0] * first_pair[1] + second_pair[1])


def gather_weights(mats, vecs):
    lane = (
        lax.all_gather(mats[0], "fsdp", axis=0, tiled=True),
        lax.all_gather(mats[1], "fsdp", axis=0, tiled=True),
        lax.all_gather(mats[2], "fsdp", axis=0, tiled=True),
        lax.all_gather(mats[3], "fsdp", axis=0, tiled=True),
        lax.all_gather(mats[4], "fsdp", axis=0, tiled=True),
        lax.all_gather(mats[5], "fsdp", axis=0, tiled=True),
        lax.all_gather(mats[6], "fsdp", axis=0, tiled=True),
        lax.all_gather(mats[7], "fsdp", axis=0, tiled=True),
        lax.all_gather(mats[8], "fsdp", axis=0, tiled=True),
        lax.all_gather(mats[9], "fsdp", axis=0, tiled=True),
        lax.all_gather(mats[10], "fsdp", axis=0, tiled=True),
    )
    wide = (
        lax.all_gather(lane[0], "ctx", axis=1, tiled=True),
        lax.all_gather(lane[1], "ctx", axis=1, tiled=True),
        lax.all_gather(lane[2], "ctx", axis=1, tiled=True),
        lax.all_gather(lane[3], "ctx", axis=1, tiled=True),
        lax.all_gather(lane[4], "ctx", axis=1, tiled=True),
        lax.all_gather(lane[5], "ctx", axis=1, tiled=True),
        lax.all_gather(lane[6], "ctx", axis=1, tiled=True),
        lax.all_gather(lane[7], "ctx", axis=1, tiled=True),
        lax.all_gather(lane[8], "ctx", axis=1, tiled=True),
        lax.all_gather(lane[9], "ctx", axis=1, tiled=True),
        lax.all_gather(lane[10], "ctx", axis=1, tiled=True),
        lax.all_gather(vecs[0].reshape(1, -1), "ctx", axis=1, tiled=True),
        lax.all_gather(vecs[1].reshape(1, -1), "ctx", axis=1, tiled=True),
        lax.all_gather(vecs[2].reshape(1, -1), "ctx", axis=1, tiled=True),
        lax.all_gather(vecs[3].reshape(1, -1), "ctx", axis=1, tiled=True),
        lax.all_gather(vecs[4].reshape(1, -1), "ctx", axis=1, tiled=True),
        lax.all_gather(vecs[5].reshape(1, -1), "ctx", axis=1, tiled=True),
    )
    return dict(zip(NAMES, wide))


def shards(
    tokens,
    cotangent,
    unit_order,
    block_seq,
    meta_tokens,
    input_gain,
    query_key_value_weight,
    w_xz,
    conv_kernel,
    state_proj,
    step_proj,
    step_bias,
    decay_log,
    skip_gain,
    attn_gain,
    ssm_gain,
    out_proj,
    ffn_gain,
    w_gate,
    w_up,
    w_down,
):
    mats = (
        meta_tokens,
        query_key_value_weight,
        w_xz,
        conv_kernel,
        state_proj,
        step_proj,
        decay_log,
        out_proj,
        w_gate,
        w_up,
        w_down,
    )
    vecs = (input_gain, step_bias, skip_gain, attn_gain, ssm_gain, ffn_gain)
    fwd_w = gather_weights(mats, vecs)
    ctx_place = lax.axis_index("ctx")
    tok_rows = tokens[0]
    device_rows = tok_rows.shape[0]
    model_width = tok_rows.shape[1]
    unit_rows = device_rows // 2
    slot_unit = unit_order[0]
    units_all = slot_unit.shape[0]
    grouped_rows = units_all * unit_rows
    conv_taps = CONV - 1
    query_width = QUERY_HEADS * HEAD_SIZE
    key_value_width = KEY_VALUE_HEADS * HEAD_SIZE
    queries_per_key_head = QUERY_HEADS // KEY_VALUE_HEADS
    score_scale = HEAD_SIZE ** (-0.5)
    slot_ids = jnp.arange(units_all, dtype=jnp.int32)
    inverse = jnp.zeros((units_all,), jnp.int32).at[slot_unit].set(slot_ids)
    unit_seq = jnp.repeat(block_seq[0], 2)
    change = unit_seq[1:] != unit_seq[:-1]
    starts = jnp.concatenate([jnp.ones((1,), jnp.bool_), change])
    finals = jnp.concatenate([change, jnp.ones((1,), jnp.bool_)])
    keep_start = 1.0 - starts.astype(jnp.float32)
    keep_final = 1.0 - finals.astype(jnp.float32)
    my_units = lax.dynamic_slice_in_dim(slot_unit, 2 * ctx_place, 2)
    my_pick = my_units[:, None] == slot_ids[None, :]
    my_seq = jnp.sum(jnp.where(my_pick, unit_seq[None, :], 0), axis=1)
    my_start = jnp.any(my_pick & starts[None, :], axis=1)
    tok_units = tok_rows.reshape(2, unit_rows, model_width).astype(jnp.float32)
    resid_in = jnp.where(
        my_start[:, None, None], fwd_w["meta"][None].astype(jnp.float32), tok_units
    ).reshape(device_rows, model_width)
    normed_f, norm_in = norm_fwd(resid_in, fwd_w["gain_in"][0].astype(jnp.float32))
    normed = normed_f.astype(jnp.bfloat16)
    query_key_value_rows = product(normed, fwd_w["qkv"]).astype(jnp.bfloat16)
    query_rows = query_key_value_rows[:, :query_width].reshape(
        device_rows, KEY_VALUE_HEADS, queries_per_key_head, HEAD_SIZE
    )
    keys_mine = query_key_value_rows[:, query_width : query_width + key_value_width]
    values_mine = query_key_value_rows[:, query_width + key_value_width :]
    xz_rows = product(normed, fwd_w["xz"]).astype(jnp.bfloat16)
    conv_in = xz_rows[:, :INNER].reshape(2, unit_rows, INNER)
    tail_rows = conv_in[:, unit_rows - conv_taps :]
    keys_slot, values_slot, tails_slot = (
        lax.all_gather(keys_mine, "ctx", axis=0, tiled=True),
        lax.all_gather(values_mine, "ctx", axis=0, tiled=True),
        lax.all_gather(tail_rows, "ctx", axis=0, tiled=True),
    )
    keys_seq = keys_slot.reshape(units_all, unit_rows, key_value_width)[inverse].reshape(
        grouped_rows, KEY_VALUE_HEADS, HEAD_SIZE
    )
    values_seq = values_slot.reshape(units_all, unit_rows, key_value_width)[inverse].reshape(
        grouped_rows, KEY_VALUE_HEADS, HEAD_SIZE
    )
    before = (slot_unit[None, :] == (my_units - 1)[:, None]).astype(jnp.bfloat16)
    tail_prev = jnp.dot(
        before, tails_slot.reshape(units_all, conv_taps * INNER), preferred_element_type=jnp.float32
    ).reshape(2, conv_taps, INNER)
    tail_prev = jnp.where(my_start[:, None, None], 0.0, tail_prev)
    extended = jnp.concatenate([tail_prev, conv_in.astype(jnp.float32)], axis=1)
    kernel = fwd_w["conv"].astype(jnp.float32)
    conv_out = kernel[0] * extended[:, 0:unit_rows]
    for offset in range(1, CONV):
        conv_out = conv_out + kernel[offset] * extended[:, offset : offset + unit_rows]
    ssm_in = silu(conv_out).astype(jnp.bfloat16).reshape(device_rows, INNER)
    ssm_in_f = ssm_in.astype(jnp.float32)
    select = product_nt(ssm_in, fwd_w["select"])
    step_low = select[:, :DT_RANK].astype(jnp.bfloat16)
    b_rows = select[:, DT_RANK : DT_RANK + STATE]
    c_rows = select[:, DT_RANK + STATE :]
    step_pre = product(step_low, fwd_w["step"]) + fwd_w["step_bias"][0].astype(jnp.float32)
    step_rows = jax.nn.softplus(step_pre)
    decay_f = fwd_w["decay"].astype(jnp.float32)
    rate = -jnp.exp(decay_f)
    x_units = ssm_in_f.reshape(2, unit_rows, INNER)
    step_units = step_rows.reshape(2, unit_rows, INNER)
    b_units = b_rows.reshape(2, unit_rows, STATE)
    c_units = c_rows.reshape(2, unit_rows, STATE)
    zero_state = jnp.zeros((STATE, INNER), jnp.float32)
    y_zero, end_state = jax.vmap(unit_scan, in_axes=(0, 0, 0, 0, None, None))(
        x_units, step_units, b_units, c_units, decay_f, zero_state
    )
    step_total = jnp.sum(step_units, axis=1)
    state_slot, total_slot = (
        lax.all_gather(end_state.astype(jnp.bfloat16), "ctx", axis=0, tiled=True).astype(
            end_state.dtype
        ),
        lax.all_gather(step_total.astype(jnp.bfloat16), "ctx", axis=0, tiled=True).astype(
            step_total.dtype
        ),
    )
    state_seq = state_slot[inverse]
    carry_seq = jnp.exp(rate[None] * total_slot[inverse][:, None, :])
    _, state_out = lax.associative_scan(link, (carry_seq * keep_start[:, None, None], state_seq))
    state_in = (
        jnp.concatenate([zero_state[None], state_out[:-1]], axis=0) * keep_start[:, None, None]
    )
    my_state_in = state_in[my_units]
    carried = jnp.exp(rate[None, None] * jnp.cumsum(step_units, axis=1)[:, :, None, :])
    y_from_in = jnp.sum(c_units[..., None] * carried * my_state_in[:, None], axis=2)
    z_gate = xz_rows[:, INNER:].astype(jnp.float32)
    y_total = (y_zero + y_from_in).reshape(device_rows, INNER) + fwd_w["skip"][0].astype(
        jnp.float32
    ) * ssm_in_f
    ssm_out = y_total * silu(z_gate)
    q_seq = jnp.repeat(my_seq, unit_rows)
    q_block = jnp.repeat(my_units // 2, unit_rows)
    key_seq = jnp.repeat(unit_seq, unit_rows)
    key_block = jnp.arange(grouped_rows, dtype=jnp.int32) // BLOCK_ROWS
    first_row = jnp.sum(unit_seq[None, :] < my_seq[:, None], axis=1) * unit_rows
    lower_block = jnp.min(first_row) // KEYS_BLK
    upper_block = ((jnp.max(my_units) // 2 + 1) * BLOCK_ROWS + KEYS_BLK - 1) // KEYS_BLK

    def block_scores(begin):
        key_part = lax.dynamic_slice_in_dim(keys_seq, begin, KEYS_BLK, 0)
        scores = (
            jnp.einsum("qhgd,khd->hgqk", query_rows, key_part, preferred_element_type=jnp.float32)
            * score_scale
        )
        allowed = (
            lax.dynamic_slice_in_dim(key_seq, begin, KEYS_BLK)[None, :] == q_seq[:, None]
        ) & (lax.dynamic_slice_in_dim(key_block, begin, KEYS_BLK)[None, :] <= q_block[:, None])
        return (scores, allowed)

    def stat_step(block, carry):
        top_score, total_weight = carry
        scores, allowed = block_scores(block * KEYS_BLK)
        new_top = jnp.maximum(
            top_score, jnp.max(jnp.where(allowed, scores, NEGATIVE_FILL), axis=-1)
        )
        weights = jnp.where(allowed, jnp.exp(scores - new_top[..., None]), 0.0)
        return (new_top, total_weight * jnp.exp(top_score - new_top) + jnp.sum(weights, axis=-1))

    top_score, total_weight = lax.fori_loop(
        lower_block,
        upper_block,
        stat_step,
        (
            jnp.full(
                (KEY_VALUE_HEADS, queries_per_key_head, device_rows), NEGATIVE_FILL, jnp.float32
            ),
            jnp.zeros((KEY_VALUE_HEADS, queries_per_key_head, device_rows), jnp.float32),
        ),
    )
    log_total = top_score + jnp.log(total_weight)

    def value_update(block, acc):
        begin = block * KEYS_BLK
        scores, allowed = block_scores(begin)
        probs = jnp.where(allowed, jnp.exp(scores - log_total[..., None]), 0.0).astype(jnp.bfloat16)
        value_part = lax.dynamic_slice_in_dim(values_seq, begin, KEYS_BLK, 0)
        return acc + jnp.einsum(
            "hgqk,khd->qhgd", probs, value_part, preferred_element_type=jnp.float32
        )

    attn_heads = lax.fori_loop(
        lower_block,
        upper_block,
        value_update,
        jnp.zeros((device_rows, KEY_VALUE_HEADS, queries_per_key_head, HEAD_SIZE), jnp.float32),
    )
    attention_output = attn_heads.reshape(device_rows, query_width)
    attn_norm, attn_factor = norm_fwd(attention_output, fwd_w["gain_attn"][0].astype(jnp.float32))
    ssm_norm, ssm_factor = norm_fwd(ssm_out, fwd_w["gain_ssm"][0].astype(jnp.float32))
    mixed = (0.5 * jnp.concatenate([attn_norm, ssm_norm], axis=1)).astype(jnp.bfloat16)
    mid_rows = resid_in + product(mixed, fwd_w["out"])
    ffn_f, mid_factor = norm_fwd(mid_rows, fwd_w["gain_ffn"][0].astype(jnp.float32))
    ffn_in = ffn_f.astype(jnp.bfloat16)
    gate_rows = product(ffn_in, fwd_w["gate"])
    up_rows = product(ffn_in, fwd_w["up"])
    hidden = (silu(gate_rows) * up_rows).astype(jnp.bfloat16)
    out_rows = mid_rows + product(hidden, fwd_w["down"])
    layer_out = out_rows.astype(jnp.bfloat16)[None]
    held = lax.optimization_barrier((mats, vecs, layer_out))
    back_w = gather_weights(held[0], held[1])
    cot_rows = cotangent[0]
    grad_down = product_tn(hidden, cot_rows)
    d_hidden = product_nt(cot_rows, back_w["down"])
    d_gate = (d_hidden * up_rows * silu_slope(gate_rows)).astype(jnp.bfloat16)
    d_up = (d_hidden * silu(gate_rows)).astype(jnp.bfloat16)
    d_ffn_in = product_nt(d_gate, back_w["gate"]) + product_nt(d_up, back_w["up"])
    d_mid_norm, grad_ffn_gain = norm_back(
        mid_rows, mid_factor, back_w["gain_ffn"][0].astype(jnp.float32), d_ffn_in
    )
    d_mid = cot_rows.astype(jnp.float32) + d_mid_norm
    d_branch = d_mid.astype(jnp.bfloat16)
    grad_out = product_tn(mixed, d_branch)
    d_mixed = 0.5 * product_nt(d_branch, back_w["out"])
    attention_gradient, grad_attn_gain = norm_back(
        attention_output,
        attn_factor,
        back_w["gain_attn"][0].astype(jnp.float32),
        d_mixed[:, :query_width],
    )
    d_ssm, grad_ssm_gain = norm_back(
        ssm_out, ssm_factor, back_w["gain_ssm"][0].astype(jnp.float32), d_mixed[:, query_width:]
    )
    skip_back = back_w["skip"][0].astype(jnp.float32)
    decay_back = back_w["decay"].astype(jnp.float32)
    d_y = d_ssm * silu(z_gate)
    d_z = d_ssm * y_total * silu_slope(z_gate)
    grad_skip = jnp.sum(d_y * ssm_in_f, axis=0)
    d_y_units = d_y.reshape(2, unit_rows, INNER)
    local_adjoint = jnp.sum(c_units[..., None] * carried * d_y_units[:, :, None, :], axis=1)
    adjoint_slot = lax.all_gather(
        local_adjoint.astype(jnp.bfloat16), "ctx", axis=0, tiled=True
    ).astype(local_adjoint.dtype)
    _, adjoint_seq = lax.associative_scan(
        link, (carry_seq * keep_final[:, None, None], adjoint_slot[inverse]), reverse=True
    )
    end_cot = (
        jnp.concatenate([adjoint_seq[1:], zero_state[None]], axis=0) * keep_final[:, None, None]
    )
    d_x_scan, d_steps, d_b, d_c, d_decay, _ = jax.vmap(
        scan_back, in_axes=(0, 0, 0, 0, None, 0, 0, 0)
    )(x_units, step_units, b_units, c_units, decay_back, my_state_in, d_y_units, end_cot[my_units])
    grad_decay = jnp.sum(d_decay, axis=0)
    d_pre = (d_steps.reshape(device_rows, INNER) * jax.nn.sigmoid(step_pre)).astype(jnp.bfloat16)
    grad_step = product_tn(step_low, d_pre)
    grad_step_bias = jnp.sum(d_pre.astype(jnp.float32), axis=0)
    d_select = jnp.concatenate(
        [
            product_nt(d_pre, back_w["step"]),
            d_b.reshape(device_rows, STATE),
            d_c.reshape(device_rows, STATE),
        ],
        axis=1,
    ).astype(jnp.bfloat16)
    grad_select = product_tn(d_select, ssm_in)
    d_ssm_in = (
        product(d_select, back_w["select"]) + d_x_scan.reshape(device_rows, INNER) + skip_back * d_y
    )
    d_conv_out = d_ssm_in.reshape(2, unit_rows, INNER) * silu_slope(conv_out)
    kernel_back = back_w["conv"].astype(jnp.float32)
    d_extended = jnp.zeros((2, unit_rows + conv_taps, INNER), jnp.float32)
    kernel_rows = []
    for offset in range(CONV):
        d_extended = d_extended.at[:, offset : offset + unit_rows].add(
            kernel_back[offset] * d_conv_out
        )
        kernel_rows.append(
            jnp.sum(d_conv_out * extended[:, offset : offset + unit_rows], axis=(0, 1))
        )
    grad_conv = jnp.stack(kernel_rows)
    d_tail = jnp.where(my_start[:, None, None], 0.0, d_extended[:, :conv_taps])
    tail_grad_slot = lax.all_gather(d_tail.astype(jnp.bfloat16), "ctx", axis=0, tiled=True).astype(
        d_tail.dtype
    )
    after = (slot_unit[None, :] == (my_units + 1)[:, None]).astype(jnp.float32)
    from_next = jnp.dot(
        after,
        tail_grad_slot.reshape(units_all, conv_taps * INNER),
        precision=lax.Precision.HIGHEST,
        preferred_element_type=jnp.float32,
    ).reshape(2, conv_taps, INNER)
    d_conv_in = d_extended[:, conv_taps:].at[:, unit_rows - conv_taps :].add(from_next)
    d_xz = jnp.concatenate([d_conv_in.reshape(device_rows, INNER), d_z], axis=1).astype(
        jnp.bfloat16
    )
    d_normed = product_nt(d_xz, back_w["xz"])
    attention_gradient_lower = attention_gradient.astype(jnp.bfloat16).reshape(
        device_rows, KEY_VALUE_HEADS, queries_per_key_head, HEAD_SIZE
    )
    delta = jnp.transpose(
        jnp.sum(attention_gradient_lower.astype(jnp.float32) * attn_heads, axis=-1), (1, 2, 0)
    )

    def grad_block(block, carry):
        d_query, d_keys, d_values = carry
        begin = block * KEYS_BLK
        scores, allowed = block_scores(begin)
        probs = jnp.where(allowed, jnp.exp(scores - log_total[..., None]), 0.0)
        key_part = lax.dynamic_slice_in_dim(keys_seq, begin, KEYS_BLK, 0)
        value_part = lax.dynamic_slice_in_dim(values_seq, begin, KEYS_BLK, 0)
        d_probs = jnp.einsum(
            "qhgd,khd->hgqk",
            attention_gradient_lower,
            value_part,
            preferred_element_type=jnp.float32,
        )
        d_scores = (probs * (d_probs - delta[..., None])).astype(jnp.bfloat16)
        d_query = (
            d_query
            + jnp.einsum("hgqk,khd->qhgd", d_scores, key_part, preferred_element_type=jnp.float32)
            * score_scale
        )
        key_grad = (
            jnp.einsum("hgqk,qhgd->khd", d_scores, query_rows, preferred_element_type=jnp.float32)
            * score_scale
        )
        value_grad = jnp.einsum(
            "hgqk,qhgd->khd",
            probs.astype(jnp.bfloat16),
            attention_gradient_lower,
            preferred_element_type=jnp.float32,
        )
        d_keys = lax.dynamic_update_slice_in_dim(
            d_keys, lax.dynamic_slice_in_dim(d_keys, begin, KEYS_BLK, 0) + key_grad, begin, 0
        )
        d_values = lax.dynamic_update_slice_in_dim(
            d_values, lax.dynamic_slice_in_dim(d_values, begin, KEYS_BLK, 0) + value_grad, begin, 0
        )
        return (d_query, d_keys, d_values)

    blank_rows = jnp.zeros((grouped_rows, KEY_VALUE_HEADS, HEAD_SIZE), jnp.float32)
    d_query, d_keys, d_values = lax.fori_loop(
        lower_block,
        upper_block,
        grad_block,
        (
            jnp.zeros((device_rows, KEY_VALUE_HEADS, queries_per_key_head, HEAD_SIZE), jnp.float32),
            blank_rows,
            blank_rows,
        ),
    )
    keys_grad_slot = d_keys.reshape(units_all, unit_rows, key_value_width)[slot_unit].reshape(
        grouped_rows, key_value_width
    )
    values_grad_slot = d_values.reshape(units_all, unit_rows, key_value_width)[slot_unit].reshape(
        grouped_rows, key_value_width
    )
    keys_grad, values_grad = (
        lax.psum_scatter(
            keys_grad_slot.astype(jnp.bfloat16), "ctx", scatter_dimension=0, tiled=True
        ).astype(jnp.float32),
        lax.psum_scatter(
            values_grad_slot.astype(jnp.bfloat16), "ctx", scatter_dimension=0, tiled=True
        ).astype(jnp.float32),
    )
    d_qkv = jnp.concatenate(
        [d_query.reshape(device_rows, query_width), keys_grad, values_grad], axis=1
    ).astype(jnp.bfloat16)
    d_normed = d_normed + product_nt(d_qkv, back_w["qkv"])
    d_resid_norm, grad_in_gain = norm_back(
        resid_in, norm_in, back_w["gain_in"][0].astype(jnp.float32), d_normed
    )
    d_resid = (d_mid + d_resid_norm).reshape(2, unit_rows, model_width)
    grad_meta = jnp.sum(jnp.where(my_start[:, None, None], d_resid, 0.0), axis=0)
    tokens_grad = (
        jnp.where(my_start[:, None, None], 0.0, d_resid)
        .reshape(1, device_rows, model_width)
        .astype(jnp.bfloat16)
    )
    grad_gate = product_tn(ffn_in, d_gate)
    grad_up = product_tn(ffn_in, d_up)
    grad_xz = product_tn(normed, d_xz)
    grad_qkv = product_tn(normed, d_qkv)
    wide = (
        lax.psum_scatter(
            grad_meta.astype(jnp.bfloat16), "ctx", scatter_dimension=1, tiled=True
        ).astype(jnp.float32),
        lax.psum_scatter(
            grad_qkv.astype(jnp.bfloat16), "ctx", scatter_dimension=1, tiled=True
        ).astype(jnp.float32),
        lax.psum_scatter(
            grad_xz.astype(jnp.bfloat16), "ctx", scatter_dimension=1, tiled=True
        ).astype(jnp.float32),
        lax.psum_scatter(
            grad_conv.astype(jnp.bfloat16), "ctx", scatter_dimension=1, tiled=True
        ).astype(jnp.float32),
        lax.psum_scatter(
            grad_select.astype(jnp.bfloat16), "ctx", scatter_dimension=1, tiled=True
        ).astype(jnp.float32),
        lax.psum_scatter(
            grad_step.astype(jnp.bfloat16), "ctx", scatter_dimension=1, tiled=True
        ).astype(jnp.float32),
        lax.psum_scatter(
            grad_decay.astype(jnp.bfloat16), "ctx", scatter_dimension=1, tiled=True
        ).astype(jnp.float32),
        lax.psum_scatter(
            grad_out.astype(jnp.bfloat16), "ctx", scatter_dimension=1, tiled=True
        ).astype(jnp.float32),
        lax.psum_scatter(
            grad_gate.astype(jnp.bfloat16), "ctx", scatter_dimension=1, tiled=True
        ).astype(jnp.float32),
        lax.psum_scatter(
            grad_up.astype(jnp.bfloat16), "ctx", scatter_dimension=1, tiled=True
        ).astype(jnp.float32),
        lax.psum_scatter(
            grad_down.astype(jnp.bfloat16), "ctx", scatter_dimension=1, tiled=True
        ).astype(jnp.float32),
        lax.psum_scatter(
            grad_in_gain[None].astype(jnp.bfloat16), "ctx", scatter_dimension=1, tiled=True
        ).astype(jnp.float32),
        lax.psum_scatter(
            grad_step_bias[None].astype(jnp.bfloat16), "ctx", scatter_dimension=1, tiled=True
        ).astype(jnp.float32),
        lax.psum_scatter(
            grad_skip[None].astype(jnp.bfloat16), "ctx", scatter_dimension=1, tiled=True
        ).astype(jnp.float32),
        lax.psum_scatter(
            grad_attn_gain[None].astype(jnp.bfloat16), "ctx", scatter_dimension=1, tiled=True
        ).astype(jnp.float32),
        lax.psum_scatter(
            grad_ssm_gain[None].astype(jnp.bfloat16), "ctx", scatter_dimension=1, tiled=True
        ).astype(jnp.float32),
        lax.psum_scatter(
            grad_ffn_gain[None].astype(jnp.bfloat16), "ctx", scatter_dimension=1, tiled=True
        ).astype(jnp.float32),
    )
    lane = (
        lax.psum_scatter(
            wide[0].astype(jnp.bfloat16), "fsdp", scatter_dimension=0, tiled=True
        ).astype(jnp.float32),
        lax.psum_scatter(
            wide[1].astype(jnp.bfloat16), "fsdp", scatter_dimension=0, tiled=True
        ).astype(jnp.float32),
        lax.psum_scatter(
            wide[2].astype(jnp.bfloat16), "fsdp", scatter_dimension=0, tiled=True
        ).astype(jnp.float32),
        lax.psum_scatter(
            wide[3].astype(jnp.bfloat16), "fsdp", scatter_dimension=0, tiled=True
        ).astype(jnp.float32),
        lax.psum_scatter(
            wide[4].astype(jnp.bfloat16), "fsdp", scatter_dimension=0, tiled=True
        ).astype(jnp.float32),
        lax.psum_scatter(
            wide[5].astype(jnp.bfloat16), "fsdp", scatter_dimension=0, tiled=True
        ).astype(jnp.float32),
        lax.psum_scatter(
            wide[6].astype(jnp.bfloat16), "fsdp", scatter_dimension=0, tiled=True
        ).astype(jnp.float32),
        lax.psum_scatter(
            wide[7].astype(jnp.bfloat16), "fsdp", scatter_dimension=0, tiled=True
        ).astype(jnp.float32),
        lax.psum_scatter(
            wide[8].astype(jnp.bfloat16), "fsdp", scatter_dimension=0, tiled=True
        ).astype(jnp.float32),
        lax.psum_scatter(
            wide[9].astype(jnp.bfloat16), "fsdp", scatter_dimension=0, tiled=True
        ).astype(jnp.float32),
        lax.psum_scatter(
            wide[10].astype(jnp.bfloat16), "fsdp", scatter_dimension=0, tiled=True
        ).astype(jnp.float32),
    )
    gains = lax.psum(
        (wide[11][0], wide[12][0], wide[13][0], wide[14][0], wide[15][0], wide[16][0]), "fsdp"
    )
    return (
        layer_out,
        tokens_grad,
        lane[0],
        gains[0],
        lane[1],
        lane[2],
        lane[3],
        lane[4],
        lane[5],
        gains[1],
        lane[6],
        gains[2],
        gains[3],
        gains[4],
        lane[7],
        gains[5],
        lane[8],
        lane[9],
        lane[10],
    )


def solution(mesh):
    return jax.shard_map(
        shards,
        mesh=mesh,
        in_specs=(
            P("fsdp", "ctx", None),
            P("fsdp", "ctx", None),
            P("fsdp", None),
            P("fsdp", None),
            P("fsdp", "ctx"),
            P("ctx"),
            P("fsdp", "ctx"),
            P("fsdp", "ctx"),
            P("fsdp", "ctx"),
            P("fsdp", "ctx"),
            P("fsdp", "ctx"),
            P("ctx"),
            P("fsdp", "ctx"),
            P("ctx"),
            P("ctx"),
            P("ctx"),
            P("fsdp", "ctx"),
            P("ctx"),
            P("fsdp", "ctx"),
            P("fsdp", "ctx"),
            P("fsdp", "ctx"),
        ),
        out_specs=(
            P("fsdp", "ctx", None),
            P("fsdp", "ctx", None),
            P("fsdp", "ctx"),
            P("ctx"),
            P("fsdp", "ctx"),
            P("fsdp", "ctx"),
            P("fsdp", "ctx"),
            P("fsdp", "ctx"),
            P("fsdp", "ctx"),
            P("ctx"),
            P("fsdp", "ctx"),
            P("ctx"),
            P("ctx"),
            P("ctx"),
            P("fsdp", "ctx"),
            P("ctx"),
            P("fsdp", "ctx"),
            P("fsdp", "ctx"),
            P("fsdp", "ctx"),
        ),
        check_vma=False,
    )
```

profile of v0, /device:TPU:0, one launch (start us, length us, event | category | flops | bytes accessed | tf_op | source)
XLA Modules:
  0.0 4360.1 jit_solution(2077853805601866035)
XLA Ops:
  8.0 36.8 all-gather.11
  47.4 32.6 all-gather.65.cloned.1.call-done
  91.4 25.3 all-reduce.44
  188.4 16.5 all-gather.15
  311.5 65.1 %while.110 = (s32[]{:T(128)}, f32[2,16,3200]{2,1,0:T(8,128)S(1)}, f32[8,16,2,3200]{3,1,0,2:T(8,128)}, f32[8,16,2,3200]{3,2,1,0:T(2,128)}, f32[16,3200]{1,0:T(8,1...) while((s32[]{:T(128)}, f32[2,16,3200]{2,1,0:T(8,128)S(1)}, ...), condition=%wide.region_31.32_spmd.clone, body=%wide.region_14.31_spmd.clone.sunk | while | flops 14950418 | bytes 10254940 | solution.py:89
  412.5 36.7 all-gather.105.cloned.1.call-done
  458.3 17.0 all-gather.63.cloned.1.call-done
  629.3 21.1 multiply_reduce_fusion.65
  679.5 36.5 all-gather.75.cloned.1.call-done
  715.9 18.6 fusion.523
  734.6 79.7 %all-gather.79.cloned.1.call-done = bf16[1600,5504]{0,1:T(8,128)(2,1)} async-done(((bf16[1600,688]{0,1:T(8,128)(2,1)}), bf16[1600,5504]{0,1:T(8,128)(2,1)}) %all-gather.79.cloned.1.call-update) | async-done | bytes 17612816 | tf_op jit(solution)/shard_map/all_gather | solution.py:126
  827.4 82.0 %all-gather.81.cloned.1.call-done = bf16[5504,1600]{0,1:T(8,128)(2,1)} async-done(((bf16[5504,200]{0,1:T(8,128)(2,1)}), bf16[5504,1600]{0,1:T(8,128)(2,1)}) %all-gather.81.cloned.1.call-update) | async-done | bytes 17612816 | tf_op jit(solution)/shard_map/all_gather | solution.py:127
  924.4 47.1 %all-gather.107.cloned.1.call-done = bf16[4,1376,200]{1,2,0:T(8,128)(2,1)} async-done(((bf16[1,1376,200]{1,2,0:T(8,128)(2,1)}), bf16[4,1376,200]{1,2,0:T(8,128)(2,1)}) %all-gather.107.cloned.1.call-update) | async-done | bytes 2201616 | tf_op jit(solution)/shard_map/all_gather | solution.py:114
  980.5 43.4 all-gather.85.cloned.1.call-done
  1028.4 47.8 %all-gather.89.cloned.1.call-done = bf16[1600,688]{1,0:T(8,128)(2,1)} async-done(((bf16[400,688]{1,0:T(8,128)(2,1)}), bf16[1600,688]{1,0:T(8,128)(2,1)}) %all-gather.89.cloned.1.call-update) | async-done | bytes 2201616 | tf_op jit(solution)/shard_map/all_gather | solution.py:113
  1080.7 40.7 all-gather.109.cloned.1.call-done
  1131.3 25.3 all-reduce.43
  1156.7 59.1 %all-gather.83.cloned.1.call-done = bf16[5504,1600]{0,1:T(8,128)(2,1)} async-done(((bf16[5504,200]{0,1:T(8,128)(2,1)}), bf16[5504,1600]{0,1:T(8,128)(2,1)}) %all-gather.83.cloned.1.call-update) | async-done | bytes 17612816 | tf_op jit(solution)/shard_map/all_gather | solution.py:127
  1215.8 16.8 multiply_convert_fusion
  1232.6 81.3 %all-gather.87.cloned.1.call-done = bf16[1600,5504]{0,1:T(8,128)(2,1)} async-done(((bf16[1600,688]{0,1:T(8,128)(2,1)}), bf16[1600,5504]{0,1:T(8,128)(2,1)}) %all-gather.87.cloned.1.call-update) | async-done | bytes 17612816 | tf_op jit(solution)/shard_map/all_gather | solution.py:125
  1326.7 85.5 %all-gather.91.cloned.1.call-done = bf16[1600,5504]{0,1:T(8,128)(2,1)} async-done(((bf16[1600,688]{0,1:T(8,128)(2,1)}), bf16[1600,5504]{0,1:T(8,128)(2,1)}) %all-gather.91.cloned.1.call-update) | async-done | bytes 17612816 | tf_op jit(solution)/shard_map/all_gather | solution.py:126
  1431.4 67.5 %all-gather.93.cloned.1.call-done = bf16[4800,1600]{0,1:T(8,128)(2,1)} async-done(((bf16[4800,200]{0,1:T(8,128)(2,1)}), bf16[4800,1600]{0,1:T(8,128)(2,1)}) %all-gather.93.cloned.1.call-update) | async-done | bytes 15360016 | tf_op jit(solution)/shard_map/all_gather | solution.py:124
  1549.6 27.8 all-gather.31
  1590.8 79.8 %while.109 = (s32[]{:T(128)}, f32[256,5,5,64]{0,3,2,1:T(8,128)}, f32[2048,5,64]{0,2,1:T(8,128)}, f32[2048,5,64]{0,2,1:T(8,128)}, s32[]{:T(128)}, /*index=5*/bf16...) while((s32[]{:T(128)}, f32[256,5,5,64]{0,3,2,1:T(8,128)}, ...), condition=%wide.region_111.112_spmd.clone, body=%wide.region_110.111_spmd.clone.sunk | while | flops 2131623936 | bytes 138440080 | solution.py:478
  1696.5 35.9 all-gather.27
  1737.7 621.7 %while.106 = (s32[]{:T(128)}, f32[2,16,3200]{2,1,0:T(8,128)S(1)}, f32[8,16,2,1,3200]{4,2,1,3,0:T(2,128)}, f32[8,16,2,16,3200]{4,3,2,1,0:T(8,128)}, f32[8,16,2,16...) while((s32[]{:T(128)}, f32[2,16,3200]{2,1,0:T(8,128)S(1)}, ...), condition=%wide.region_41.42_spmd, body=%wide.region_40.41_spmd.sunk | while | flops 18227212 | bytes 162323920 | solution.py:89
  2435.0 327.7 %while.111 = (s32[]{:T(128)}, f32[2,16,3200]{2,1,0:T(8,128)}, f32[2,16,3200]{2,1,0:T(8,128)S(1)}, f32[8,16,2,3200]{3,2,1,0:T(2,128)}, f32[8,16,2,3200]{3,2,1,0:T...) while((s32[]{:T(128)}, f32[2,16,3200]{2,1,0:T(8,128)}, ...), condition=%wide.region_107.108_spmd.clone, body=%wide.region_42.107_spmd.clone.sunk | while | flops 24984592 | bytes 56821064 | solution.py:89
  2813.4 16.1 all-gather.30
  3064.1 19.6 all-reduce.49.cloned.1.call-done
  3085.3 81.0 %reduce-scatter.99.cloned.1.call-done = bf16[1600,280]{0,1:T(8,128)(2,1)} async-done(((bf16[1600,2240]{0,1:T(8,128)(2,1)}), bf16[1600,280]{0,1:T(8,128)(2,1)}) %reduce-scatter.99.cloned.1.call-update) | async-done | bytes 896016
  3168.8 114.4 %reduce-scatter.69.cloned.1.call-done = bf16[4800,200]{0,1:T(8,128)(2,1)} async-done(((bf16[4800,1600]{0,1:T(8,128)(2,1)}), bf16[4800,200]{0,1:T(8,128)(2,1)}) %reduce-scatter.69.cloned.1.call-update) | async-done | bytes 1920016 | tf_op jit(solution)/shard_map/reduce_scatter | solution.py:542
  3287.4 158.3 %reduce-scatter.71.cloned.1.call-done = bf16[1600,688]{0,1:T(8,128)(2,1)} async-done(((bf16[1600,5504]{0,1:T(8,128)(2,1)}), bf16[1600,688]{0,1:T(8,128)(2,1)}) %reduce-scatter.71.cloned.1.call-update) | async-done | bytes 2201616 | tf_op jit(solution)/shard_map/reduce_scatter | solution.py:545
  3450.2 157.9 %reduce-scatter.73.cloned.1.call-done = bf16[1600,688]{0,1:T(8,128)(2,1)} async-done(((bf16[1600,5504]{0,1:T(8,128)(2,1)}), bf16[1600,688]{0,1:T(8,128)(2,1)}) %reduce-scatter.73.cloned.1.call-update) | async-done | bytes 2201616 | tf_op jit(solution)/shard_map/reduce_scatter | solution.py:548
  3612.7 144.7 %reduce-scatter.65.cloned.1.call-done = bf16[1600,800]{0,1:T(8,128)(2,1)} async-done(((bf16[1600,6400]{0,1:T(8,128)(2,1)}), bf16[1600,800]{0,1:T(8,128)(2,1)}) %reduce-scatter.65.cloned.1.call-update) | async-done | bytes 2560016 | tf_op jit(solution)/shard_map/reduce_scatter | solution.py:527
  3764.9 31.1 reduce-scatter.87.cloned.1.call-done
  3797.0 37.4 reduce-scatter.89.cloned.1.call-done
  3835.5 37.6 reduce-scatter.83.cloned.1.call-done
  3874.1 37.4 reduce-scatter.79.cloned.1.call-done
  3912.5 37.2 reduce-scatter.85.cloned.1.call-done
  3950.6 18.9 all-reduce.45
  3971.4 20.5 reduce-scatter.81.cloned.1.call-done
  4009.5 18.7 all-reduce.51.cloned.1.call-done
  4030.7 55.1 %reduce-scatter.97.cloned.1.call-done = bf16[1376,200]{1,0:T(8,128)(2,1)} async-done(((bf16[5504,200]{1,0:T(8,128)(2,1)}), bf16[1376,200]{1,0:T(8,128)(2,1)}) %reduce-scatter.97.cloned.1.call-update) | async-done | bytes 550416
  4088.3 24.4 all-reduce.42
  4141.0 48.7 %reduce-scatter.91.cloned.1.call-done = bf16[1200,200]{1,0:T(8,128)(2,1)} async-done(((bf16[4800,200]{1,0:T(8,128)(2,1)}), bf16[1200,200]{1,0:T(8,128)(2,1)}) %reduce-scatter.91.cloned.1.call-update) | async-done | bytes 480016
  4192.0 49.0 %reduce-scatter.93.cloned.1.call-done = bf16[400,688]{1,0:T(8,128)(2,1)} async-done(((bf16[1600,688]{1,0:T(8,128)(2,1)}), bf16[400,688]{1,0:T(8,128)(2,1)}) %reduce-scatter.93.cloned.1.call-update) | async-done | bytes 550416
  4243.6 48.7 %reduce-scatter.95.cloned.1.call-done = bf16[400,688]{1,0:T(8,128)(2,1)} async-done(((bf16[1600,688]{1,0:T(8,128)(2,1)}), bf16[400,688]{1,0:T(8,128)(2,1)}) %reduce-scatter.95.cloned.1.call-update) | async-done | bytes 550416
  4295.0 55.4 %reduce-scatter.77.cloned.1.call-done = bf16[400,800]{1,0:T(8,128)(2,1)} async-done(((bf16[1600,800]{1,0:T(8,128)(2,1)}), bf16[400,800]{1,0:T(8,128)(2,1)}) %reduce-scatter.77.cloned.1.call-update) | async-done | bytes 640016
  (2461 shorter events, 2167.4 us)
Async XLA Ops:
  7.9 138.2 %all-gather.59.cloned.1.call-start = ((), (), s32[]{:S(2)}) async-start(), calls=%async_computation.22 | async-start | bytes 8386560 | tf_op jit(solution)/shard_map/all_gather | solution.py:118
  47.3 209.4 %all-gather.67.cloned.1.call-start = ((), (), s32[]{:S(2)}) async-start(), calls=%async_computation.26 | async-start | bytes 23961600 | tf_op jit(solution)/shard_map/all_gather | solution.py:119
  85.2 292.4 %all-gather.103.cloned.1.call-start = ((), (), s32[]{:S(2)}) async-start(), calls=%async_computation.52 | async-start | bytes 2560000 | tf_op jit(solution)/shard_map/all_gather | solution.py:111
  85.8 300.3 %all-gather.73.cloned.1.call-start = ((), (), s32[]{:S(2)}) async-start(), calls=%async_computation.29 | async-start | bytes 3072000 | tf_op jit(solution)/shard_map/all_gather | solution.py:112
  86.4 313.7 %all-gather.77.cloned.1.call-start = ((), (), s32[]{:S(2)}) async-start(), calls=%async_computation.31 | async-start | bytes 3072000 | tf_op jit(solution)/shard_map/all_gather | solution.py:113
  87.0 362.3 %all-gather.105.cloned.1.call-start = ((), (), s32[]{:S(2)}) async-start(), calls=%async_computation.53 | async-start | bytes 2816000 | tf_op jit(solution)/shard_map/all_gather | solution.py:114
  87.7 387.5 %all-gather.63.cloned.1.call-start = ((), (), s32[]{:S(2)}) async-start(), calls=%async_computation.24 | async-start | bytes 1474560 | tf_op jit(solution)/shard_map/all_gather | solution.py:217
  153.1 349.3 %all-gather.61.cloned.1.call-start = ((), (), s32[]{:S(2)}) async-start(), calls=%async_computation.23 | async-start | bytes 1474560 | tf_op jit(solution)/shard_map/all_gather | solution.py:218
  256.7 319.6 %all-gather.69.cloned.1.call-start = ((), (), s32[]{:S(2)}) async-start(), calls=%async_computation.27 | async-start | bytes 1843200 | tf_op jit(solution)/shard_map/all_gather | solution.py:257
  377.4 285.6 %all-gather.71.cloned.1.call-start = ((), (), s32[]{:S(2)}) async-start(), calls=%async_computation.28 | async-start | bytes 17510400 | tf_op jit(solution)/shard_map/all_gather | solution.py:124
  386.0 329.9 %all-gather.75.cloned.1.call-start = ((), (), s32[]{:S(2)}) async-start(), calls=%async_computation.30 | async-start | bytes 20606976 | tf_op jit(solution)/shard_map/all_gather | solution.py:125
  390.5 423.7 %all-gather.79.cloned.1.call-start = ((), (), s32[]{:S(2)}) async-start(), calls=%async_computation.32 | async-start | bytes 20606976 | tf_op jit(solution)/shard_map/all_gather | solution.py:126
  404.6 504.8 %all-gather.81.cloned.1.call-start = ((), (), s32[]{:S(2)}) async-start(), calls=%async_computation.33 | async-start | bytes 19814400 | tf_op jit(solution)/shard_map/all_gather | solution.py:127
  458.2 513.3 %all-gather.107.cloned.1.call-start = ((), (), s32[]{:S(2)}) async-start(), calls=%async_computation.54 | async-start | bytes 2816000 | tf_op jit(solution)/shard_map/all_gather | solution.py:114
  923.2 153.0 %all-gather.89.cloned.1.call-start = ((), (), s32[]{:S(2)}) async-start(), calls=%async_computation.37 | async-start | bytes 3072000 | tf_op jit(solution)/shard_map/all_gather | solution.py:113
  923.8 197.7 %all-gather.109.cloned.1.call-start = ((), (), s32[]{:S(2)}) async-start(), calls=%async_computation.55 | async-start | bytes 2560000 | tf_op jit(solution)/shard_map/all_gather | solution.py:111
  924.3 291.5 %all-gather.83.cloned.1.call-start = ((), (), s32[]{:S(2)}) async-start(), calls=%async_computation.34 | async-start | bytes 19814400 | tf_op jit(solution)/shard_map/all_gather | solution.py:127
  980.5 333.5 %all-gather.87.cloned.1.call-start = ((), (), s32[]{:S(2)}) async-start(), calls=%async_computation.36 | async-start | bytes 20606976 | tf_op jit(solution)/shard_map/all_gather | solution.py:125
  1028.4 383.9 %all-gather.91.cloned.1.call-start = ((), (), s32[]{:S(2)}) async-start(), calls=%async_computation.38 | async-start | bytes 20606976 | tf_op jit(solution)/shard_map/all_gather | solution.py:126
  1080.7 418.2 %all-gather.93.cloned.1.call-start = ((), (), s32[]{:S(2)}) async-start(), calls=%async_computation.39 | async-start | bytes 17510400 | tf_op jit(solution)/shard_map/all_gather | solution.py:124
  1130.0 1229.4 %all-gather.97.cloned.1.call-start = ((), (), s32[]{:S(2)}) async-start(), calls=%async_computation.41 | async-start | bytes 3584000 | tf_op jit(solution)/shard_map/all_gather | solution.py:106
  1156.7 1213.9 %all-gather.95.cloned.1.call-start = ((), (), s32[]{:S(2)}) async-start(), calls=%async_computation.40 | async-start | bytes 1843200 | tf_op jit(solution)/shard_map/all_gather | solution.py:377
  1549.5 1317.9 %all-gather.101.cloned.1.call-start = ((), (), s32[]{:S(2)}) async-start(), calls=%async_computation.45 | async-start | bytes 8386560 | tf_op jit(solution)/shard_map/all_gather | solution.py:118
  1580.0 1287.4 %reduce-scatter.59.cloned.1.call-start = ((), (), s32[]{:S(2)}) async-start(), calls=%async_computation.43 | async-start | bytes 1474560 | tf_op jit(solution)/shard_map/reduce_scatter | solution.py:495
  1680.2 1187.3 %reduce-scatter.61.cloned.1.call-start = ((), (), s32[]{:S(2)}) async-start(), calls=%async_computation.44 | async-start | bytes 1474560 | tf_op jit(solution)/shard_map/reduce_scatter | solution.py:498
  1737.6 1220.3 %all-gather.99.cloned.1.call-start = ((), (), s32[]{:S(2)}) async-start(), calls=%async_computation.42 | async-start | bytes 23961600 | tf_op jit(solution)/shard_map/all_gather | solution.py:119
  2364.7 693.6 %reduce-scatter.67.cloned.1.call-start = ((), (), s32[]{:S(2)}) async-start(), calls=%async_computation.48 | async-start | bytes 921600 | tf_op jit(solution)/shard_map/reduce_scatter | solution.py:536
  2774.8 284.1 %reduce-scatter.101.cloned.1.call-start = ((), (), s32[]{:S(2)}) async-start(), calls=%async_computation.71 | async-start | bytes 19814400
  2785.5 298.1 %all-reduce.49.cloned.1.call-start = ((), (), s32[]{:S(2)}) async-start(), calls=%async_computation.68 | async-start | bytes 851968
  2991.7 174.6 %reduce-scatter.99.cloned.1.call-start = ((), (), s32[]{:S(2)}) async-start(), calls=%async_computation.70 | async-start | bytes 8386560
  2998.4 284.8 %reduce-scatter.69.cloned.1.call-start = ((), (), s32[]{:S(2)}) async-start(), calls=%async_computation.49 | async-start | bytes 17510400 | tf_op jit(solution)/shard_map/reduce_scatter | solution.py:542
  3008.8 436.8 %reduce-scatter.71.cloned.1.call-start = ((), (), s32[]{:S(2)}) async-start(), calls=%async_computation.50 | async-start | bytes 20606976 | tf_op jit(solution)/shard_map/reduce_scatter | solution.py:545
  3021.4 586.7 %reduce-scatter.73.cloned.1.call-start = ((), (), s32[]{:S(2)}) async-start(), calls=%async_computation.51 | async-start | bytes 20606976 | tf_op jit(solution)/shard_map/reduce_scatter | solution.py:548
  3032.9 724.5 %reduce-scatter.65.cloned.1.call-start = ((), (), s32[]{:S(2)}) async-start(), calls=%async_computation.47 | async-start | bytes 23961600 | tf_op jit(solution)/shard_map/reduce_scatter | solution.py:527
  3048.3 747.7 %reduce-scatter.87.cloned.1.call-start = ((), (), s32[]{:S(2)}) async-start(), calls=%async_computation.62 | async-start | bytes 921600
  3050.3 784.1 %reduce-scatter.89.cloned.1.call-start = ((), (), s32[]{:S(2)}) async-start(), calls=%async_computation.63 | async-start | bytes 921600
  3051.8 821.2 %reduce-scatter.83.cloned.1.call-start = ((), (), s32[]{:S(2)}) async-start(), calls=%async_computation.60 | async-start | bytes 921600
  3053.3 858.2 %reduce-scatter.79.cloned.1.call-start = ((), (), s32[]{:S(2)}) async-start(), calls=%async_computation.58 | async-start | bytes 921600
  3054.7 895.0 %reduce-scatter.85.cloned.1.call-start = ((), (), s32[]{:S(2)}) async-start(), calls=%async_computation.61 | async-start | bytes 921600
  3056.1 935.8 %reduce-scatter.81.cloned.1.call-start = ((), (), s32[]{:S(2)}) async-start(), calls=%async_computation.59 | async-start | bytes 1843200
  3058.3 969.9 %all-reduce.51.cloned.1.call-start = ((), (), s32[]{:S(2)}) async-start(), calls=%async_computation.69 | async-start | bytes 204800
  3058.9 1027.0 %reduce-scatter.97.cloned.1.call-start = ((), (), s32[]{:S(2)}) async-start(), calls=%async_computation.67 | async-start | bytes 3522560
  3063.4 1062.0 %reduce-scatter.63.cloned.1.call-start = ((), (), s32[]{:S(2)}) async-start(), calls=%async_computation.46 | async-start | bytes 81920 | tf_op jit(solution)/shard_map/reduce_scatter | solution.py:574
  3085.3 1053.7 %reduce-scatter.75.cloned.1.call-start = ((), (), s32[]{:S(2)}) async-start(), calls=%async_computation.56 | async-start | bytes 1536000
  3168.7 1020.9 %reduce-scatter.91.cloned.1.call-start = ((), (), s32[]{:S(2)}) async-start(), calls=%async_computation.64 | async-start | bytes 3072000
  3287.4 953.7 %reduce-scatter.93.cloned.1.call-start = ((), (), s32[]{:S(2)}) async-start(), calls=%async_computation.65 | async-start | bytes 3072000
  3450.1 842.2 %reduce-scatter.95.cloned.1.call-start = ((), (), s32[]{:S(2)}) async-start(), calls=%async_computation.66 | async-start | bytes 3072000
  3612.6 737.7 %reduce-scatter.77.cloned.1.call-start = ((), (), s32[]{:S(2)}) async-start(), calls=%async_computation.57 | async-start | bytes 3584000
  (159 other events, 3082.4 us)
Sparse Core Ops, SparseCore 0:
  9.6 70.3 all-gather.64
  82.4 50.2 all-gather.58
  134.7 114.2 all-gather.66
  250.4 44.9 all-gather.102
  296.8 50.8 all-gather.72
  349.1 50.8 all-gather.76
  401.6 47.5 all-gather.104
  477.7 24.7 all-gather.60
  504.7 25.9 all-gather.68
  532.6 85.0 all-gather.70
  619.5 96.3 all-gather.74
  717.8 96.3 all-gather.78
  816.0 93.3 all-gather.80
  922.7 48.7 all-gather.106
  972.9 50.9 all-gather.84
  1025.3 50.8 all-gather.88
  1077.7 43.7 all-gather.108
  1123.3 92.4 all-gather.82
  1217.5 96.3 all-gather.86
  1315.8 96.3 all-gather.90
  1414.1 84.7 all-gather.92
  1500.5 63.0 all-gather.96
  1565.3 25.6 all-gather.94
  1593.4 50.4 all-gather.100
  1680.3 62.0 reduce-scatter.58
  1745.5 37.3 reduce-scatter.60
  2364.8 106.3 all-gather.98
  2775.0 32.0 reduce-scatter.66
  2809.4 217.3 reduce-scatter.100
  3030.8 52.7 all-reduce.48
  3087.5 78.7 reduce-scatter.98
  3169.8 113.3 reduce-scatter.68
  3287.2 158.4 reduce-scatter.70
  3449.7 158.3 reduce-scatter.72
  3612.1 145.2 reduce-scatter.64
  3761.5 34.4 reduce-scatter.86
  3799.9 34.4 reduce-scatter.88
  3838.6 34.4 reduce-scatter.82
  3877.0 34.4 reduce-scatter.78
  3915.2 34.4 reduce-scatter.84
  3953.0 38.8 reduce-scatter.80
  3994.1 34.0 all-reduce.50
  4030.6 55.1 reduce-scatter.96
  4110.1 28.7 reduce-scatter.74
  4141.1 48.5 reduce-scatter.90
  4191.8 49.1 reduce-scatter.92
  4243.2 49.1 reduce-scatter.94
  4294.7 55.6 reduce-scatter.76
  (2 shorter events, 42.2 us)
where the time goes:
time: 4410 us; the launch traced here: 4360 us
  waiting for transfers between devices  1940 us (44%)
  local copies, waits for them, and re-layouts  918 us (21%)
  other arithmetic  662 us (15%)
  blocking collectives  470 us (11%)
  matrix products  332 us (8%)
    unnamed x67, waiting for transfers between devices  595 us
    while x827, local copies, waits for them, and re-layouts  300 us
    while x408, other arithmetic  221 us
    dynamic_update_slice x64, local copies, waits for them, and re-layouts, unit_scan(): lax.scan(advance, start, (inputs, step_rows, b_rows, c_rows), unroll=16)  169 us
    all_gather x2, waiting for transfers between devices, gather_weights(): lax.all_gather(lane[9], 'ctx', axis=1, tiled=True)  165 us
    reduce_scatter x1, waiting for transfers between devices, shards(): lax.psum_scatter(grad_gate.astype(jnp.bfloat16), 'ctx', scatter_dimension...  158 us
    reduce_scatter x1, waiting for transfers between devices, shards(): lax.psum_scatter(grad_up.astype(jnp.bfloat16), 'ctx', scatter_dimension=1...  158 us
    reduce_scatter x1, waiting for transfers between devices, shards(): lax.psum_scatter(grad_xz.astype(jnp.bfloat16), 'ctx', scatter_dimension=1...  145 us
  transfers between devices with their start and end apart: 51, of which 35 were waited for; matrix products, arithmetic and copies ran while one was open for 42% of the time, Pallas kernels for 0%

commit v1 on v0

v1 whole, which is shorter than its diff:
```python
import functools
import jax
import jax.numpy as jnp
from jax import lax
from jax.experimental import pallas as pl
from jax.experimental.pallas import tpu as pltpu
from jax.sharding import PartitionSpec as P

QUERY_HEADS = 25
KEY_VALUE_HEADS = 5
HEAD_SIZE = 64
INNER = 3200
STATE = 16
CONV = 4
DT_RANK = 100
EPS = 1e-06
LOG2E = 1.4426950408889634
LN2 = 0.6931471805599453
VMEM_LIMIT = 56 * 1024 * 1024
STEP_GROUP = 8
F32 = jnp.float32
BF16 = jnp.bfloat16


def sigmoid(value):
    return 1.0 / (1.0 + jnp.exp(-value))


def dot_nn(left, right):
    return lax.dot_general(left, right, (((1,), (0,)), ((), ())), preferred_element_type=F32)


def dot_nt(left, right):
    return lax.dot_general(left, right, (((1,), (1,)), ((), ())), preferred_element_type=F32)


def dot_tn(left, right):
    return lax.dot_general(left, right, (((0,), (0,)), ((), ())), preferred_element_type=F32)


def unit_spec(rows, width, reverse_units=None):
    if reverse_units is None:
        return pl.BlockSpec((rows, width), lambda u, slot, *_: (slot[u], 0))
    last = reverse_units - 1
    return pl.BlockSpec((rows, width), lambda i, slot, *_: (slot[last - i], 0))


def whole_spec(shape):
    zeros = (0,) * len(shape)
    return pl.BlockSpec(shape, lambda *_: zeros)


def params():
    return pltpu.CompilerParams(
        dimension_semantics=("arbitrary",), vmem_limit_bytes=VMEM_LIMIT
    )


def conv_kernel_fwd(slot, start, xin_ref, w_ref, sel_ref, xc_ref, xs_ref, part_ref, ext):
    u = pl.program_id(0)
    rows = xin_ref.shape[0]
    keep = jnp.where(start[u] == 1, 0.0, 1.0)

    @pl.when(u == 0)
    def _():
        ext[...] = jnp.zeros_like(ext)

    ext[0:8, :] = ext[rows : rows + 8, :] * keep
    ext[8 : 8 + rows, :] = xin_ref[...].astype(F32)
    acc = w_ref[0:1, :] * ext[5 : 5 + rows, :]
    for k in range(1, CONV):
        acc = acc + w_ref[k : k + 1, :] * ext[5 + k : 5 + k + rows, :]
    xc_ref[...] = acc
    xs = (acc * sigmoid(acc)).astype(BF16)
    xs_ref[...] = xs
    part_ref[...] = dot_nt(xs, sel_ref[...]).astype(BF16)


def conv_forward(slot, start, xin, conv_w, sel_w, unit_rows):
    rows, width = xin.shape
    units = rows // unit_rows
    sel_rows = sel_w.shape[0]
    return pl.pallas_call(
        conv_kernel_fwd,
        out_shape=(
            jax.ShapeDtypeStruct((rows, width), F32),
            jax.ShapeDtypeStruct((rows, width), BF16),
            jax.ShapeDtypeStruct((rows, sel_rows), BF16),
        ),
        grid_spec=pltpu.PrefetchScalarGridSpec(
            num_scalar_prefetch=2,
            grid=(units,),
            in_specs=[
                unit_spec(unit_rows, width),
                whole_spec((CONV, width)),
                whole_spec((sel_rows, width)),
            ],
            out_specs=[
                unit_spec(unit_rows, width),
                unit_spec(unit_rows, width),
                unit_spec(unit_rows, sel_rows),
            ],
            scratch_shapes=[pltpu.VMEM((unit_rows + 8, width), F32)],
        ),
        compiler_params=params(),
        cost_estimate=pl.CostEstimate(
            flops=2 * rows * width * (sel_rows + 8), bytes_accessed=rows * width * 8, transcendentals=rows * width
        ),
    )(slot, start, xin, conv_w, sel_w)


def conv_kernel_bwd(
    slot, start, dsel_ref, part_ref, xc_ref, xin_ref, w_ref, sel_ref,
    dxin_ref, gw_ref, dext, ext,
):
    i = pl.program_id(0)
    units = pl.num_programs(0)
    u = units - 1 - i
    rows = xin_ref.shape[0]
    after = jnp.where(start[jnp.minimum(u + 1, units - 1)] == 1, 0.0, 1.0)

    @pl.when(i == 0)
    def _():
        dext[...] = jnp.zeros_like(dext)
        gw_ref[...] = jnp.zeros_like(gw_ref)

    dext[rows : rows + 8, :] = dext[0:8, :] * after
    xc = xc_ref[...]
    sig = sigmoid(xc)
    dxs = dot_nn(dsel_ref[...], sel_ref[...]) + part_ref[...]
    dxc = dxs * (sig * (1.0 + xc * (1.0 - sig)))
    dext[0:rows, :] = dxc
    acc = w_ref[CONV - 1 : CONV, :] * dxc
    for k in range(CONV - 1):
        off = CONV - 1 - k
        acc = acc + w_ref[k : k + 1, :] * dext[off : off + rows, :]
    dxin_ref[...] = acc.astype(BF16)
    xin = xin_ref[...].astype(F32)
    for k in range(CONV):
        off = CONV - 1 - k
        gw_ref[k : k + 1, :] += jnp.sum(dext[off : off + rows, :] * xin, axis=0, keepdims=True)


def conv_backward(slot, start, dsel, part, xc, xin, conv_w, sel_w, unit_rows):
    rows, width = xin.shape
    units = rows // unit_rows
    sel_rows = sel_w.shape[0]
    return pl.pallas_call(
        conv_kernel_bwd,
        out_shape=(
            jax.ShapeDtypeStruct((rows, width), BF16),
            jax.ShapeDtypeStruct((8, width), F32),
        ),
        grid_spec=pltpu.PrefetchScalarGridSpec(
            num_scalar_prefetch=2,
            grid=(units,),
            in_specs=[
                unit_spec(unit_rows, sel_rows, units),
                unit_spec(unit_rows, width, units),
                unit_spec(unit_rows, width, units),
                unit_spec(unit_rows, width, units),
                whole_spec((CONV, width)),
                whole_spec((sel_rows, width)),
            ],
            out_specs=[unit_spec(unit_rows, width, units), whole_spec((8, width))],
            scratch_shapes=[
                pltpu.VMEM((unit_rows + 8, width), F32),
                pltpu.VMEM((8, width), F32),
            ],
        ),
        compiler_params=params(),
        cost_estimate=pl.CostEstimate(
            flops=2 * rows * width * (sel_rows + 16), bytes_accessed=rows * width * 12, transcendentals=rows * width
        ),
    )(slot, start, dsel, part, xc, xin, conv_w, sel_w)


def step_sizes(low_ref, step_ref, bias_ref):
    pre = dot_nn(low_ref[...], step_ref[...]) + bias_ref[...]
    return jnp.maximum(pre, 0.0) + jnp.log(1.0 + jnp.exp(-jnp.abs(pre)))


def scan_kernel_fwd(
    slot, start, xs_ref, z_ref, low_ref, bc_ref, step_ref, bias_ref, rate_ref, skip_ref, gain_ref,
    y_ref, comb_ref, square_ref, begin_ref, dt_buf, dtx_buf, y_buf, state,
):
    u = pl.program_id(0)
    rows = xs_ref.shape[0]
    width = xs_ref.shape[1]
    keep = jnp.where(start[u] == 1, 0.0, 1.0)

    @pl.when(u == 0)
    def _():
        state[...] = jnp.zeros_like(state)

    xs = xs_ref[...].astype(F32)
    dt = step_sizes(low_ref, step_ref, bias_ref)
    dt_buf[...] = dt
    dtx_buf[...] = dt * xs
    first = state[...] * keep
    begin_ref[0] = first
    rate = rate_ref[...]
    bc = bc_ref[0]

    def group(g, h):
        base = pl.multiple_of(g * STEP_GROUP, STEP_GROUP)
        turned = pltpu.roll(bc, lax.rem(rows - base, rows), 1)
        for k in range(STEP_GROUP):
            dt_row = jnp.broadcast_to(dt_buf[pl.ds(base + k, 1), :], (STATE, width))
            dtx_row = jnp.broadcast_to(dtx_buf[pl.ds(base + k, 1), :], (STATE, width))
            b = jnp.broadcast_to(turned[0:STATE, k : k + 1], (STATE, width))
            c = jnp.broadcast_to(turned[STATE : 2 * STATE, k : k + 1], (STATE, width))
            h = jnp.exp2(dt_row * rate) * h + dtx_row * b
            y_buf[pl.ds(base + k, 1), :] = jnp.sum(c * h, axis=0, keepdims=True)
        return h

    state[...] = lax.fori_loop(0, rows // STEP_GROUP, group, first)
    y = y_buf[...] + skip_ref[...] * xs
    y_ref[...] = y
    z = z_ref[...].astype(F32)
    ys = y * (z * sigmoid(z))
    comb_ref[...] = (ys * gain_ref[...]).astype(BF16)
    square_ref[...] = jnp.broadcast_to(jnp.sum(ys * ys, axis=1, keepdims=True), square_ref.shape)


def scan_forward(slot, start, xs, z, low, bc, step_w, bias, rate2, skip, gain, unit_rows):
    rows, width = xs.shape
    units = rows // unit_rows
    rank = low.shape[1]
    return pl.pallas_call(
        scan_kernel_fwd,
        out_shape=(
            jax.ShapeDtypeStruct((rows, width), F32),
            jax.ShapeDtypeStruct((rows, width), BF16),
            jax.ShapeDtypeStruct((rows, 128), F32),
            jax.ShapeDtypeStruct((units, STATE, width), F32),
        ),
        grid_spec=pltpu.PrefetchScalarGridSpec(
            num_scalar_prefetch=2,
            grid=(units,),
            in_specs=[
                unit_spec(unit_rows, width),
                unit_spec(unit_rows, width),
                unit_spec(unit_rows, rank),
                pl.BlockSpec((1, 2 * STATE, unit_rows), lambda u, slot, *_: (slot[u], 0, 0)),
                whole_spec((rank, width)),
                whole_spec((1, width)),
                whole_spec((STATE, width)),
                whole_spec((1, width)),
                whole_spec((1, width)),
            ],
            out_specs=[
                unit_spec(unit_rows, width),
                unit_spec(unit_rows, width),
                unit_spec(unit_rows, 128),
                pl.BlockSpec((1, STATE, width), lambda u, *_: (u, 0, 0)),
            ],
            scratch_shapes=[
                pltpu.VMEM((unit_rows, width), F32),
                pltpu.VMEM((unit_rows, width), F32),
                pltpu.VMEM((unit_rows, width), F32),
                pltpu.VMEM((STATE, width), F32),
            ],
        ),
        compiler_params=params(),
        cost_estimate=pl.CostEstimate(
            flops=rows * width * STATE * 8, bytes_accessed=rows * width * 12,
            transcendentals=rows * width * STATE,
        ),
    )(slot, start, xs, z, low, bc, step_w, bias, rate2, skip, gain)


def scan_kernel_bwd(
    slot, start, dc_ref, stat_ref, y_ref, z_ref, xs_ref, low_ref, bc_ref, begin_ref,
    step_ref, bias_ref, rate_ref, skip_ref, gain_ref,
    dz_ref, part_ref, dlow_ref, dbc_ref, gstep_ref, gvec_ref, gdecay_ref,
    dt_buf, dtx_buf, dy_buf, gx_buf, ddt_buf, h_buf, da_buf, pb_buf, pc_buf, adj,
):
    i = pl.program_id(0)
    units = pl.num_programs(0)
    u = units - 1 - i
    rows = xs_ref.shape[0]
    width = xs_ref.shape[1]
    after = jnp.where(start[jnp.minimum(u + 1, units - 1)] == 1, 0.0, 1.0)

    @pl.when(i == 0)
    def _():
        adj[...] = jnp.zeros_like(adj)
        gstep_ref[...] = jnp.zeros_like(gstep_ref)
        gvec_ref[...] = jnp.zeros_like(gvec_ref)
        gdecay_ref[...] = jnp.zeros_like(gdecay_ref)

    xs = xs_ref[...].astype(F32)
    dt = step_sizes(low_ref, step_ref, bias_ref)
    dt_buf[...] = dt
    dtx_buf[...] = dt * xs
    rate = rate_ref[...]
    bc = bc_ref[0]
    h_buf[0] = begin_ref[0]

    def replay(g, h):
        base = pl.multiple_of(g * STEP_GROUP, STEP_GROUP)
        turned = pltpu.roll(bc, lax.rem(rows - base, rows), 1)
        for k in range(STEP_GROUP):
            dt_row = jnp.broadcast_to(dt_buf[pl.ds(base + k, 1), :], (STATE, width))
            dtx_row = jnp.broadcast_to(dtx_buf[pl.ds(base + k, 1), :], (STATE, width))
            b = jnp.broadcast_to(turned[0:STATE, k : k + 1], (STATE, width))
            da = jnp.exp2(dt_row * rate)
            da_buf[base + k] = da
            h = da * h + dtx_row * b
            h_buf[base + k + 1] = h
        return h

    lax.fori_loop(0, rows // STEP_GROUP, replay, begin_ref[0])

    factor = stat_ref[:, 0:1]
    shift = stat_ref[:, 1:2]
    z = z_ref[...].astype(F32)
    sig = sigmoid(z)
    gate = z * sig
    y = y_ref[...]
    ys = y * gate
    half = 0.5 * dc_ref[...]
    dys = factor * (half * gain_ref[...]) - ys * shift
    dy = dys * gate
    dz_ref[...] = (dys * y * (sig * (1.0 + z * (1.0 - sig)))).astype(BF16)
    dy_buf[...] = dy
    gvec_ref[0:1, :] += jnp.sum(half * ys * factor, axis=0, keepdims=True)
    gvec_ref[1:2, :] += jnp.sum(dy * xs, axis=0, keepdims=True)

    pairs = -(-width // 128)

    def fold(value):
        total = None
        for p in range(pairs):
            lo, hi = p * 128, min(width, p * 128 + 128)
            piece = value[:, lo:hi]
            if hi - lo < 128:
                piece = jnp.concatenate([piece, jnp.zeros((STATE, 128 - (hi - lo)), F32)], axis=1)
            total = piece if total is None else total + piece
        return total

    def group(index, carry):
        lam, acc = carry
        g = rows // STEP_GROUP - 1 - index
        base = pl.multiple_of(g * STEP_GROUP, STEP_GROUP)
        turned = pltpu.roll(bc, lax.rem(rows - base, rows), 1)
        for k in range(STEP_GROUP - 1, -1, -1):
            t = base + k
            dt_row = jnp.broadcast_to(dt_buf[pl.ds(t, 1), :], (STATE, width))
            dtx_row = jnp.broadcast_to(dtx_buf[pl.ds(t, 1), :], (STATE, width))
            dy_row = jnp.broadcast_to(dy_buf[pl.ds(t, 1), :], (STATE, width))
            b = jnp.broadcast_to(turned[0:STATE, k : k + 1], (STATE, width))
            c = jnp.broadcast_to(turned[STATE : 2 * STATE, k : k + 1], (STATE, width))
            lam = lam + c * dy_row
            pc_buf[t] = fold(dy_row * h_buf[t + 1])
            pb_buf[t] = fold(dtx_row * lam)
            gx_buf[pl.ds(t, 1), :] = jnp.sum(b * lam, axis=0, keepdims=True)
            lam = da_buf[t] * lam
            w = lam * h_buf[t]
            ddt_buf[pl.ds(t, 1), :] = jnp.sum(rate * w, axis=0, keepdims=True)
            acc = acc + dt_row * w
        return lam, acc

    lam, acc = lax.fori_loop(
        0, rows // STEP_GROUP, group, (adj[...] * after, jnp.zeros((STATE, width), F32))
    )
    adj[...] = lam
    gdecay_ref[...] += acc
    gx = gx_buf[...]
    part_ref[...] = gx * dt + skip_ref[...] * dy
    ddt = gx * xs + LN2 * ddt_buf[...]
    dpre = (ddt * (1.0 - jnp.exp(-dt))).astype(BF16)
    gstep_ref[...] += dot_tn(low_ref[...], dpre)
    gvec_ref[2:3, :] += jnp.sum(dpre.astype(F32), axis=0, keepdims=True)
    dlow_ref[...] = dot_nt(dpre, step_ref[...]).astype(BF16)
    ones = jnp.ones((8, 128), BF16)
    dbc_ref[0, 0] = dot_nt(ones, pb_buf[...].reshape(rows * STATE, 128).astype(BF16))
    dbc_ref[0, 1] = dot_nt(ones, pc_buf[...].reshape(rows * STATE, 128).astype(BF16))


def scan_backward(
    slot, start, dc, stat, y, z, xs, low, bc, begin, step_w, bias, rate2, skip, gain, unit_rows
):
    rows, width = xs.shape
    units = rows // unit_rows
    rank = low.shape[1]
    last = units - 1
    return pl.pallas_call(
        scan_kernel_bwd,
        out_shape=(
            jax.ShapeDtypeStruct((rows, width), BF16),
            jax.ShapeDtypeStruct((rows, width), F32),
            jax.ShapeDtypeStruct((rows, rank), BF16),
            jax.ShapeDtypeStruct((units, 2, 8, unit_rows * STATE), F32),
            jax.ShapeDtypeStruct((rank, width), F32),
            jax.ShapeDtypeStruct((8, width), F32),
            jax.ShapeDtypeStruct((STATE, width), F32),
        ),
        grid_spec=pltpu.PrefetchScalarGridSpec(
            num_scalar_prefetch=2,
            grid=(units,),
            in_specs=[
                unit_spec(unit_rows, width, units),
                unit_spec(unit_rows, 128, units),
                unit_spec(unit_rows, width, units),
                unit_spec(unit_rows, width, units),
                unit_spec(unit_rows, width, units),
                unit_spec(unit_rows, rank, units),
                pl.BlockSpec(
                    (1, 2 * STATE, unit_rows), lambda i, slot, *_: (slot[last - i], 0, 0)
                ),
                pl.BlockSpec((1, STATE, width), lambda i, *_: (last - i, 0, 0)),
                whole_spec((rank, width)),
                whole_spec((1, width)),
                whole_spec((STATE, width)),
                whole_spec((1, width)),
                whole_spec((1, width)),
            ],
            out_specs=[
                unit_spec(unit_rows, width, units),
                unit_spec(unit_rows, width, units),
                unit_spec(unit_rows, rank, units),
                pl.BlockSpec(
                    (1, 2, 8, unit_rows * STATE), lambda i, slot, *_: (slot[last - i], 0, 0, 0)
                ),
                whole_spec((rank, width)),
                whole_spec((8, width)),
                whole_spec((STATE, width)),
            ],
            scratch_shapes=[
                pltpu.VMEM((unit_rows, width), F32),
                pltpu.VMEM((unit_rows, width), F32),
                pltpu.VMEM((unit_rows, width), F32),
                pltpu.VMEM((unit_rows, width), F32),
                pltpu.VMEM((unit_rows, width), F32),
                pltpu.VMEM((unit_rows + 1, STATE, width), F32),
                pltpu.VMEM((unit_rows, STATE, width), F32),
                pltpu.VMEM((unit_rows, STATE, 128), F32),
                pltpu.VMEM((unit_rows, STATE, 128), F32),
                pltpu.VMEM((STATE, width), F32),
            ],
        ),
        compiler_params=params(),
        cost_estimate=pl.CostEstimate(
            flops=rows * width * STATE * 24, bytes_accessed=rows * width * 24,
            transcendentals=rows * width * STATE,
        ),
    )(slot, start, dc, stat, y, z, xs, low, bc, begin, step_w, bias, rate2, skip, gain)


def attn_kernel_fwd(slot, low_block, pair, q_ref, k_ref, v_ref, gain_ref, o_ref, comb_ref, stat_ref):
    u = pl.program_id(0)
    rows = q_ref.shape[0]
    heads = q_ref.shape[1] // HEAD_SIZE
    q = q_ref[...] * BF16(HEAD_SIZE**-0.5)
    queries = [q[:, h * HEAD_SIZE : (h + 1) * HEAD_SIZE] for h in range(heads)]

    def block(ref, which, j):
        first = pl.multiple_of(slot[2 * j] * rows, rows)
        second = pl.multiple_of(slot[2 * j + 1] * rows, rows)
        return jnp.concatenate([ref[which, pl.ds(first, rows), :], ref[which, pl.ds(second, rows), :]], axis=0)

    def body(j, carry):
        out = []
        for h in range(heads):
            top, total, acc = carry[h]
            s = dot_nt(queries[h], block(k_ref, pair[h], j))
            new_top = jnp.maximum(top, jnp.max(s, axis=1, keepdims=True))
            p = jnp.exp(s - new_top)
            fade = jnp.exp(top - new_top)
            total = total * fade + jnp.sum(p, axis=1, keepdims=True)
            acc = acc * fade + dot_nn(p.astype(BF16), block(v_ref, pair[h], j))
            out.append((new_top, total, acc))
        return tuple(out)

    start = tuple(
        (jnp.full((rows, 1), -1e30, F32), jnp.zeros((rows, 1), F32), jnp.zeros((rows, HEAD_SIZE), F32))
        for _ in range(heads)
    )
    result = lax.fori_loop(low_block[u], u // 2 + 1, body, start)
    lane = lax.broadcasted_iota(jnp.int32, (rows, 128), 1)
    stat = jnp.zeros((rows, 128), F32)
    outs = []
    for h in range(heads):
        top, total, acc = result[h]
        outs.append(acc / total)
        stat = jnp.where(lane == h, top + jnp.log(total), stat)
    o = outs[0] if heads == 1 else jnp.concatenate(outs, axis=1)
    o_ref[...] = o
    comb_ref[...] = (o * gain_ref[...]).astype(BF16)
    stat_ref[...] = jnp.where(lane == 127, jnp.sum(o * o, axis=1, keepdims=True), stat)


def attn_forward(slot, low_block, pair, q, k, v, gain, unit_rows):
    rows, width = q.shape
    units = rows // unit_rows
    return pl.pallas_call(
        attn_kernel_fwd,
        out_shape=(
            jax.ShapeDtypeStruct((rows, width), F32),
            jax.ShapeDtypeStruct((rows, width), BF16),
            jax.ShapeDtypeStruct((rows, 128), F32),
        ),
        grid_spec=pltpu.PrefetchScalarGridSpec(
            num_scalar_prefetch=3,
            grid=(units,),
            in_specs=[
                unit_spec(unit_rows, width),
                whole_spec(k.shape),
                whole_spec(v.shape),
                whole_spec((1, width)),
            ],
            out_specs=[
                unit_spec(unit_rows, width),
                unit_spec(unit_rows, width),
                unit_spec(unit_rows, 128),
            ],
        ),
        compiler_params=params(),
        cost_estimate=pl.CostEstimate(
            flops=2 * rows * rows * width, bytes_accessed=rows * width * 8,
            transcendentals=rows * rows * (width // HEAD_SIZE) // 2,
        ),
    )(slot, low_block, pair, q, k, v, gain)


def attn_kernel_bwd(
    slot, low_block, pair, q_ref, o_ref, do_ref, stat_ref, k_ref, v_ref, dq_ref, dk_ref, dv_ref
):
    u = pl.program_id(0)
    rows = q_ref.shape[0]
    heads = q_ref.shape[1] // HEAD_SIZE

    @pl.when(u == 0)
    def _():
        dk_ref[...] = jnp.zeros_like(dk_ref)
        dv_ref[...] = jnp.zeros_like(dv_ref)

    q = q_ref[...] * BF16(HEAD_SIZE**-0.5)
    do = do_ref[...]
    prod = do.astype(F32) * o_ref[...]
    stat = stat_ref[...]
    cut = lambda a, h: a[:, h * HEAD_SIZE : (h + 1) * HEAD_SIZE]
    queries = [cut(q, h) for h in range(heads)]
    grads = [cut(do, h) for h in range(heads)]
    deltas = [jnp.sum(cut(prod, h), axis=1, keepdims=True) for h in range(heads)]

    def body(j, carry):
        first = pl.multiple_of(slot[2 * j] * rows, rows)
        second = pl.multiple_of(slot[2 * j + 1] * rows, rows)
        out = []
        for h in range(heads):
            which = pair[h]
            kb = jnp.concatenate([k_ref[which, pl.ds(first, rows), :], k_ref[which, pl.ds(second, rows), :]], axis=0)
            vb = jnp.concatenate([v_ref[which, pl.ds(first, rows), :], v_ref[which, pl.ds(second, rows), :]], axis=0)
            p = jnp.exp(dot_nt(queries[h], kb) - stat[:, h : h + 1])
            ds = (p * (dot_nt(grads[h], vb) - deltas[h])).astype(BF16)
            dv = dot_tn(p.astype(BF16), grads[h])
            dk = dot_tn(ds, queries[h])
            dv_ref[which, pl.ds(first, rows), :] += dv[0:rows]
            dv_ref[which, pl.ds(second, rows), :] += dv[rows : 2 * rows]
            dk_ref[which, pl.ds(first, rows), :] += dk[0:rows]
            dk_ref[which, pl.ds(second, rows), :] += dk[rows : 2 * rows]
            out.append(carry[h] + dot_nn(ds, kb))
        return tuple(out)

    start = tuple(jnp.zeros((rows, HEAD_SIZE), F32) for _ in range(heads))
    result = lax.fori_loop(low_block[u], u // 2 + 1, body, start)
    dq = result[0] if heads == 1 else jnp.concatenate(result, axis=1)
    dq_ref[...] = (dq * HEAD_SIZE**-0.5).astype(BF16)


def attn_backward(slot, low_block, pair, q, o, do, stat, k, v, unit_rows):
    rows, width = q.shape
    units = rows // unit_rows
    return pl.pallas_call(
        attn_kernel_bwd,
        out_shape=(
            jax.ShapeDtypeStruct((rows, width), BF16),
            jax.ShapeDtypeStruct(k.shape, F32),
            jax.ShapeDtypeStruct(v.shape, F32),
        ),
        grid_spec=pltpu.PrefetchScalarGridSpec(
            num_scalar_prefetch=3,
            grid=(units,),
            in_specs=[
                unit_spec(unit_rows, width),
                unit_spec(unit_rows, width),
                unit_spec(unit_rows, width),
                unit_spec(unit_rows, 128),
                whole_spec(k.shape),
                whole_spec(v.shape),
            ],
            out_specs=[unit_spec(unit_rows, width), whole_spec(k.shape), whole_spec(v.shape)],
        ),
        compiler_params=params(),
        cost_estimate=pl.CostEstimate(
            flops=5 * rows * rows * width, bytes_accessed=rows * width * 12,
            transcendentals=rows * rows * (width // HEAD_SIZE) // 2,
        ),
    )(slot, low_block, pair, q, o, do, stat, k, v)


def rows_gather(value):
    return lax.all_gather(value, "ctx", axis=0, tiled=True)


def rows_scatter(value):
    return lax.psum_scatter(value, "ctx", scatter_dimension=0, tiled=True)


def lane_gather(value):
    return lax.all_gather(value, "fsdp", axis=0, tiled=True)


def lane_scatter(value):
    return lax.psum_scatter(value, "fsdp", scatter_dimension=0, tiled=True)


def columns_to_rows(value, devices):
    width = value.shape[1]
    blocks = value.reshape(devices, -1, width)
    got = lax.all_to_all(blocks, "ctx", split_axis=0, concat_axis=0, tiled=True)
    return jnp.transpose(got, (1, 0, 2)).reshape(-1, devices * width)


def rows_to_columns(value, devices):
    rows = value.shape[0]
    blocks = jnp.transpose(value.reshape(rows, devices, -1), (1, 0, 2))
    got = lax.all_to_all(blocks, "ctx", split_axis=0, concat_axis=0, tiled=True)
    return got.reshape(devices * rows, -1)


def pair_routes(devices):
    half = devices // 2
    first = [(d, 2 * d) for d in range(half)] + [(d, 2 * (d - half) + 1) for d in range(half, devices)]
    second = [(d, 2 * d + 1) for d in range(half)] + [(d, 2 * (d - half)) for d in range(half, devices)]
    return first, second


def split_pairs(value, place, devices):
    width = value.shape[1] // 2
    first, second = pair_routes(devices)
    low, high = value[:, :width], value[:, width:]
    early = place < devices // 2
    got_a = lax.ppermute(jnp.where(early, low, high), "ctx", first)
    got_b = lax.ppermute(jnp.where(early, high, low), "ctx", second)
    even = place % 2 == 0
    return jnp.where(even, got_a, got_b), jnp.where(even, got_b, got_a)


def join_pairs(left, right, place, devices):
    first, second = pair_routes(devices)
    even = place % 2 == 0
    got_a = lax.ppermute(jnp.where(even, left, right), "ctx", [(b, a) for a, b in first])
    got_b = lax.ppermute(jnp.where(even, right, left), "ctx", [(b, a) for a, b in second])
    early = place < devices // 2
    return jnp.concatenate([jnp.where(early, got_a, got_b), jnp.where(early, got_b, got_a)], axis=1)


def pad_to(value, size, axis):
    widths = [(0, 0)] * value.ndim
    widths[axis] = (0, size - value.shape[axis])
    return jnp.pad(value, widths)


def rms_factor(value):
    return lax.rsqrt(jnp.mean(value * value, axis=-1, keepdims=True) + EPS)


def norm_back(value, factor, gain, grad):
    weighted = grad * gain
    d_value = factor * weighted - value * factor * factor * factor * jnp.mean(
        value * weighted, axis=-1, keepdims=True
    )
    return d_value, jnp.sum(grad * value * factor, axis=0)


def shards(
    tokens, cotangent, unit_order, block_seq, meta_tokens, input_gain, query_key_value_weight, w_xz,
    conv_kernel, state_proj, step_proj, step_bias, decay_log, skip_gain, attn_gain, ssm_gain,
    out_proj, ffn_gain, w_gate, w_up, w_down,
):
    devices = lax.axis_size("ctx")
    lanes = lax.axis_size("fsdp")
    place = lax.axis_index("ctx")
    own_rows = tokens.shape[1]
    model = tokens.shape[2]
    unit_rows = own_rows // 2
    slot_unit = unit_order[0]
    units = slot_unit.shape[0]
    rows = units * unit_rows
    width = conv_kernel.shape[1]
    hidden_width = w_gate.shape[1]
    heads = -(-QUERY_HEADS // devices)
    head_width = heads * HEAD_SIZE
    group = QUERY_HEADS // KEY_VALUE_HEADS
    query_width = QUERY_HEADS * HEAD_SIZE
    kv_width = KEY_VALUE_HEADS * HEAD_SIZE
    model_part = input_gain.shape[0]

    slot_ids = jnp.arange(units, dtype=jnp.int32)
    place_of = jnp.sum(
        jnp.where(slot_unit[None, :] == slot_ids[:, None], slot_ids[None, :], 0), axis=1
    ).astype(jnp.int32)
    unit_seq = jnp.repeat(block_seq[0], 2)
    starts = jnp.concatenate([jnp.ones((1,), jnp.bool_), unit_seq[1:] != unit_seq[:-1]])
    starts_int = starts.astype(jnp.int32)
    low_block = (jnp.sum(unit_seq[None, :] < unit_seq[:, None], axis=1) // 2).astype(jnp.int32)
    my_units = lax.dynamic_slice_in_dim(slot_unit, 2 * place, 2)
    my_start = jnp.any((my_units[:, None] == slot_ids[None, :]) & starts[None, :], axis=1)

    small = jnp.concatenate([conv_kernel, state_proj, step_proj, decay_log], axis=0)
    small_all = lax.all_gather(small, "fsdp", axis=0)
    marks = [conv_kernel.shape[0], state_proj.shape[0], step_proj.shape[0], decay_log.shape[0]]
    ends = [sum(marks[: i + 1]) for i in range(4)]
    conv_w = small_all[:, : ends[0]].reshape(-1, width).astype(F32)
    sel_w = small_all[:, ends[0] : ends[1]].reshape(-1, width)
    step_w = small_all[:, ends[1] : ends[2]].reshape(-1, width)
    decay = small_all[:, ends[2] :].reshape(-1, width).astype(F32)
    rate = -jnp.exp(decay)
    rate2 = rate * LOG2E
    meta_part = lax.all_gather(meta_tokens, "fsdp", axis=0, tiled=True)
    meta_rows = meta_part.shape[0]
    wide = jnp.concatenate(
        [meta_part, input_gain[None], ffn_gain[None], attn_gain[None]], axis=0
    )
    wide = lax.all_gather(wide, "ctx", axis=1, tiled=True).astype(F32)
    meta = wide[:meta_rows]
    gain_in = wide[meta_rows]
    gain_ffn = wide[meta_rows + 1]
    gain_attn = lax.dynamic_slice_in_dim(
        pad_to(wide[meta_rows + 2], devices * head_width, 0), place * head_width, head_width
    )[None]
    bias = step_bias.astype(F32)[None]
    skip = skip_gain.astype(F32)[None]
    gain_ssm = ssm_gain.astype(F32)[None]

    first_kv = (place * heads) // group
    qkv_row = lax.all_gather(query_key_value_weight, "ctx", axis=1, tiled=True)
    q_part = lax.dynamic_slice_in_dim(
        pad_to(qkv_row[:, :query_width], devices * head_width, 1), place * head_width, head_width, 1
    )
    kv_room = (devices * heads // group + 3) * HEAD_SIZE
    k_part = lax.dynamic_slice_in_dim(
        pad_to(qkv_row[:, query_width : query_width + kv_width], kv_room, 1),
        first_kv * HEAD_SIZE, 2 * HEAD_SIZE, 1,
    )
    v_part = lax.dynamic_slice_in_dim(
        pad_to(qkv_row[:, query_width + kv_width :], kv_room, 1),
        first_kv * HEAD_SIZE, 2 * HEAD_SIZE, 1,
    )
    pair = jnp.clip(
        (place * heads + jnp.arange(heads, dtype=jnp.int32)) // group - first_kv, 0, 1
    ).astype(jnp.int32)
    x_part, z_part = split_pairs(w_xz, place, devices)
    in_w = lane_gather(jnp.concatenate([q_part, k_part, v_part, x_part, z_part], axis=1))
    qkv_width = head_width + 4 * HEAD_SIZE
    qkv_w = in_w[:, :qkv_width]
    x_w = in_w[:, qkv_width : qkv_width + width]
    z_w = in_w[:, qkv_width + width :]

    out_cols = lane_gather(out_proj)
    blocks = jnp.concatenate(
        [
            pad_to(out_cols[:query_width], devices * head_width, 0).reshape(
                devices, head_width, model_part
            ),
            out_cols[query_width:].reshape(devices, width, model_part),
        ],
        axis=1,
    )
    out_w = columns_to_rows(blocks.reshape(-1, model_part), devices)
    gate_w = lane_gather(w_gate)
    up_w = lane_gather(w_up)
    down_w = columns_to_rows(lane_gather(w_down), devices)

    own_tok = tokens[0]
    resid = jnp.where(
        my_start[:, None, None], meta[None], own_tok.reshape(2, unit_rows, model).astype(F32)
    ).reshape(own_rows, model)
    in_factor = rms_factor(resid)
    normed = rows_gather((resid * in_factor * gain_in).astype(BF16))
    cot = rows_gather(cotangent[0])

    qkv = dot_nn(normed, qkv_w).astype(BF16)
    queries = qkv[:, :head_width]
    keys = jnp.transpose(
        qkv[:, head_width : head_width + 2 * HEAD_SIZE].reshape(rows, 2, HEAD_SIZE), (1, 0, 2)
    )
    values = jnp.transpose(
        qkv[:, head_width + 2 * HEAD_SIZE :].reshape(rows, 2, HEAD_SIZE), (1, 0, 2)
    )
    x_in = dot_nn(normed, x_w).astype(BF16)
    z_gate = dot_nn(normed, z_w).astype(BF16)
    conv_out, ssm_in, select = conv_forward(place_of, starts_int, x_in, conv_w, sel_w, unit_rows)
    select = lax.psum(select, "ctx").astype(F32)
    attn, attn_comb, attn_stat = attn_forward(
        place_of, low_block, pair, queries, keys, values, gain_attn, unit_rows
    )
    attn_out = rows_scatter(dot_nn(attn_comb, out_w[:head_width]).astype(BF16)).astype(F32)
    step_low = select[:, :DT_RANK].astype(BF16)
    bc = jnp.transpose(select[:, DT_RANK:].reshape(units, unit_rows, 2 * STATE), (0, 2, 1))
    y_total, ssm_comb, ssm_square, begins = scan_forward(
        place_of, starts_int, ssm_in, z_gate, step_low, bc, step_w, bias, rate2, skip, gain_ssm,
        unit_rows,
    )
    ssm_out = rows_scatter(dot_nn(ssm_comb, out_w[head_width:]).astype(BF16)).astype(F32)
    squares = jnp.stack([attn_stat[:, 127], ssm_square[:, 0]])
    squares = jnp.sum(lax.all_gather(squares, "ctx", axis=0), axis=0)
    factors = lax.rsqrt(
        squares / jnp.array([[query_width], [devices * width]], F32) + EPS
    )
    own_factors = lax.dynamic_slice_in_dim(factors, place * own_rows, own_rows, 1)
    mid = (
        resid
        + 0.5 * own_factors[0][:, None] * attn_out
        + 0.5 * own_factors[1][:, None] * ssm_out
    )
    mid_factor = rms_factor(mid)
    ffn_in = rows_gather((mid * mid_factor * gain_ffn).astype(BF16))

    gate = dot_nn(ffn_in, gate_w)
    up = dot_nn(ffn_in, up_w)
    sig = sigmoid(gate)
    act = gate * sig
    hidden = (act * up).astype(BF16)
    d_hidden = dot_nt(cot, down_w)
    d_gate = (d_hidden * up * (sig * (1.0 + gate * (1.0 - sig)))).astype(BF16)
    d_up = (d_hidden * act).astype(BF16)
    d_ffn = rows_scatter((dot_nt(d_gate, gate_w) + dot_nt(d_up, up_w)).astype(BF16)).astype(F32)
    ffn_out = rows_scatter(dot_nn(hidden, down_w).astype(BF16)).astype(F32)
    layer_out = (mid + ffn_out).astype(BF16)[None]
    gate_grad = lane_scatter(dot_tn(ffn_in, d_gate).astype(BF16)).astype(F32)
    up_grad = lane_scatter(dot_tn(ffn_in, d_up).astype(BF16)).astype(F32)
    down_grad = lane_scatter(
        rows_to_columns(dot_tn(hidden, cot).astype(BF16), devices)
    ).astype(F32)

    d_mid_norm, ffn_gain_part = norm_back(mid, mid_factor, gain_ffn, d_ffn)
    d_mid = cotangent[0].astype(F32) + d_mid_norm
    d_branch_own = d_mid.astype(BF16)
    d_branch = rows_gather(d_branch_own)
    branch_f = d_branch_own.astype(F32)
    dots = jnp.stack(
        [
            jnp.sum(branch_f * attn_out, axis=1) * (0.5 / query_width),
            jnp.sum(branch_f * ssm_out, axis=1) * (0.5 / (devices * width)),
        ]
    )
    dots = lax.all_gather(dots, "ctx", axis=1, tiled=True)
    shifts = dots * factors * factors * factors

    d_comb_attn = dot_nt(d_branch, out_w[:head_width])
    d_comb_ssm = dot_nt(d_branch, out_w[head_width:])
    attn_mixed = (attn * (0.5 * factors[0][:, None] * gain_attn)).astype(BF16)
    ssm_mixed = (ssm_comb.astype(F32) * (0.5 * factors[1][:, None])).astype(BF16)
    out_part = dot_tn(jnp.concatenate([attn_mixed, ssm_mixed], axis=1), d_branch).astype(BF16)
    out_back = rows_to_columns(out_part, devices).reshape(devices, -1, model_part)
    out_grad = lane_scatter(
        jnp.concatenate(
            [
                out_back[:, :head_width].reshape(-1, model_part)[:query_width],
                out_back[:, head_width:].reshape(-1, model_part),
            ],
            axis=0,
        )
    ).astype(F32)
    half = 0.5 * d_comb_attn
    d_attn = factors[0][:, None] * (half * gain_attn) - attn * shifts[0][:, None]
    attn_gain_part = jnp.sum(half * attn * factors[0][:, None], axis=0)
    stat = jnp.transpose(pad_to(jnp.stack([factors[1], shifts[1]]), 128, 0))
    d_z, x_part_grad, d_low, d_bc, step_grad, vec_grads, decay_sum = scan_backward(
        place_of, starts_int, d_comb_ssm, stat, y_total, z_gate, ssm_in, step_low, bc, begins,
        step_w, bias, rate2, skip, gain_ssm, unit_rows,
    )
    d_bc = jnp.transpose(
        d_bc[:, :, 0].reshape(units, 2, unit_rows, STATE), (0, 2, 1, 3)
    ).reshape(rows, 2 * STATE)
    d_select = lax.psum(jnp.concatenate([d_low, d_bc.astype(BF16)], axis=1), "ctx")
    d_query, d_keys, d_values = attn_backward(
        place_of, low_block, pair, queries, attn, d_attn.astype(BF16), attn_stat, keys, values,
        unit_rows,
    )
    d_x, conv_grads = conv_backward(
        place_of, starts_int, d_select, x_part_grad, conv_out, x_in, conv_w, sel_w, unit_rows
    )
    select_grad = dot_tn(d_select, ssm_in)
    d_in = jnp.concatenate(
        [
            d_query,
            jnp.transpose(d_keys, (1, 0, 2)).reshape(rows, 2 * HEAD_SIZE).astype(BF16),
            jnp.transpose(d_values, (1, 0, 2)).reshape(rows, 2 * HEAD_SIZE).astype(BF16),
            d_x,
            d_z,
        ],
        axis=1,
    )
    d_normed = rows_scatter(dot_nt(d_in, in_w).astype(BF16)).astype(F32)
    in_grad = lane_scatter(dot_tn(normed, d_in).astype(BF16))
    xz_grad = join_pairs(
        in_grad[:, qkv_width : qkv_width + width], in_grad[:, qkv_width + width :], place, devices
    ).astype(F32)
    spread = jnp.zeros((in_grad.shape[0], devices * head_width), BF16)
    spread = lax.dynamic_update_slice_in_dim(spread, in_grad[:, :head_width], place * head_width, 1)
    kv_zero = jnp.zeros((in_grad.shape[0], kv_room), BF16)
    qkv_full = jnp.concatenate(
        [
            spread[:, :query_width],
            lax.dynamic_update_slice_in_dim(
                kv_zero, in_grad[:, head_width : head_width + 2 * HEAD_SIZE],
                first_kv * HEAD_SIZE, 1,
            )[:, :kv_width],
            lax.dynamic_update_slice_in_dim(
                kv_zero, in_grad[:, head_width + 2 * HEAD_SIZE : qkv_width],
                first_kv * HEAD_SIZE, 1,
            )[:, :kv_width],
        ],
        axis=1,
    )
    part = query_key_value_weight.shape[1]
    qkv_blocks = jnp.transpose(qkv_full.reshape(-1, devices, part), (1, 0, 2))
    qkv_grad = jnp.sum(
        lax.all_to_all(qkv_blocks, "ctx", split_axis=0, concat_axis=0, tiled=True).astype(F32), axis=0
    )

    d_norm_in, in_gain_part = norm_back(resid, in_factor, gain_in, d_normed)
    d_resid = (d_mid + d_norm_in).reshape(2, unit_rows, model)
    flag = my_start[:, None, None]
    tokens_grad = jnp.where(flag, 0.0, d_resid).reshape(1, own_rows, model).astype(BF16)
    meta_sum = jnp.sum(jnp.where(flag, d_resid, 0.0), axis=0)

    gain_rows = jnp.stack(
        [
            in_gain_part,
            ffn_gain_part,
            lax.dynamic_update_slice_in_dim(
                jnp.zeros((devices * head_width,), F32), attn_gain_part, place * head_width, 0
            )[:query_width],
        ]
    )
    by_lane = jnp.concatenate(
        [
            meta_sum.reshape(lanes, -1, model),
            jnp.broadcast_to(gain_rows[None], (lanes, 3, model)),
        ],
        axis=1,
    )
    count = by_lane.shape[1]
    packed = jnp.transpose(
        by_lane.reshape(lanes, count, devices, model_part), (0, 2, 1, 3)
    ).reshape(lanes * devices, count, model_part)
    totals = jnp.sum(
        lax.all_to_all(
            packed.astype(BF16), ("fsdp", "ctx"), split_axis=0, concat_axis=0, tiled=True
        ).astype(F32),
        axis=0,
    )
    local = jnp.concatenate(
        [conv_grads[:CONV], select_grad, step_grad, rate * decay_sum, vec_grads[:3]], axis=0
    )
    local = jnp.sum(lax.all_gather(local, "fsdp", axis=0), axis=0)
    lane_place = lax.axis_index("fsdp")

    def lane_part(begin, count):
        each = count // lanes
        return lax.dynamic_slice_in_dim(local, begin + lane_place * each, each, 0)

    sel_count = select_grad.shape[0]
    at = [CONV, CONV + sel_count, CONV + sel_count + DT_RANK, CONV + sel_count + DT_RANK + STATE]
    return (
        layer_out,
        tokens_grad,
        totals[: count - 3],
        totals[count - 3],
        qkv_grad,
        xz_grad,
        lane_part(0, CONV),
        lane_part(at[0], sel_count),
        lane_part(at[1], DT_RANK),
        local[at[3] + 2],
        lane_part(at[2], STATE),
        local[at[3] + 1],
        totals[count - 1],
        local[at[3]],
        out_grad,
        totals[count - 2],
        gate_grad,
        up_grad,
        down_grad,
    )


def solution(mesh):
    rows = P("fsdp", "ctx", None)
    index = P("fsdp", None)
    mat = P("fsdp", "ctx")
    vec = P("ctx")
    return jax.shard_map(
        shards,
        mesh=mesh,
        in_specs=(
            rows, rows, index, index, mat, vec, mat, mat, mat, mat, mat, vec, mat, vec, vec, vec,
            mat, vec, mat, mat, mat,
        ),
        out_specs=(
            rows, rows, mat, vec, mat, mat, mat, mat, mat, vec, mat, vec, vec, vec, mat, vec, mat,
            mat, mat,
        ),
        check_vma=False,
    )
```

time: 4410 us -> 1630 us (0.37)
  waiting for transfers between devices: 1940 us -> 715 us
  local copies, waits for them, and re-layouts: 918 us -> 137 us
  other arithmetic: 662 us -> 56.4 us
  Pallas kernels: 0 us -> 347 us
  blocking collectives: 470 us -> 133 us
  matrix products: 332 us -> 182 us
    unnamed x67 -> x25, waiting for transfers between devices: 595 us -> 42.9 us
    all_gather x26 -> x11, waiting for transfers between devices: 771 us -> 363 us  [the longest x4 174 us: rows_gather(): return lax.all_gather(value, 'ctx', axis=0, tiled=True)]
    pallas_call x0 -> x6, Pallas kernels: none -> 347 us  [the longest x1 145 us: scan_backward(): pl.pallas_call(scan_kernel_bwd, out_shape=(jax.ShapeDtypeStruct((rows, wi...]
    while x827 -> x0, local copies, waits for them, and re-layouts: 300 us -> none
    all_gather x23 -> x5, blocking collectives: 349 us -> 60.8 us  [the longest x1 18.8 us: shards(): small_all = lax.all_gather(small, 'fsdp', axis=0)]
    reduce_scatter x8, waiting for transfers between devices: 575 us -> 294 us  [the longest x5 235 us: rows_scatter(): return lax.psum_scatter(value, 'ctx', scatter_dimension=0, tiled=True)]
    reduce_sum x210 -> x10, other arithmetic: 257 us -> 19.5 us  [the longest x1 6.96 us: shards(): meta_sum = jnp.sum(jnp.where(flag, d_resid, 0.0), axis=0)]
    while x408 -> x0, other arithmetic: 221 us -> none
  transfers between devices with their start and end apart: 51 -> 31, of which waited for: 35 -> 18; matrix products, arithmetic and copies ran while one was open for 42% -> 18% of each run, Pallas kernels for 0% -> 12%
where the time goes in v1:
time: 1630 us; the launch traced here: 1610 us
  waiting for transfers between devices  715 us (44%)
  Pallas kernels  347 us (21%)
  matrix products  182 us (11%)
  local copies, waits for them, and re-layouts  137 us (8%)
  blocking collectives  133 us (8%)
  other arithmetic  56.4 us (3%)
  starting transfers between devices  26.6 us (2%)
    reduce_scatter x5, waiting for transfers between devices, rows_scatter(): return lax.psum_scatter(value, 'ctx', scatter_dimension=0, tiled=True)  235 us
    all_gather x4, waiting for transfers between devices, rows_gather(): return lax.all_gather(value, 'ctx', axis=0, tiled=True)  174 us
    all_gather x5, waiting for transfers between devices, lane_gather(): return lax.all_gather(value, 'fsdp', axis=0, tiled=True)  166 us
    pallas_call x1, Pallas kernels, scan_backward(): pl.pallas_call(scan_kernel_bwd, out_shape=(jax.ShapeDtypeStruct((rows, wi...  145 us
    all_to_all x2, blocking collectives, rows_to_columns(): got = lax.all_to_all(blocks, 'ctx', split_axis=0, concat_axis=0, tiled=True)  72.4 us
    pallas_call x1, Pallas kernels, scan_forward(): pl.pallas_call(scan_kernel_fwd, out_shape=(jax.ShapeDtypeStruct((rows, wi...  67.7 us
    dot_general x8, matrix products, dot_nn(): lax.dot_general(left, right, (((1,), (0,)), ((), ())), preferred_element_...  66.6 us
    pallas_call x1, Pallas kernels, attn_backward(): pl.pallas_call(attn_kernel_bwd, out_shape=(jax.ShapeDtypeStruct((rows, wi...  63.4 us
  transfers between devices with their start and end apart: 31, of which 18 were waited for; matrix products, arithmetic and copies ran while one was open for 18% of the time, Pallas kernels for 12%

profile of v1, /device:TPU:0, one launch (start us, length us, event | category | flops | bytes accessed | tf_op | source)
XLA Modules:
  0.0 1614.3 jit_solution(12230478699839294405)
XLA Ops:
  11.4 7.6 collective-permute-done.1
  19.1 23.8 %all-gather.24.cloned.1.call-done = bf16[400,2240]{0,1:T(8,128)(2,1)} async-done(((bf16[400,280]{0,1:T(8,128)(2,1)}), bf16[400,2240]{0,1:T(8,128)(2,1)}) %all-gather.24.cloned.1.call-update) | async-done | bytes 1792016 | tf_op jit(solution)/shard_map/all_gather | solution.py:741
  48.8 13.6 all_gather.57
  62.4 10.0 all-gather.4
  82.9 7.2 all-gather.38.cloned.1.call-done
  116.3 18.8 %all-gather.5 = bf16[4,63,400]{2,1,0:T(8,128)(2,1)S(1)} all-gather(bf16[1,63,400]{2,1,0:T(8,128)(2,1)S(1)} %maximum_bitcast_fusion.2), channel_id=2, replica_groups=mesh['ctx'=8,'fsdp'=4] {'fsdp'}, dimensions={0}, use_global_device_ids=true | all-gather | bytes 252000 | tf_op jit(solution)/shard_map/all_gather | solution.py:715
  147.9 33.7 %all-gather.26.cloned.1.call-done = bf16[1600,1312]{1,0:T(8,128)(2,1)} async-done(((bf16[400,1312]{1,0:T(8,128)(2,1)}), bf16[1600,1312]{1,0:T(8,128)(2,1)}) %all-gather.26.cloned.1.call-update) | async-done | bytes 4198416 | tf_op jit(solution)/shard_map/all_gather | solution.py:614
  181.6 48.7 %all-gather.22.cloned.1.call-done = bf16[2048,1600]{0,1:T(8,128)(2,1)} async-done(((bf16[256,1600]{0,1:T(8,128)(2,1)}), bf16[2048,1600]{0,1:T(8,128)(2,1)}) %all-gather.22.cloned.1.call-update) | async-done | bytes 6553616 | tf_op jit(solution)/shard_map/all_gather | solution.py:606
  230.3 7.3 convolution_convert_fusion.10
  243.6 8.7 convolution_convert_fusion.9.xin_ref
  252.3 13.3 shard_map.358
  265.9 41.5 %shard_map.357 = (f32[2048,256]{1,0:T(8,128)}, bf16[2048,256]{1,0:T(8,128)(2,1)}, f32[2048,128]{1,0:T(8,128)}) custom-call(s32[16]{0:T(128)} %select_reduce_fusion.1.slot, s32[16]{0:T(128)} %and_select_fusion.1.low_block, s32[4]{0:T(128)} %subtract_clamp_fusion.pair, bf16[2048,256]{1,0:T(8,128)(2,1)} %slice.252.q_ref, bf16[2,2048,64]{2,1,0:T(8,128)(2,1)} %bitcast.199, ...), custom_call_target="tpu_custom_call" | custom-call | flops 2147483648 | bytes 4194304 | tf_op jit(solution)/shard_map/pallas_call | solution.py:498
  320.2 8.7 convolution_convert_fusion.8.z_ref
  333.2 67.7 %shard_map.359 = (f32[2048,400]{1,0:T(8,128)}, bf16[2048,400]{1,0:T(8,128)(2,1)}, f32[2048,128]{1,0:T(8,128)}, f32[16,16,400]{2,1,0:T(8,128)}) custom-call(s32[16]{0:T(128)} %select_reduce_fusion.1.slot, s32[16]{0:T(128)} %get-tuple-element.212.start, bf16[2048,400]{1,0:T(8,128)(2,1)} %get-tuple-element.42.xs_ref, ...), custom_call_target="tpu_custom_call" | custom-call | flops 104857600 | bytes 9830400 | tf_op jit(solution)/shard_map/pallas_call | solution.py:230
  401.0 7.1 convolution_convert_fusion.3
  411.9 9.5 all-gather.6
  421.6 52.7 %reduce-scatter.17.cloned.1.call-done = bf16[256,1600]{0,1:T(8,128)(2,1)} async-done(((bf16[2048,1600]{0,1:T(8,128)(2,1)}), bf16[256,1600]{0,1:T(8,128)(2,1)}) %reduce-scatter.17.cloned.1.call-update) | async-done | bytes 819216 | tf_op jit(solution)/shard_map/reduce_scatter | solution.py:610
  478.8 45.7 %all-gather.40.cloned.1.call-done = bf16[4,1376,200]{1,2,0:T(8,128)(2,1)} async-done(((bf16[1,1376,200]{1,2,0:T(8,128)(2,1)}), bf16[4,1376,200]{1,2,0:T(8,128)(2,1)}) %all-gather.40.cloned.1.call-update) | async-done | bytes 2201616 | tf_op jit(solution)/shard_map/all_gather | solution.py:614
  541.8 35.3 %all-gather.32.cloned.1.call-done = bf16[1600,688]{1,0:T(8,128)(2,1)} async-done(((bf16[400,688]{1,0:T(8,128)(2,1)}), bf16[1600,688]{1,0:T(8,128)(2,1)}) %all-gather.32.cloned.1.call-update) | async-done | bytes 2201616 | tf_op jit(solution)/shard_map/all_gather | solution.py:614
  577.1 49.0 %all-gather.28.cloned.1.call-done = bf16[2048,1600]{0,1:T(8,128)(2,1)} async-done(((bf16[256,1600]{0,1:T(8,128)(2,1)}), bf16[2048,1600]{0,1:T(8,128)(2,1)}) %all-gather.28.cloned.1.call-update) | async-done | bytes 6553616 | tf_op jit(solution)/shard_map/all_gather | solution.py:606
  626.0 9.8 fusion.54
  635.8 44.0 %all-gather.30.cloned.1.call-done = bf16[1600,688]{1,0:T(8,128)(2,1)} async-done(((bf16[400,688]{1,0:T(8,128)(2,1)}), bf16[1600,688]{1,0:T(8,128)(2,1)}) %all-gather.30.cloned.1.call-update) | async-done | bytes 2201616 | tf_op jit(solution)/shard_map/all_gather | solution.py:614
  679.7 9.8 fusion.53
  689.5 38.6 %all-gather.36.cloned.1.call-done = bf16[1,2048,1600]{1,2,0:T(8,128)(2,1)} async-done(((bf16[1,256,1600]{1,2,0:T(8,128)(2,1)}), bf16[1,2048,1600]{1,2,0:T(8,128)(2,1)}) %all-gather.36.cloned.1.call-update) | async-done | bytes 6553616 | tf_op jit(solution)/shard_map/all_gather | solution.py:606
  728.1 15.3 multiply_convert_fusion
  743.4 7.3 fusion.57
  750.7 9.2 add_convert_fusion
  760.0 9.3 convolution_convert_fusion
  769.4 53.7 %reduce-scatter.21.cloned.1.call-done = bf16[256,1600]{0,1:T(8,128)(2,1)} async-done(((bf16[2048,1600]{0,1:T(8,128)(2,1)}), bf16[256,1600]{0,1:T(8,128)(2,1)}) %reduce-scatter.21.cloned.1.call-update) | async-done | bytes 819216 | tf_op jit(solution)/shard_map/reduce_scatter | solution.py:610
  825.1 64.7 %reduce-scatter.19.cloned.1.call-done = bf16[256,1600]{0,1:T(8,128)(2,1)} async-done(((bf16[2048,1600]{0,1:T(8,128)(2,1)}), bf16[256,1600]{0,1:T(8,128)(2,1)}) %reduce-scatter.19.cloned.1.call-update) | async-done | bytes 819216 | tf_op jit(solution)/shard_map/reduce_scatter | solution.py:610
  893.8 8.9 all_gather.73
  904.3 37.4 %all-gather.34.cloned.1.call-done = bf16[2048,1600]{0,1:T(8,128)(2,1)} async-done(((bf16[256,1600]{0,1:T(8,128)(2,1)}), bf16[2048,1600]{0,1:T(8,128)(2,1)}) %all-gather.34.cloned.1.call-update) | async-done | bytes 6553616 | tf_op jit(solution)/shard_map/all_gather | solution.py:606
  941.7 8.7 fusion.55.dc_ref
  950.4 145.2 %shard_map.361 = (bf16[2048,400]{1,0:T(8,128)(2,1)}, f32[2048,400]{1,0:T(8,128)}, bf16[2048,100]{1,0:T(8,128)(2,1)}, f32[16,2,8,2048]{3,2,1,0:T(8,128)}, f32[100...) custom-call(s32[16]{0:T(128)} %select_reduce_fusion.1.slot, s32[16]{0:T(128)} %get-tuple-element.212.start, ...), custom_call_target="tpu_custom_call" | custom-call | flops 314572800 | bytes 19660800 | tf_op jit(solution)/shard_map/pallas_call | solution.py:389
  1100.6 9.5 convolution_convert_fusion.5
  1110.2 9.6 convolution_convert_fusion.6
  1119.9 9.3 fusion.5
  1134.8 38.2 %all_to_all.30 = bf16[8,688,200]{1,2,0:T(8,128)(2,1)S(1)} all-to-all(bf16[8,688,200]{1,2,0:T(8,128)(2,1)} %bitcast.178), channel_id=1, replica_groups=mesh['ctx'=8,'fsdp'=4] {'ctx'}, dimensions={0} | all-to-all | bytes 4403200 | tf_op jit(solution)/shard_map/all_to_all | solution.py:631
  1183.1 63.4 %shard_map.360 = (bf16[2048,256]{1,0:T(8,128)(2,1)}, f32[2,2048,64]{2,1,0:T(8,128)}, f32[2,2048,64]{2,1,0:T(8,128)}) custom-call(s32[16]{0:T(128)} %select_reduce_fusion.1.slot, s32[16]{0:T(128)} %and_select_fusion.1.low_block, s32[4]{0:T(128)} %subtract_clamp_fusion.pair, bf16[2048,256]{1,0:T(8,128)(2,1)} %slice.252.q_ref, ...), custom_call_target="tpu_custom_call" | custom-call | flops 5368709120 | bytes 6291456 | tf_op jit(solution)/shard_map/pallas_call | solution.py:577
  1249.0 16.3 %shard_map.362 = (bf16[2048,400]{1,0:T(8,128)(2,1)}, f32[8,400]{1,0:T(8,128)}) custom-call(s32[16]{0:T(128)} %select_reduce_fusion.1.slot, s32[16]{0:T(128)} %get-tuple-element.212.start, bf16[2048,132]{1,0:T(8,128)(2,1)} %all-reduce.9.cloned.1.call-done.dsel_ref, f32[2048,400]{1,0:T(8,128)} %get-tuple-element.55.part_ref, ...), custom_call_target="tpu_custom_call" | custom-call | flops 242483200 | bytes 9830400 | tf_op jit(solution)/shard_map/pallas_call | solution.py:148
  1270.4 10.2 concatenate.50
  1280.6 15.6 convolution_convert_fusion.1
  1296.2 15.6 convolution_convert_fusion.2
  1313.9 9.0 convolution_convert_fusion.7
  1328.4 34.2 %all_to_all.31 = bf16[8,656,200]{1,2,0:T(8,128)(2,1)S(1)} all-to-all(bf16[8,656,200]{1,2,0:T(8,128)(2,1)} %bitcast.179), channel_id=1, replica_groups=mesh['ctx'=8,'fsdp'=4] {'ctx'}, dimensions={0} | all-to-all | bytes 4198400 | tf_op jit(solution)/shard_map/all_to_all | solution.py:631
  1384.9 59.5 %reduce-scatter.25.cloned.1.call-done = bf16[400,1312]{1,0:T(8,128)(2,1)} async-done(((bf16[1600,1312]{1,0:T(8,128)(2,1)}), bf16[400,1312]{1,0:T(8,128)(2,1)}) %reduce-scatter.25.cloned.1.call-update) | async-done | bytes 1049616 | tf_op jit(solution)/shard_map/reduce_scatter | solution.py:618
  1472.2 63.6 %reduce-scatter.23.cloned.1.call-done = bf16[256,1600]{0,1:T(8,128)(2,1)} async-done(((bf16[2048,1600]{0,1:T(8,128)(2,1)}), bf16[256,1600]{0,1:T(8,128)(2,1)}) %reduce-scatter.23.cloned.1.call-update) | async-done | bytes 819216 | tf_op jit(solution)/shard_map/reduce_scatter | solution.py:610
  1559.5 38.7 %reduce-scatter.31.cloned.1.call-done = bf16[1200,200]{1,0:T(8,128)(2,1)} async-done(((bf16[4800,200]{1,0:T(8,128)(2,1)}), bf16[1200,200]{1,0:T(8,128)(2,1)}) %reduce-scatter.31.cloned.1.call-update) | async-done | bytes 480016
  (378 shorter events, 234.0 us)
Async XLA Ops:
  7.2 35.7 %all-gather.24.cloned.1.call-start = ((), (), s32[]{:S(2)}) async-start(), calls=%async_computation.17 | async-start | bytes 2580480 | tf_op jit(solution)/shard_map/all_gather | solution.py:741
  7.9 82.1 %all-gather.38.cloned.1.call-start = ((), (), s32[]{:S(2)}) async-start(), calls=%async_computation.34 | async-start | bytes 2560000 | tf_op jit(solution)/shard_map/all_gather | solution.py:614
  8.7 172.9 %all-gather.26.cloned.1.call-start = ((), (), s32[]{:S(2)}) async-start(), calls=%async_computation.18 | async-start | bytes 5632000 | tf_op jit(solution)/shard_map/all_gather | solution.py:614
  10.1 9.0 collective-permute-start.1
  10.6 8.4 collective-permute-start
  48.6 181.7 %all-gather.22.cloned.1.call-start = ((), (), s32[]{:S(2)}) async-start(), calls=%async_computation.16 | async-start | bytes 7372800 | tf_op jit(solution)/shard_map/all_gather | solution.py:606
  80.1 809.7 %copy-start.28 = (f32[1600]{0:T(1024)}, f32[1600]{0:T(1024)S(1)}, u32[]{:S(2)}) copy-start(f32[1600]{0:T(1024)S(1)} %get-tuple-element.162) | copy-start | bytes 19204
  82.9 391.3 %copy-start.2 = (f32[256,1600]{0,1:T(8,128)}, f32[256,1600]{0,1:T(8,128)S(1)}, u32[]{:S(2)}) copy-start(f32[256,1600]{0,1:T(8,128)S(1)} %get-tuple-element.178) | copy-start | bytes 4915204
  111.4 35.2 %all-to-all-start = ((bf16[8,656,200]{1,2,0:T(8,128)(2,1)}), bf16[8,656,200]{1,2,0:T(8,128)(2,1)}, u32[]{:S(2)}, u32[]{:S(2)}) async-start(bf16[8,656,200]{1,2,0:T(8,128)(2,1)} %pad_maximum_fusion), calls=%async_computation | async-start | bytes 4915200 | tf_op jit(solution)/shard_map/all_to_all | solution.py:624
  116.1 212.8 %all-reduce.7.cloned.1.call-start = ((), (), s32[]{:S(2)}) async-start(), calls=%async_computation.19 | async-start | bytes 2097152 | tf_op jit(solution)/shard_map/psum | solution.py:798
  147.9 159.5 %copy-start.11 = (bf16[256,8,200]{0,2,1:T(8,128)(2,1)}, bf16[256,8,200]{0,2,1:T(8,128)(2,1)S(1)}, u32[]{:S(2)}) copy-start(bf16[256,8,200]{0,2,1:T(8,128)(2,1)S(1)} %slice.266) | copy-start | bytes 2457604
  265.6 155.9 %reduce-scatter.15.cloned.1.call-start = ((), (), s32[]{:S(2)}) async-start(), calls=%async_computation.20 | async-start | bytes 7372800 | tf_op jit(solution)/shard_map/reduce_scatter | solution.py:610
  313.4 160.8 %reduce-scatter.17.cloned.1.call-start = ((), (), s32[]{:S(2)}) async-start(), calls=%async_computation.21 | async-start | bytes 7372800 | tf_op jit(solution)/shard_map/reduce_scatter | solution.py:610
  333.2 67.7 %copy-start.17 = (bf16[400,8,200]{0,2,1:T(8,128)(2,1)S(1)}, bf16[400,8,200]{0,2,1:T(8,128)(2,1)}, u32[]{:S(2)}) copy-start(bf16[400,8,200]{0,2,1:T(8,128)(2,1)} %slice.267) | copy-start | bytes 3840004
  408.1 116.4 %all-gather.40.cloned.1.call-start = ((), (), s32[]{:S(2)}) async-start(), calls=%async_computation.35 | async-start | bytes 2816000 | tf_op jit(solution)/shard_map/all_gather | solution.py:614
  408.8 168.2 %all-gather.32.cloned.1.call-start = ((), (), s32[]{:S(2)}) async-start(), calls=%async_computation.24 | async-start | bytes 3072000 | tf_op jit(solution)/shard_map/all_gather | solution.py:614
  409.6 216.4 %all-gather.28.cloned.1.call-start = ((), (), s32[]{:S(2)}) async-start(), calls=%async_computation.22 | async-start | bytes 7372800 | tf_op jit(solution)/shard_map/all_gather | solution.py:606
  476.0 413.7 %copy-start = (f32[256,1600]{0,1:T(8,128)}, f32[256,1600]{0,1:T(8,128)S(1)}, u32[]{:S(2)}) copy-start(f32[256,1600]{0,1:T(8,128)S(1)} %get-tuple-element.176) | copy-start | bytes 4915204
  476.1 413.7 %copy-start.35 = (f32[256]{0:T(256)}, f32[256]{0:T(256)S(1)}, u32[]{:S(2)}) copy-start(f32[256]{0:T(256)S(1)} %add_rsqrt_fusion) | copy-start | bytes 3076
  477.5 202.2 %all-gather.30.cloned.1.call-start = ((), (), s32[]{:S(2)}) async-start(), calls=%async_computation.23 | async-start | bytes 3072000 | tf_op jit(solution)/shard_map/all_gather | solution.py:614
  478.2 249.9 %all-gather.36.cloned.1.call-start = ((), (), s32[]{:S(2)}) async-start(), calls=%async_computation.33 | async-start | bytes 7372800 | tf_op jit(solution)/shard_map/all_gather | solution.py:606
  537.3 152.2 %all-to-all-start.1 = ((bf16[8,688,200]{1,2,0:T(8,128)(2,1)}), bf16[8,688,200]{1,2,0:T(8,128)(2,1)}, u32[]{:S(2)}, u32[]{:S(2)}) async-start(bf16[8,688,200]{1,2,0:T(8,128)(2,1)} %copy.326), calls=%async_computation.3 | async-start | bytes 4915200 | tf_op jit(solution)/shard_map/all_to_all | solution.py:624
  541.7 281.3 %reduce-scatter.21.cloned.1.call-start = ((), (), s32[]{:S(2)}) async-start(), calls=%async_computation.26 | async-start | bytes 7372800 | tf_op jit(solution)/shard_map/reduce_scatter | solution.py:610
  759.9 129.9 %reduce-scatter.19.cloned.1.call-start = ((), (), s32[]{:S(2)}) async-start(), calls=%async_computation.25 | async-start | bytes 7372800 | tf_op jit(solution)/shard_map/reduce_scatter | solution.py:610
  769.3 120.5 %copy-start.6 = (bf16[1,256,1600]{1,2,0:T(8,128)(2,1)S(1)}, bf16[1,256,1600]{1,2,0:T(8,128)(2,1)}, u32[]{:S(2)}) copy-start(bf16[1,256,1600]{1,2,0:T(8,128)(2,1)} %param.23) | copy-start | bytes 2457604
  769.3 172.3 %all-gather.34.cloned.1.call-start = ((), (), s32[]{:S(2)}) async-start(), calls=%async_computation.27 | async-start | bytes 7372800 | tf_op jit(solution)/shard_map/all_gather | solution.py:606
  823.1 66.7 %copy-start.7 = (bf16[256,1600]{0,1:T(8,128)(2,1)S(1)}, bf16[256,1600]{0,1:T(8,128)(2,1)}, u32[]{:S(2)}) copy-start(bf16[256,1600]{0,1:T(8,128)(2,1)} %reduce-scatter.21.cloned.1.call-done) | copy-start | bytes 2457604
  825.1 68.6 %copy-start.40 = (f32[256]{0:T(256)}, f32[256]{0:T(256)S(1)}, u32[]{:S(2)}) copy-start(f32[256]{0:T(256)S(1)} %broadcast_multiply_fusion.7) | copy-start | bytes 3076
  893.7 355.3 %all-reduce.9.cloned.1.call-start = ((), (), s32[]{:S(2)}) async-start(), calls=%async_computation.28 | async-start | bytes 2097152 | tf_op jit(solution)/shard_map/psum | solution.py:881
  1100.6 272.8 %reduce-scatter.29.cloned.1.call-start = ((), (), s32[]{:S(2)}) async-start(), calls=%async_computation.32 | async-start | bytes 3072000 | tf_op jit(solution)/shard_map/reduce_scatter | solution.py:618
  1110.1 265.4 %reduce-scatter.27.cloned.1.call-start = ((), (), s32[]{:S(2)}) async-start(), calls=%async_computation.31 | async-start | bytes 3072000 | tf_op jit(solution)/shard_map/reduce_scatter | solution.py:618
  1119.8 257.9 %reduce-scatter.33.cloned.1.call-start = ((), (), s32[]{:S(2)}) async-start(), calls=%async_computation.38 | async-start | bytes 3522560
  1175.8 204.9 %all-gather.42.cloned.1.call-start = ((), (), s32[]{:S(2)}) async-start(), calls=%async_computation.36 | async-start | bytes 2048000 | tf_op jit(solution)/shard_map/all_gather | solution.py:963
  1267.9 176.5 %reduce-scatter.25.cloned.1.call-start = ((), (), s32[]{:S(2)}) async-start(), calls=%async_computation.30 | async-start | bytes 5632000 | tf_op jit(solution)/shard_map/reduce_scatter | solution.py:618
  1296.2 239.7 %reduce-scatter.23.cloned.1.call-start = ((), (), s32[]{:S(2)}) async-start(), calls=%async_computation.29 | async-start | bytes 7372800 | tf_op jit(solution)/shard_map/reduce_scatter | solution.py:610
  1311.9 286.3 %reduce-scatter.31.cloned.1.call-start = ((), (), s32[]{:S(2)}) async-start(), calls=%async_computation.37 | async-start | bytes 3072000
  1450.1 150.5 %collective-permute-start.2 = (bf16[400,400]{1,0:T(8,128)(2,1)}, bf16[400,400]{1,0:T(8,128)(2,1)}, u32[]{:S(2)}, u32[]{:S(2)}) collective-permute-start(bf16[400,400]{1,0:T(8,128)(2,1)} %get-tuple-element.190), channel_id=1, source_target_pairs={{0,0},{8,4},{16,8},{24,12},{4,16},{12,20},{20,24},{28,28},{1,1},{9... | collective-permute-start | bytes 960008 | tf_op jit(solution)/shard_map/ppermute | solution.py:656
  1455.0 145.6 %collective-permute-start.3 = (bf16[400,400]{1,0:T(8,128)(2,1)}, bf16[400,400]{1,0:T(8,128)(2,1)}, u32[]{:S(2)}, u32[]{:S(2)}) collective-permute-start(bf16[400,400]{1,0:T(8,128)(2,1)} %get-tuple-element.191), channel_id=1, source_target_pairs={{4,0},{12,4},{20,8},{28,12},{0,16},{8,20},{16,24},{24,28},{5,1},{1... | collective-permute-start | bytes 960008 | tf_op jit(solution)/shard_map/ppermute | solution.py:657
  1467.3 68.5 %copy-start.3 = (f32[256,1600]{0,1:T(8,128)S(1)}, f32[256,1600]{0,1:T(8,128)}, u32[]{:S(2)}) copy-start(f32[256,1600]{0,1:T(8,128)} %copy-done.2) | copy-start | bytes 4915204
  1467.3 68.5 %copy-start.31 = (f32[1600]{0:T(1024)S(1)}, f32[1600]{0:T(1024)}, u32[]{:S(2)}) copy-start(f32[1600]{0:T(1024)} %copy-done.30) | copy-start | bytes 19204
  1467.3 68.5 %copy-start.39 = (f32[256]{0:T(256)S(1)}, f32[256]{0:T(256)}, u32[]{:S(2)}) copy-start(f32[256]{0:T(256)} %copy-done.38) | copy-start | bytes 3076
  1467.3 85.8 %all-to-all-start.3 = ((bf16[8,400,280]{1,2,0:T(8,128)(2,1)}), bf16[8,400,280]{1,2,0:T(8,128)(2,1)}, u32[]{:S(2)}, u32[]{:S(2)}) async-start(bf16[8,400,280]{1,2,0:T(8,128)(2,1)} %copy.339), calls=%async_computation.9 | async-start | bytes 4587520 | tf_op jit(solution)/shard_map/all_to_all | solution.py:925
  1472.1 65.7 %copy-start.1 = (f32[256,1600]{0,1:T(8,128)S(1)}, f32[256,1600]{0,1:T(8,128)}, u32[]{:S(2)}) copy-start(f32[256,1600]{0,1:T(8,128)} %copy-done) | copy-start | bytes 4915204
  1472.1 65.7 %copy-start.29 = (f32[1600]{0:T(1024)S(1)}, f32[1600]{0:T(1024)}, u32[]{:S(2)}) copy-start(f32[1600]{0:T(1024)} %copy-done.28) | copy-start | bytes 19204
  1472.2 65.7 %copy-start.36 = (f32[256]{0:T(256)S(1)}, f32[256]{0:T(256)}, u32[]{:S(2)}) copy-start(f32[256]{0:T(256)} %copy-done.35) | copy-start | bytes 3076
  1472.2 65.7 %copy-start.41 = (f32[256]{0:T(256)S(1)}, f32[256]{0:T(256)}, u32[]{:S(2)}) copy-start(f32[256]{0:T(256)} %copy-done.40) | copy-start | bytes 3076
  1472.2 65.7 %copy-start.43 = (pred[256]{0:T(512)(128)(4,1)S(1)}, pred[256]{0:T(512)(128)(4,1)}, u32[]{:S(2)}) copy-start(pred[256]{0:T(512)(128)(4,1)} %copy-done.42) | copy-start | bytes 772
  1553.1 52.8 %all-to-all-start.2 = ((bf16[32,35,200]{2,1,0:T(8,128)(2,1)}), bf16[32,35,200]{2,1,0:T(8,128)(2,1)S(1)}, u32[]{:S(2)}, u32[]{:S(2)}) async-start(bf16[32,35,200]{2,1,0:T(8,128)(2,1)} %copy.338), calls=%async_computation.7 | async-start | bytes 1310720 | tf_op jit(solution)/shard_map/all_to_all | solution.py:955
  (49 other events, 291.8 us)
Sparse Core Ops, SparseCore 0:
  9.9 32.9 all-gather.23
  44.5 45.5 all-gather.37
  92.2 89.3 all-gather.25
  183.9 46.3 all-gather.21
  265.7 56.7 all-reduce.6
  325.9 62.1 reduce-scatter.14
  408.2 65.9 reduce-scatter.16
  475.8 48.6 all-gather.39
  526.1 50.9 all-gather.31
  579.4 46.6 all-gather.27
  627.6 52.0 all-gather.29
  681.5 46.6 all-gather.35
  760.0 63.0 reduce-scatter.20
  826.8 62.9 reduce-scatter.18
  893.8 47.8 all-gather.33
  1100.7 60.0 all-reduce.8
  1163.0 49.5 reduce-scatter.28
  1214.8 49.1 reduce-scatter.26
  1266.3 54.7 reduce-scatter.32
  1323.1 37.9 all-gather.41
  1363.5 80.8 reduce-scatter.24
  1447.9 87.9 reduce-scatter.22
  1538.2 59.9 reduce-scatter.30

commit v2 on v1

v2 whole, which is shorter than its diff:
```python
import functools
import jax
import jax.numpy as jnp
from jax import lax
from jax.experimental import pallas as pl
from jax.experimental.pallas import tpu as pltpu
from jax.sharding import PartitionSpec as P

QUERY_HEADS = 25
KEY_VALUE_HEADS = 5
HEAD_SIZE = 64
INNER = 3200
STATE = 16
CONV = 4
DT_RANK = 100
EPS = 1e-06
LOG2E = 1.4426950408889634
LN2 = 0.6931471805599453
VMEM_LIMIT = 56 * 1024 * 1024
STEP_GROUP = 8
F32 = jnp.float32
BF16 = jnp.bfloat16


def sigmoid(value):
    return 0.5 * jnp.tanh(0.5 * value) + 0.5


def dot_nn(left, right):
    return lax.dot_general(left, right, (((1,), (0,)), ((), ())), preferred_element_type=F32)


def dot_nt(left, right):
    return lax.dot_general(left, right, (((1,), (1,)), ((), ())), preferred_element_type=F32)


def dot_tn(left, right):
    return lax.dot_general(left, right, (((0,), (0,)), ((), ())), preferred_element_type=F32)


def unit_spec(rows, width, reverse_units=None, which=0):
    if reverse_units is None:
        return pl.BlockSpec((rows, width), lambda u, *maps: (maps[which][u], 0))
    last = reverse_units - 1
    return pl.BlockSpec((rows, width), lambda i, *maps: (maps[which][last - i], 0))


def whole_spec(shape):
    zeros = (0,) * len(shape)
    return pl.BlockSpec(shape, lambda *_: zeros)


def params():
    return pltpu.CompilerParams(
        dimension_semantics=("arbitrary",), vmem_limit_bytes=VMEM_LIMIT
    )


def norm_unit(value, meta, gain, begins):
    value = jnp.where(begins == 1, meta, value.astype(F32))
    factor = lax.rsqrt(jnp.mean(value * value, axis=-1, keepdims=True) + EPS)
    return (value * factor * gain).astype(BF16)


def norm_pieces_kernel(begins, meta_ref, gain_ref, *refs):
    pieces, out_ref = refs[:-1], refs[-1]
    unit_rows = meta_ref.shape[0]
    unit = 0
    for piece in pieces:
        for i in range(piece.shape[0] // unit_rows):
            out_ref[unit * unit_rows : (unit + 1) * unit_rows, :] = norm_unit(
                piece[i * unit_rows : (i + 1) * unit_rows, :], meta_ref[...], gain_ref[...],
                begins[unit],
            )
            unit += 1


def norm_rows_kernel(begins, meta_ref, gain_ref, in_ref, out_ref):
    out_ref[...] = norm_unit(
        in_ref[...], meta_ref[...], gain_ref[...], begins[pl.program_id(0)]
    )


def norm_all(begins, meta, gain, pieces):
    unit_rows, width = meta.shape
    rows = sum(piece.shape[0] for piece in pieces)
    shape = jax.ShapeDtypeStruct((rows, width), BF16)
    if len(pieces) > 1:
        return pl.pallas_call(
            norm_pieces_kernel,
            out_shape=shape,
            in_specs=[pl.BlockSpec(memory_space=pltpu.SMEM)]
            + [pl.BlockSpec(memory_space=pltpu.VMEM)] * (2 + len(pieces)),
            out_specs=pl.BlockSpec(memory_space=pltpu.VMEM),
            compiler_params=pltpu.CompilerParams(vmem_limit_bytes=VMEM_LIMIT),
        )(begins, meta, gain, *pieces)
    by_unit = pl.BlockSpec((unit_rows, width), lambda u, *_: (u, 0))
    return pl.pallas_call(
        norm_rows_kernel,
        out_shape=shape,
        grid_spec=pltpu.PrefetchScalarGridSpec(
            num_scalar_prefetch=1,
            grid=(rows // unit_rows,),
            in_specs=[whole_spec((unit_rows, width)), whole_spec((1, width)), by_unit],
            out_specs=by_unit,
        ),
        compiler_params=params(),
    )(begins, meta, gain, pieces[0])


def conv_kernel_fwd(slot, fixed, start, xin_ref, w_ref, sel_ref, xc_ref, xs_ref, part_ref, ext):
    u = pl.program_id(0)
    rows = xin_ref.shape[0]
    keep = jnp.where(start[u] == 1, 0.0, 1.0)

    @pl.when(u == 0)
    def _():
        ext[...] = jnp.zeros_like(ext)

    ext[0:8, :] = ext[rows : rows + 8, :] * keep
    ext[8 : 8 + rows, :] = xin_ref[...].astype(F32)
    acc = w_ref[0:1, :] * ext[5 : 5 + rows, :]
    for k in range(1, CONV):
        acc = acc + w_ref[k : k + 1, :] * ext[5 + k : 5 + k + rows, :]
    xc_ref[...] = acc
    xs = (acc * sigmoid(acc)).astype(BF16)
    xs_ref[...] = xs
    part_ref[...] = dot_nt(xs, sel_ref[...]).astype(BF16)


def conv_forward(slot, fixed, start, xin, conv_w, sel_w, unit_rows):
    rows, width = xin.shape
    units = rows // unit_rows
    sel_rows = sel_w.shape[0]
    return pl.pallas_call(
        conv_kernel_fwd,
        out_shape=(
            jax.ShapeDtypeStruct((rows, width), F32),
            jax.ShapeDtypeStruct((rows, width), BF16),
            jax.ShapeDtypeStruct((rows, sel_rows), BF16),
        ),
        grid_spec=pltpu.PrefetchScalarGridSpec(
            num_scalar_prefetch=3,
            grid=(units,),
            in_specs=[
                unit_spec(unit_rows, width),
                whole_spec((CONV, width)),
                whole_spec((sel_rows, width)),
            ],
            out_specs=[
                unit_spec(unit_rows, width),
                unit_spec(unit_rows, width),
                unit_spec(unit_rows, sel_rows, None, 1),
            ],
            scratch_shapes=[pltpu.VMEM((unit_rows + 8, width), F32)],
        ),
        compiler_params=params(),
        cost_estimate=pl.CostEstimate(
            flops=2 * rows * width * (sel_rows + 8), bytes_accessed=rows * width * 8, transcendentals=rows * width
        ),
    )(slot, fixed, start, xin, conv_w, sel_w)


def conv_kernel_bwd(
    slot, fixed, start, dsel_ref, part_ref, xc_ref, xin_ref, xs_ref, w_ref, sel_ref,
    dxin_ref, gw_ref, gsel_ref, dext,
):
    i = pl.program_id(0)
    units = pl.num_programs(0)
    u = units - 1 - i
    rows = xin_ref.shape[0]
    after = jnp.where(start[jnp.minimum(u + 1, units - 1)] == 1, 0.0, 1.0)

    @pl.when(i == 0)
    def _():
        dext[...] = jnp.zeros_like(dext)
        gw_ref[...] = jnp.zeros_like(gw_ref)
        gsel_ref[...] = jnp.zeros_like(gsel_ref)

    gsel_ref[...] += dot_tn(dsel_ref[...], xs_ref[...])
    dext[rows : rows + 8, :] = dext[0:8, :] * after
    xc = xc_ref[...]
    sig = sigmoid(xc)
    dxs = dot_nn(dsel_ref[...], sel_ref[...]) + part_ref[...]
    dxc = dxs * (sig * (1.0 + xc * (1.0 - sig)))
    dext[0:rows, :] = dxc
    acc = w_ref[CONV - 1 : CONV, :] * dxc
    for k in range(CONV - 1):
        off = CONV - 1 - k
        acc = acc + w_ref[k : k + 1, :] * dext[off : off + rows, :]
    dxin_ref[...] = acc.astype(BF16)
    xin = xin_ref[...].astype(F32)
    for k in range(CONV):
        off = CONV - 1 - k
        gw_ref[k : k + 1, :] += jnp.sum(dext[off : off + rows, :] * xin, axis=0, keepdims=True)


def conv_backward(slot, fixed, start, dsel, part, xc, xin, xs, conv_w, sel_w, unit_rows):
    rows, width = xin.shape
    units = rows // unit_rows
    sel_rows = sel_w.shape[0]
    return pl.pallas_call(
        conv_kernel_bwd,
        out_shape=(
            jax.ShapeDtypeStruct((rows, width), BF16),
            jax.ShapeDtypeStruct((8, width), F32),
            jax.ShapeDtypeStruct((sel_rows, width), F32),
        ),
        grid_spec=pltpu.PrefetchScalarGridSpec(
            num_scalar_prefetch=3,
            grid=(units,),
            in_specs=[
                unit_spec(unit_rows, sel_rows, units, 1),
                unit_spec(unit_rows, width, units),
                unit_spec(unit_rows, width, units),
                unit_spec(unit_rows, width, units),
                unit_spec(unit_rows, width, units),
                whole_spec((CONV, width)),
                whole_spec((sel_rows, width)),
            ],
            out_specs=[
                unit_spec(unit_rows, width, units),
                whole_spec((8, width)),
                whole_spec((sel_rows, width)),
            ],
            scratch_shapes=[pltpu.VMEM((unit_rows + 8, width), F32)],
        ),
        compiler_params=params(),
        cost_estimate=pl.CostEstimate(
            flops=2 * rows * width * (sel_rows + 16), bytes_accessed=rows * width * 12, transcendentals=rows * width
        ),
    )(slot, fixed, start, dsel, part, xc, xin, xs, conv_w, sel_w)


def step_sizes(low_ref, step_ref, bias_ref):
    pre = dot_nn(low_ref[...], step_ref[...]) + bias_ref[...]
    return jnp.maximum(pre, 0.0) + jnp.log(1.0 + jnp.exp(-jnp.abs(pre)))


def lane_tiles(width):
    return [(lo, min(width, lo + 128)) for lo in range(0, width, 128)]


def fold_into(total, value, k):
    line = lax.broadcasted_iota(jnp.int32, (STEP_GROUP, 128), 0)
    return jnp.where(
        line == k, jnp.sum(value[0:8] + value[8:STATE], axis=0, keepdims=True), total
    )


def store_tiles(ref, value):
    for i, (lo, hi) in enumerate(lane_tiles(value.shape[1])):
        ref[i] = widen(value[:, lo:hi])


def load_tiles(ref, width):
    tiles = lane_tiles(width)
    return jnp.concatenate([ref[i, :, : hi - lo] for i, (lo, hi) in enumerate(tiles)], axis=1)


def widen(value):
    size = value.shape[1]
    if size == 128:
        return value
    return jnp.concatenate([value, jnp.zeros((value.shape[0], 128 - size), value.dtype)], axis=1)


def row_over_states(ref, i, t):
    return jnp.broadcast_to(ref[i, pl.ds(t, 1), :], (STATE, 128))


def scan_kernel_fwd(
    slot, fixed, start, xs_ref, z_ref, low_ref, bc_ref, step_ref, bias_ref, rate_ref, skip_ref,
    gain_ref, y_ref, comb_ref, square_ref, wide_ref, before_ref, last_ref, dt_buf, dtx_buf, y_buf,
    state,
):
    u = pl.program_id(0)
    rows = xs_ref.shape[0]
    width = xs_ref.shape[1]
    tiles = lane_tiles(width)
    count = len(tiles)
    keep = jnp.where(start[u] == 1, 0.0, 1.0)

    @pl.when(u == 0)
    def _():
        state[...] = jnp.zeros_like(state)

    xs = xs_ref[...].astype(F32)
    dt = step_sizes(low_ref, step_ref, bias_ref)
    store_tiles(dt_buf, dt)
    store_tiles(dtx_buf, dt * xs)
    rates = [widen(rate_ref[:, lo:hi]) for lo, hi in tiles]
    bc = bc_ref[0]
    for t in range(rows):
        wide_ref[0, t] = jnp.broadcast_to(bc[:, t : t + 1], (2 * STATE, 128))

    def group(g, carry):
        base = pl.multiple_of(g * STEP_GROUP, STEP_GROUP)
        h = list(carry)
        y = [jnp.zeros((STEP_GROUP, 128), F32) for _ in tiles]
        for k in range(STEP_GROUP):
            b = wide_ref[0, base + k, 0:STATE]
            c = wide_ref[0, base + k, STATE : 2 * STATE]
            for i in range(count):
                before_ref[0, base + k, i] = h[i]
                decay = jnp.exp2(row_over_states(dt_buf, i, base + k) * rates[i])
                h[i] = decay * h[i] + row_over_states(dtx_buf, i, base + k) * b
                y[i] = fold_into(y[i], c * h[i], k)
        for i in range(count):
            y_buf[i, pl.ds(base, STEP_GROUP), :] = y[i]
        return tuple(h)

    last = lax.fori_loop(
        0, rows // STEP_GROUP, group, tuple(state[i] * keep for i in range(count)), unroll=2
    )
    for i in range(count):
        state[i] = last[i]
        last_ref[0, i] = last[i]
    y = load_tiles(y_buf, width) + skip_ref[...] * xs
    y_ref[...] = y
    z = z_ref[...].astype(F32)
    ys = y * (z * sigmoid(z))
    comb_ref[...] = (ys * gain_ref[...]).astype(BF16)
    square_ref[...] = jnp.broadcast_to(jnp.sum(ys * ys, axis=1, keepdims=True), square_ref.shape)


def scan_forward(slot, fixed, start, xs, z, low, bc, step_w, bias, rate2, skip, gain, unit_rows):
    rows, width = xs.shape
    units = rows // unit_rows
    rank = low.shape[1]
    count = -(-width // 128)
    return pl.pallas_call(
        scan_kernel_fwd,
        out_shape=(
            jax.ShapeDtypeStruct((rows, width), F32),
            jax.ShapeDtypeStruct((rows, width), BF16),
            jax.ShapeDtypeStruct((rows, 128), F32),
            jax.ShapeDtypeStruct((units, unit_rows, 2 * STATE, 128), F32),
            jax.ShapeDtypeStruct((units, unit_rows, count, STATE, 128), F32),
            jax.ShapeDtypeStruct((units, count, STATE, 128), F32),
        ),
        grid_spec=pltpu.PrefetchScalarGridSpec(
            num_scalar_prefetch=3,
            grid=(units,),
            in_specs=[
                unit_spec(unit_rows, width),
                unit_spec(unit_rows, width),
                unit_spec(unit_rows, rank, None, 1),
                pl.BlockSpec(
                    (1, 2 * STATE, unit_rows), lambda u, slot, fixed, *_: (fixed[u], 0, 0)
                ),
                whole_spec((rank, width)),
                whole_spec((1, width)),
                whole_spec((STATE, width)),
                whole_spec((1, width)),
                whole_spec((1, width)),
            ],
            out_specs=[
                unit_spec(unit_rows, width),
                unit_spec(unit_rows, width),
                unit_spec(unit_rows, 128),
                pl.BlockSpec((1, unit_rows, 2 * STATE, 128), lambda u, *_: (u, 0, 0, 0)),
                pl.BlockSpec((1, unit_rows, count, STATE, 128), lambda u, *_: (u, 0, 0, 0, 0)),
                pl.BlockSpec((1, count, STATE, 128), lambda u, *_: (u, 0, 0, 0)),
            ],
            scratch_shapes=[
                pltpu.VMEM((count, unit_rows, 128), F32),
                pltpu.VMEM((count, unit_rows, 128), F32),
                pltpu.VMEM((count, unit_rows, 128), F32),
                pltpu.VMEM((count, STATE, 128), F32),
            ],
        ),
        compiler_params=params(),
        cost_estimate=pl.CostEstimate(
            flops=rows * width * STATE * 8, bytes_accessed=rows * width * 12,
            transcendentals=rows * width * STATE,
        ),
    )(slot, fixed, start, xs, z, low, bc, step_w, bias, rate2, skip, gain)


def scan_kernel_bwd(
    slot, fixed, start, dc_ref, stat_ref, y_ref, z_ref, xs_ref, low_ref, wide_ref, before_ref,
    last_ref, step_ref, bias_ref, rate_ref, skip_ref, gain_ref,
    dz_ref, part_ref, dlow_ref, dbc_ref, gstep_ref, gvec_ref, gdecay_ref,
    dt_buf, dtx_buf, dy_buf, gx_buf, ddt_buf, pb_buf, pc_buf, adj,
):
    i = pl.program_id(0)
    units = pl.num_programs(0)
    u = units - 1 - i
    rows = xs_ref.shape[0]
    width = xs_ref.shape[1]
    after = jnp.where(start[jnp.minimum(u + 1, units - 1)] == 1, 0.0, 1.0)

    @pl.when(i == 0)
    def _():
        adj[...] = jnp.zeros_like(adj)
        gstep_ref[...] = jnp.zeros_like(gstep_ref)
        gvec_ref[...] = jnp.zeros_like(gvec_ref)
        gdecay_ref[...] = jnp.zeros_like(gdecay_ref)

    xs = xs_ref[...].astype(F32)
    dt = step_sizes(low_ref, step_ref, bias_ref)
    store_tiles(dt_buf, dt)
    store_tiles(dtx_buf, dt * xs)
    tiles = lane_tiles(width)
    count = len(tiles)
    rates = [widen(rate_ref[:, lo:hi]) for lo, hi in tiles]

    factor = stat_ref[:, 0:1]
    shift = stat_ref[:, 1:2]
    z = z_ref[...].astype(F32)
    sig = sigmoid(z)
    gate = z * sig
    y = y_ref[...]
    ys = y * gate
    half = 0.5 * dc_ref[...]
    dys = factor * (half * gain_ref[...]) - ys * shift
    dy = dys * gate
    dz_ref[...] = (dys * y * (sig * (1.0 + z * (1.0 - sig)))).astype(BF16)
    store_tiles(dy_buf, dy)
    gvec_ref[0:1, :] += jnp.sum(half * ys * factor, axis=0, keepdims=True)
    gvec_ref[1:2, :] += jnp.sum(dy * xs, axis=0, keepdims=True)

    def group(index, carry):
        lams, accs, states = list(carry[0]), list(carry[1]), list(carry[2])
        g = rows // STEP_GROUP - 1 - index
        base = pl.multiple_of(g * STEP_GROUP, STEP_GROUP)
        gx = [jnp.zeros((STEP_GROUP, 128), F32) for _ in tiles]
        ddt = [jnp.zeros((STEP_GROUP, 128), F32) for _ in tiles]
        for k in range(STEP_GROUP - 1, -1, -1):
            t = base + k
            b = wide_ref[0, t, 0:STATE]
            c = wide_ref[0, t, STATE : 2 * STATE]
            pb = pc = None
            for i in range(count):
                dt_row = row_over_states(dt_buf, i, t)
                dy_row = row_over_states(dy_buf, i, t)
                lam = lams[i] + c * dy_row
                more_c = dy_row * states[i]
                more_b = row_over_states(dtx_buf, i, t) * lam
                pc = more_c if pc is None else pc + more_c
                pb = more_b if pb is None else pb + more_b
                gx[i] = fold_into(gx[i], b * lam, k)
                lams[i] = jnp.exp2(dt_row * rates[i]) * lam
                states[i] = before_ref[0, t, i]
                w = lams[i] * states[i]
                ddt[i] = fold_into(ddt[i], rates[i] * w, k)
                accs[i] = accs[i] + dt_row * w
            pb_buf[t] = pb
            pc_buf[t] = pc
        for i in range(count):
            gx_buf[i, pl.ds(base, STEP_GROUP), :] = gx[i]
            ddt_buf[i, pl.ds(base, STEP_GROUP), :] = ddt[i]
        return tuple(lams), tuple(accs), tuple(states)

    lams, accs, _ = lax.fori_loop(
        0,
        rows // STEP_GROUP,
        group,
        (
            tuple(adj[i] * after for i in range(count)),
            tuple(jnp.zeros((STATE, 128), F32) for _ in tiles),
            tuple(last_ref[0, i] for i in range(count)),
        ),
    )
    for i, (lo, hi) in enumerate(tiles):
        adj[i] = lams[i]
        gdecay_ref[:, lo:hi] += accs[i][:, : hi - lo]
    gx = load_tiles(gx_buf, width)
    part_ref[...] = gx * dt + skip_ref[...] * dy
    ddt = gx * xs + LN2 * load_tiles(ddt_buf, width)
    dpre = (ddt * (1.0 - jnp.exp(-dt))).astype(BF16)
    gstep_ref[...] += dot_tn(low_ref[...], dpre)
    gvec_ref[2:3, :] += jnp.sum(dpre.astype(F32), axis=0, keepdims=True)
    dlow_ref[...] = dot_nt(dpre, step_ref[...]).astype(BF16)
    ones = jnp.ones((8, 128), BF16)
    dbc_ref[0, 0] = dot_nt(ones, pb_buf[...].reshape(rows * STATE, 128).astype(BF16))
    dbc_ref[0, 1] = dot_nt(ones, pc_buf[...].reshape(rows * STATE, 128).astype(BF16))


def scan_backward(
    slot, fixed, start, dc, stat, y, z, xs, low, wide, before, final, step_w, bias, rate2, skip, gain, unit_rows
):
    rows, width = xs.shape
    units = rows // unit_rows
    rank = low.shape[1]
    count = -(-width // 128)
    last = units - 1
    return pl.pallas_call(
        scan_kernel_bwd,
        out_shape=(
            jax.ShapeDtypeStruct((rows, width), BF16),
            jax.ShapeDtypeStruct((rows, width), F32),
            jax.ShapeDtypeStruct((rows, rank), BF16),
            jax.ShapeDtypeStruct((units, 2, 8, unit_rows * STATE), F32),
            jax.ShapeDtypeStruct((rank, width), F32),
            jax.ShapeDtypeStruct((8, width), F32),
            jax.ShapeDtypeStruct((STATE, width), F32),
        ),
        grid_spec=pltpu.PrefetchScalarGridSpec(
            num_scalar_prefetch=3,
            grid=(units,),
            in_specs=[
                unit_spec(unit_rows, width, units),
                unit_spec(unit_rows, 128, units),
                unit_spec(unit_rows, width, units),
                unit_spec(unit_rows, width, units),
                unit_spec(unit_rows, width, units),
                unit_spec(unit_rows, rank, units, 1),
                pl.BlockSpec((1, unit_rows, 2 * STATE, 128), lambda i, *_: (last - i, 0, 0, 0)),
                pl.BlockSpec(
                    (1, unit_rows, count, STATE, 128), lambda i, *_: (last - i, 0, 0, 0, 0)
                ),
                pl.BlockSpec((1, count, STATE, 128), lambda i, *_: (last - i, 0, 0, 0)),
                whole_spec((rank, width)),
                whole_spec((1, width)),
                whole_spec((STATE, width)),
                whole_spec((1, width)),
                whole_spec((1, width)),
            ],
            out_specs=[
                unit_spec(unit_rows, width, units),
                unit_spec(unit_rows, width, units),
                unit_spec(unit_rows, rank, units, 1),
                pl.BlockSpec(
                    (1, 2, 8, unit_rows * STATE),
                    lambda i, slot, fixed, *_: (fixed[last - i], 0, 0, 0),
                ),
                whole_spec((rank, width)),
                whole_spec((8, width)),
                whole_spec((STATE, width)),
            ],
            scratch_shapes=[
                pltpu.VMEM((count, unit_rows, 128), F32),
                pltpu.VMEM((count, unit_rows, 128), F32),
                pltpu.VMEM((count, unit_rows, 128), F32),
                pltpu.VMEM((count, unit_rows, 128), F32),
                pltpu.VMEM((count, unit_rows, 128), F32),
                pltpu.VMEM((unit_rows, STATE, 128), F32),
                pltpu.VMEM((unit_rows, STATE, 128), F32),
                pltpu.VMEM((count, STATE, 128), F32),
            ],
        ),
        compiler_params=params(),
        cost_estimate=pl.CostEstimate(
            flops=rows * width * STATE * 24, bytes_accessed=rows * width * 24,
            transcendentals=rows * width * STATE,
        ),
    )(slot, fixed, start, dc, stat, y, z, xs, low, wide, before, final, step_w, bias, rate2, skip, gain)


PAIR_WIDTH = 2 * HEAD_SIZE


def stack_heads(value, pair):
    parts = []
    for h in range(value.shape[1] // HEAD_SIZE):
        part = value[:, h * HEAD_SIZE : (h + 1) * HEAD_SIZE]
        none = jnp.zeros_like(part)
        left = jnp.where(pair[h] == 0, part, none)
        right = jnp.where(pair[h] == 0, none, part)
        parts.append(jnp.concatenate([left, right], axis=1))
    return parts[0] if len(parts) == 1 else jnp.concatenate(parts, axis=0)


def unstack_heads(value, pair, rows):
    parts = []
    for h in range(value.shape[1] // rows):
        part = value[:, h * rows : (h + 1) * rows]
        parts.append(jnp.where(pair[h] == 0, part[:HEAD_SIZE], part[HEAD_SIZE:]))
    return jnp.transpose(parts[0] if len(parts) == 1 else jnp.concatenate(parts, axis=0))


def attn_kernel_fwd(
    slot, low_block, pair, q_ref, k_ref, vt_ref, gain_ref, o_ref, comb_ref, stat_ref
):
    u = pl.program_id(0)
    rows = q_ref.shape[0]
    heads = q_ref.shape[1] // HEAD_SIZE
    stacked = stack_heads(q_ref[...] * BF16(HEAD_SIZE**-0.5), pair)
    ones = jnp.ones((16, 2 * rows), BF16)

    def body(j, carry):
        top, acc = carry
        first = pl.multiple_of(slot[2 * j] * rows, rows)
        second = pl.multiple_of(slot[2 * j + 1] * rows, rows)
        kb = jnp.concatenate([k_ref[pl.ds(first, rows), :], k_ref[pl.ds(second, rows), :]], axis=0)
        vt = jnp.concatenate(
            [vt_ref[:, pl.ds(first, rows)], vt_ref[:, pl.ds(second, rows)]], axis=1
        )
        s = dot_nt(kb, stacked)
        new_top = jnp.maximum(top, jnp.max(s, axis=0, keepdims=True))
        p = jnp.exp(s - new_top).astype(BF16)
        acc = acc * jnp.exp(top - new_top) + dot_nn(jnp.concatenate([vt, ones], axis=0), p)
        return new_top, acc

    start = (
        jnp.full((1, heads * rows), -1e30, F32),
        jnp.zeros((PAIR_WIDTH + 16, heads * rows), F32),
    )
    top, acc = lax.fori_loop(low_block[u], u // 2 + 1, body, start)
    total = acc[PAIR_WIDTH : PAIR_WIDTH + 1]
    o = unstack_heads(acc[:PAIR_WIDTH] / total, pair, rows)
    o_ref[...] = o
    comb_ref[...] = (o * gain_ref[...]).astype(BF16)
    stat_ref[0, 0:1, :] = top + jnp.log(total)
    ones_row = jnp.ones((8, heads * HEAD_SIZE), F32)
    stat_ref[0, 1:2, 0:rows] = lax.dot_general(
        ones_row, o * o, (((1,), (1,)), ((), ())), precision=lax.Precision.HIGHEST,
        preferred_element_type=F32,
    )[0:1]


def attn_forward(slot, low_block, pair, q, k, vt, gain, unit_rows):
    rows, width = q.shape
    units = rows // unit_rows
    lanes = width // HEAD_SIZE * unit_rows
    return pl.pallas_call(
        attn_kernel_fwd,
        out_shape=(
            jax.ShapeDtypeStruct((rows, width), F32),
            jax.ShapeDtypeStruct((rows, width), BF16),
            jax.ShapeDtypeStruct((units, 8, lanes), F32),
        ),
        grid_spec=pltpu.PrefetchScalarGridSpec(
            num_scalar_prefetch=3,
            grid=(units,),
            in_specs=[
                unit_spec(unit_rows, width),
                whole_spec(k.shape),
                whole_spec(vt.shape),
                whole_spec((1, width)),
            ],
            out_specs=[
                unit_spec(unit_rows, width),
                unit_spec(unit_rows, width),
                pl.BlockSpec((1, 8, lanes), lambda u, slot, *_: (slot[u], 0, 0)),
            ],
        ),
        compiler_params=params(),
        cost_estimate=pl.CostEstimate(
            flops=2 * rows * rows * width, bytes_accessed=rows * width * 8,
            transcendentals=rows * rows * (width // HEAD_SIZE) // 2,
        ),
    )(slot, low_block, pair, q, k, vt, gain)


def attn_kernel_bwd(
    slot, low_block, pair, q_ref, o_ref, do_ref, stat_ref, k_ref, kt_ref, v_ref,
    dq_ref, dk_ref, dv_ref,
):
    u = pl.program_id(0)
    rows = q_ref.shape[0]
    heads = q_ref.shape[1] // HEAD_SIZE

    @pl.when(u == 0)
    def _():
        dk_ref[...] = jnp.zeros_like(dk_ref)
        dv_ref[...] = jnp.zeros_like(dv_ref)

    queries = stack_heads(q_ref[...] * BF16(HEAD_SIZE**-0.5), pair)
    do = do_ref[...]
    grads = stack_heads(do, pair)
    prod = do.astype(F32) * o_ref[...]
    prod = [prod[:, h * HEAD_SIZE : (h + 1) * HEAD_SIZE] for h in range(heads)]
    prod = prod[0] if heads == 1 else jnp.concatenate(prod, axis=0)
    delta = lax.dot_general(
        jnp.ones((8, HEAD_SIZE), F32), prod, (((1,), (1,)), ((), ())),
        precision=lax.Precision.HIGHEST, preferred_element_type=F32,
    )[0:1]
    log_total = stat_ref[0, 0:1, :]

    def body(j, dq):
        first = pl.multiple_of(slot[2 * j] * rows, rows)
        second = pl.multiple_of(slot[2 * j + 1] * rows, rows)
        kb = jnp.concatenate([k_ref[pl.ds(first, rows), :], k_ref[pl.ds(second, rows), :]], axis=0)
        vb = jnp.concatenate([v_ref[pl.ds(first, rows), :], v_ref[pl.ds(second, rows), :]], axis=0)
        kt = jnp.concatenate(
            [kt_ref[:, pl.ds(first, rows)], kt_ref[:, pl.ds(second, rows)]], axis=1
        )
        p = jnp.exp(dot_nt(kb, queries) - log_total)
        ds = (p * (dot_nt(vb, grads) - delta)).astype(BF16)
        dv = dot_nn(p.astype(BF16), grads)
        dk = dot_nn(ds, queries)
        dv_ref[pl.ds(first, rows), :] += dv[0:rows]
        dv_ref[pl.ds(second, rows), :] += dv[rows : 2 * rows]
        dk_ref[pl.ds(first, rows), :] += dk[0:rows]
        dk_ref[pl.ds(second, rows), :] += dk[rows : 2 * rows]
        return dq + dot_nn(kt, ds)

    dq = lax.fori_loop(
        low_block[u], u // 2 + 1, body, jnp.zeros((PAIR_WIDTH, heads * rows), F32)
    )
    dq_ref[...] = (unstack_heads(dq, pair, rows) * HEAD_SIZE**-0.5).astype(BF16)


def attn_backward(slot, low_block, pair, q, o, do, stat, k, kt, v, unit_rows):
    rows, width = q.shape
    units = rows // unit_rows
    lanes = width // HEAD_SIZE * unit_rows
    return pl.pallas_call(
        attn_kernel_bwd,
        out_shape=(
            jax.ShapeDtypeStruct((rows, width), BF16),
            jax.ShapeDtypeStruct(k.shape, F32),
            jax.ShapeDtypeStruct(v.shape, F32),
        ),
        grid_spec=pltpu.PrefetchScalarGridSpec(
            num_scalar_prefetch=3,
            grid=(units,),
            in_specs=[
                unit_spec(unit_rows, width),
                unit_spec(unit_rows, width),
                unit_spec(unit_rows, width),
                pl.BlockSpec((1, 8, lanes), lambda u, slot, *_: (slot[u], 0, 0)),
                whole_spec(k.shape),
                whole_spec(kt.shape),
                whole_spec(v.shape),
            ],
            out_specs=[unit_spec(unit_rows, width), whole_spec(k.shape), whole_spec(v.shape)],
        ),
        compiler_params=params(),
        cost_estimate=pl.CostEstimate(
            flops=5 * rows * rows * width, bytes_accessed=rows * width * 12,
            transcendentals=rows * rows * (width // HEAD_SIZE) // 2,
        ),
    )(slot, low_block, pair, q, o, do, stat, k, kt, v)


ORDER = (0, 2, 4, 6, 1, 3, 5, 7)
CUBE = len(ORDER)


def swap(value, mask):
    return lax.ppermute(value, "ctx", [(d, d ^ mask) for d in range(CUBE)])


def block_order(place, devices):
    if devices == CUBE:
        return place ^ jnp.array(ORDER, jnp.int32)
    return jnp.arange(devices, dtype=jnp.int32)


def block_index(owner, place, devices):
    if devices == CUBE:
        k = owner ^ place
        return k // 2 + (k % 2) * (CUBE // 2)
    return owner


def rows_gather(own, devices):
    pieces = gather_pieces(own, devices)
    return pieces[0] if len(pieces) == 1 else jnp.concatenate(pieces, axis=0)


def gather_pieces(own, devices):
    if devices != CUBE:
        return [lax.all_gather(own, "ctx", axis=0, tiled=True)]
    half = own.shape[0] // 2
    by_x, by_y, mate = swap(own, 2), swap(own, 4), swap(own, 1)
    far = jnp.concatenate([swap(by_x[:half], 4), swap(by_y[half:], 2)], axis=0)
    mates = [mate, swap(by_x, 1), swap(by_y, 1), swap(far, 1)]
    return [own, by_x, by_y, far] + mates


def rows_scatter(make, rows, devices):
    if devices != CUBE:
        return lax.psum_scatter(make(0, rows), "ctx", scatter_dimension=0, tiled=True).astype(F32)
    size = rows // CUBE
    half = size // 2
    from_mate = swap(make(rows // 2, rows), 1)
    total = make(0, rows // 2).astype(F32) + from_mate.astype(F32)
    cut = lambda i, a, b: total[i * size + a : i * size + b]
    far_x = swap(cut(3, 0, half).astype(BF16), 2)
    far_y = swap(cut(3, half, size).astype(BF16), 4)
    x_top = swap(cut(1, 0, half).astype(BF16), 2)
    y_end = swap(cut(2, half, size).astype(BF16), 4)
    x_end = swap((cut(1, half, size) + far_y.astype(F32)).astype(BF16), 2)
    y_top = swap((cut(2, 0, half) + far_x.astype(F32)).astype(BF16), 4)
    top = cut(0, 0, half) + x_top.astype(F32) + y_top.astype(F32)
    end = cut(0, half, size) + x_end.astype(F32) + y_end.astype(F32)
    return jnp.concatenate([top, end], axis=0)


def offload_gather(own, place, devices):
    got = lax.all_gather(own, "ctx", axis=0)
    if devices == CUBE:
        got = got[block_order(place, devices)]
    return got.reshape(-1, own.shape[1])


def offload_scatter(value, place, devices):
    blocks = value.reshape(devices, -1, value.shape[1])
    if devices == CUBE:
        blocks = blocks[block_index(jnp.arange(CUBE, dtype=jnp.int32), place, devices)]
    return lax.psum_scatter(blocks, "ctx", scatter_dimension=0, tiled=False).astype(F32)


def exchange(blocks):
    return lax.all_to_all(blocks, "ctx", split_axis=0, concat_axis=0, tiled=True)


def small_scatter(value, place, devices):
    if devices != CUBE:
        return lax.psum_scatter(value, "ctx", scatter_dimension=0, tiled=False)
    return sum(swap(value[i], k) if k else value[i] for i, k in enumerate(ORDER))


def small_gather(value, place, devices):
    if devices != CUBE:
        return lax.all_gather(value, "ctx", axis=0)
    return jnp.stack([swap(value, k) if k else value for k in ORDER])


def place_gather(value, place, devices):
    got = small_gather(value, place, devices)
    if devices != CUBE:
        return got
    return got[block_index(jnp.arange(CUBE, dtype=jnp.int32), place, devices)]


def all_sum(value, devices):
    if devices != CUBE:
        return lax.psum(value, "ctx")
    add = lambda a, b: (a.astype(F32) + b.astype(F32)).astype(BF16)
    value = add(value, swap(value, 1))
    half = value.shape[0] // 2
    top, end = value[:half], value[half:]
    top, end = add(top, swap(top, 2)), add(end, swap(end, 4))
    top, end = add(top, swap(top, 4)), add(end, swap(end, 2))
    return jnp.concatenate([top, end], axis=0)


def lane_gather(value):
    return lax.all_gather(value, "fsdp", axis=0, tiled=True)


def lane_scatter(value):
    return lax.psum_scatter(value, "fsdp", scatter_dimension=0, tiled=True)


def lane_shift(value, lanes, step):
    return lax.ppermute(value, "fsdp", [(z, (z + step) % lanes) for z in range(lanes)])


def lane_small_gather(value, lanes):
    lane = lax.axis_index("fsdp")
    got = jnp.stack([value] + [lane_shift(value, lanes, k) for k in range(1, lanes)])
    return got[(lane - jnp.arange(lanes, dtype=jnp.int32)) % lanes]


def lane_small_scatter(blocks, lanes):
    lane = lax.axis_index("fsdp")
    pick = lambda k: lax.dynamic_index_in_dim(blocks, (lane + k) % lanes, 0, False)
    return pick(0) + sum(lane_shift(pick(k), lanes, k) for k in range(1, lanes))


def after(value, *earlier):
    return lax.optimization_barrier((value,) + earlier)[0]


def columns_to_rows(value, devices):
    width = value.shape[1]
    got = exchange(value.reshape(devices, -1, width))
    return jnp.transpose(got, (1, 0, 2)).reshape(-1, devices * width)


def rows_to_columns(value, devices):
    rows = value.shape[0]
    blocks = jnp.transpose(value.reshape(rows, devices, -1), (1, 0, 2))
    return exchange(blocks).reshape(devices * rows, -1)


def pair_routes(devices):
    half = devices // 2
    first = [(d, 2 * d) for d in range(half)] + [(d, 2 * (d - half) + 1) for d in range(half, devices)]
    second = [(d, 2 * d + 1) for d in range(half)] + [(d, 2 * (d - half)) for d in range(half, devices)]
    return first, second


def split_pairs(value, place, devices):
    width = value.shape[1] // 2
    first, second = pair_routes(devices)
    low, high = value[:, :width], value[:, width:]
    early = place < devices // 2
    got_a = lax.ppermute(jnp.where(early, low, high), "ctx", first)
    got_b = lax.ppermute(jnp.where(early, high, low), "ctx", second)
    even = place % 2 == 0
    return jnp.where(even, got_a, got_b), jnp.where(even, got_b, got_a)


def join_pairs(left, right, place, devices):
    first, second = pair_routes(devices)
    even = place % 2 == 0
    got_a = lax.ppermute(jnp.where(even, left, right), "ctx", [(b, a) for a, b in first])
    got_b = lax.ppermute(jnp.where(even, right, left), "ctx", [(b, a) for a, b in second])
    early = place < devices // 2
    return jnp.concatenate([jnp.where(early, got_a, got_b), jnp.where(early, got_b, got_a)], axis=1)


def pad_to(value, size, axis):
    widths = [(0, 0)] * value.ndim
    widths[axis] = (0, size - value.shape[axis])
    return jnp.pad(value, widths)


def rms_factor(value):
    return lax.rsqrt(jnp.mean(value * value, axis=-1, keepdims=True) + EPS)


def norm_back(value, factor, gain, grad):
    weighted = grad * gain
    d_value = factor * weighted - value * factor * factor * factor * jnp.mean(
        value * weighted, axis=-1, keepdims=True
    )
    return d_value, jnp.sum(grad * value * factor, axis=0)


def shards(
    tokens, cotangent, unit_order, block_seq, meta_tokens, input_gain, query_key_value_weight, w_xz,
    conv_kernel, state_proj, step_proj, step_bias, decay_log, skip_gain, attn_gain, ssm_gain,
    out_proj, ffn_gain, w_gate, w_up, w_down,
):
    devices = lax.axis_size("ctx")
    lanes = lax.axis_size("fsdp")
    place = lax.axis_index("ctx")
    own_rows = tokens.shape[1]
    model = tokens.shape[2]
    unit_rows = own_rows // 2
    slot_unit = unit_order[0]
    units = slot_unit.shape[0]
    rows = units * unit_rows
    width = conv_kernel.shape[1]
    hidden_width = w_gate.shape[1]
    heads = -(-QUERY_HEADS // devices)
    head_width = heads * HEAD_SIZE
    group = QUERY_HEADS // KEY_VALUE_HEADS
    query_width = QUERY_HEADS * HEAD_SIZE
    kv_width = KEY_VALUE_HEADS * HEAD_SIZE
    model_part = input_gain.shape[0]

    slot_ids = jnp.arange(units, dtype=jnp.int32)
    fixed = jnp.sum(
        jnp.where(slot_unit[None, :] == slot_ids[:, None], slot_ids[None, :], 0), axis=1
    ).astype(jnp.int32)
    slot = (2 * block_index(fixed // 2, place, devices) + fixed % 2).astype(jnp.int32)
    unit_seq = jnp.repeat(block_seq[0], 2)
    starts = jnp.concatenate([jnp.ones((1,), jnp.bool_), unit_seq[1:] != unit_seq[:-1]])
    starts_int = starts.astype(jnp.int32)
    low_block = (jnp.sum(unit_seq[None, :] < unit_seq[:, None], axis=1) // 2).astype(jnp.int32)
    my_units = lax.dynamic_slice_in_dim(slot_unit, 2 * place, 2)
    my_start = jnp.any((my_units[:, None] == slot_ids[None, :]) & starts[None, :], axis=1)

    x_part, z_part = split_pairs(w_xz, place, devices)

    small = after(
        jnp.concatenate([conv_kernel, state_proj, step_proj, decay_log], axis=0), x_part
    )
    small_all = lane_small_gather(small, lanes)
    marks = [conv_kernel.shape[0], state_proj.shape[0], step_proj.shape[0], decay_log.shape[0]]
    ends = [sum(marks[: i + 1]) for i in range(4)]
    conv_w = small_all[:, : ends[0]].reshape(-1, width).astype(F32)
    sel_w = small_all[:, ends[0] : ends[1]].reshape(-1, width)
    step_w = small_all[:, ends[1] : ends[2]].reshape(-1, width)
    decay = small_all[:, ends[2] :].reshape(-1, width).astype(F32)
    rate = -jnp.exp(decay)
    rate2 = rate * LOG2E
    meta_part = lane_small_gather(after(meta_tokens, x_part), lanes).reshape(-1, model_part)
    meta_rows = meta_part.shape[0]
    wide = jnp.concatenate(
        [meta_part, input_gain[None], ffn_gain[None], attn_gain[None]], axis=0
    )
    wide = place_gather(wide, place, devices)
    wide = jnp.transpose(wide, (1, 0, 2)).reshape(-1, model).astype(F32)
    meta = wide[:meta_rows]
    gain_in = wide[meta_rows]
    gain_ffn = wide[meta_rows + 1]
    gain_attn = lax.dynamic_slice_in_dim(
        pad_to(wide[meta_rows + 2], devices * head_width, 0), place * head_width, head_width
    )[None]
    bias = step_bias.astype(F32)[None]
    skip = skip_gain.astype(F32)[None]
    gain_ssm = ssm_gain.astype(F32)[None]

    first_kv = (place * heads) // group
    qkv_row = place_gather(after(query_key_value_weight, x_part), place, devices)
    qkv_row = jnp.transpose(qkv_row, (1, 0, 2)).reshape(qkv_row.shape[1], -1)
    q_part = lax.dynamic_slice_in_dim(
        pad_to(qkv_row[:, :query_width], devices * head_width, 1), place * head_width, head_width, 1
    )
    kv_room = (devices * heads // group + 3) * HEAD_SIZE
    k_part = lax.dynamic_slice_in_dim(
        pad_to(qkv_row[:, query_width : query_width + kv_width], kv_room, 1),
        first_kv * HEAD_SIZE, 2 * HEAD_SIZE, 1,
    )
    v_part = lax.dynamic_slice_in_dim(
        pad_to(qkv_row[:, query_width + kv_width :], kv_room, 1),
        first_kv * HEAD_SIZE, 2 * HEAD_SIZE, 1,
    )
    pair = jnp.clip(
        (place * heads + jnp.arange(heads, dtype=jnp.int32)) // group - first_kv, 0, 1
    ).astype(jnp.int32)
    qkv_width = head_width + 4 * HEAD_SIZE
    x_w = lane_gather(x_part)
    qkvz_w = lane_gather(jnp.concatenate([q_part, k_part, v_part, z_part], axis=1))
    qkv_w = qkvz_w[:, :qkv_width]
    z_w = qkvz_w[:, qkv_width:]
    out_cols = lane_gather(after(out_proj, x_w))
    gate_up_w = lane_gather(jnp.concatenate([after(w_gate, qkvz_w), w_up], axis=1))
    gate_w = gate_up_w[:, :hidden_width]
    up_w = gate_up_w[:, hidden_width:]
    down_cols = lane_gather(after(w_down, out_cols))
    blocks = jnp.concatenate(
        [
            pad_to(out_cols[:query_width], devices * head_width, 0).reshape(
                devices, head_width, model_part
            ),
            out_cols[query_width:].reshape(devices, width, model_part),
        ],
        axis=1,
    )
    out_w = columns_to_rows(blocks.reshape(-1, model_part), devices)
    down_w = columns_to_rows(down_cols, devices)

    own_tok = tokens[0]
    slot_start = jnp.sum(
        jnp.where(slot[None, :] == slot_ids[:, None], starts_int[None, :], 0), axis=1
    ).astype(jnp.int32)
    normed = norm_all(slot_start, meta, gain_in[None], gather_pieces(own_tok, devices))
    resid = jnp.where(
        my_start[:, None, None], meta[None], own_tok.reshape(2, unit_rows, model).astype(F32)
    ).reshape(own_rows, model)
    in_factor = rms_factor(resid)

    x_in = dot_nn(normed, x_w).astype(BF16)
    cot = offload_gather(after(cotangent[0], gate_up_w), place, devices)
    conv_out, ssm_in, select = conv_forward(
        slot, fixed, starts_int, x_in, conv_w, sel_w, unit_rows
    )
    select = all_sum(select, devices).astype(F32)
    qkv = dot_nn(normed, qkv_w).astype(BF16)
    queries = qkv[:, :head_width]
    keys = qkv[:, head_width : head_width + PAIR_WIDTH]
    values = qkv[:, head_width + PAIR_WIDTH :]
    attn, attn_comb, attn_stat = attn_forward(
        slot, low_block, pair, queries, keys, jnp.transpose(values), gain_attn, unit_rows
    )
    attn_out = rows_scatter(
        lambda a, b: dot_nn(attn_comb[a:b], out_w[:head_width]).astype(BF16), rows, devices
    )
    z_gate = dot_nn(normed, z_w).astype(BF16)
    step_low = select[:, :DT_RANK].astype(BF16)
    bc = jnp.transpose(select[:, DT_RANK:].reshape(units, unit_rows, 2 * STATE), (0, 2, 1))
    y_total, ssm_comb, ssm_square, wide_bc, states, last_states = scan_forward(
        slot, fixed, starts_int, ssm_in, z_gate, step_low, bc, step_w, bias, rate2, skip, gain_ssm,
        unit_rows,
    )
    ssm_out = rows_scatter(
        lambda a, b: dot_nn(ssm_comb[a:b], out_w[head_width:]).astype(BF16), rows, devices
    )
    squares = jnp.stack(
        [
            attn_stat[:, 1, :unit_rows].reshape(devices, own_rows),
            ssm_square[:, 0].reshape(devices, own_rows),
        ],
        axis=1,
    )
    squares = small_scatter(squares, place, devices)
    own_factors = lax.rsqrt(squares / jnp.array([[query_width], [devices * width]], F32) + EPS)
    mid = (
        resid
        + 0.5 * own_factors[0][:, None] * attn_out
        + 0.5 * own_factors[1][:, None] * ssm_out
    )
    mid_factor = rms_factor(mid)
    ffn_in = rows_gather((mid * mid_factor * gain_ffn).astype(BF16), devices)

    gate = dot_nn(ffn_in, gate_w)
    up = dot_nn(ffn_in, up_w)
    sig = jax.nn.sigmoid(gate)
    act = gate * sig
    hidden = (act * up).astype(BF16)
    d_hidden = dot_nt(cot, down_w)
    d_gate = (d_hidden * up * (sig * (1.0 + gate * (1.0 - sig)))).astype(BF16)
    d_up = (d_hidden * act).astype(BF16)
    d_ffn = rows_scatter(
        lambda a, b: (dot_nt(d_gate[a:b], gate_w) + dot_nt(d_up[a:b], up_w)).astype(BF16),
        rows, devices,
    )
    ffn_out = offload_scatter(dot_nn(hidden, down_w).astype(BF16), place, devices)
    layer_out = (mid + ffn_out).astype(BF16)[None]
    down_part = dot_tn(hidden, cot).astype(BF16)
    gate_up_part = jnp.concatenate(
        [dot_tn(ffn_in, d_gate).astype(BF16), dot_tn(ffn_in, d_up).astype(BF16)], axis=1
    )
    down_grad = lane_scatter(rows_to_columns(down_part, devices)).astype(F32)
    gate_up_grad = lane_scatter(gate_up_part).astype(F32)
    gate_grad, up_grad = gate_up_grad[:, :hidden_width], gate_up_grad[:, hidden_width:]
    d_ffn = after(d_ffn, gate_up_part, down_part)

    d_mid_norm, ffn_gain_part = norm_back(mid, mid_factor, gain_ffn, d_ffn)
    d_mid = cotangent[0].astype(F32) + d_mid_norm
    d_branch_own = d_mid.astype(BF16)
    d_branch = rows_gather(d_branch_own, devices)
    branch_f = d_branch_own.astype(F32)
    dots = jnp.stack(
        [
            jnp.sum(branch_f * attn_out, axis=1) * (0.5 / query_width),
            jnp.sum(branch_f * ssm_out, axis=1) * (0.5 / (devices * width)),
        ]
    )
    shifts = dots * own_factors * own_factors * own_factors
    spread_rows = small_gather(jnp.concatenate([own_factors, shifts], axis=0), place, devices)
    spread_rows = jnp.transpose(spread_rows, (1, 0, 2)).reshape(4, rows)
    factors, shifts = spread_rows[:2], spread_rows[2:]

    d_comb_attn = dot_nt(d_branch, out_w[:head_width])
    d_comb_ssm = dot_nt(d_branch, out_w[head_width:])
    attn_mixed = (attn * (0.5 * factors[0][:, None] * gain_attn)).astype(BF16)
    ssm_mixed = (ssm_comb.astype(F32) * (0.5 * factors[1][:, None])).astype(BF16)
    out_part = dot_tn(jnp.concatenate([attn_mixed, ssm_mixed], axis=1), d_branch).astype(BF16)
    out_back = rows_to_columns(out_part, devices).reshape(devices, -1, model_part)
    out_grad = lane_scatter(
        jnp.concatenate(
            [
                out_back[:, :head_width].reshape(-1, model_part)[:query_width],
                out_back[:, head_width:].reshape(-1, model_part),
            ],
            axis=0,
        )
    ).astype(F32)
    half = 0.5 * d_comb_attn
    d_attn = factors[0][:, None] * (half * gain_attn) - attn * shifts[0][:, None]
    attn_gain_part = jnp.sum(half * attn * factors[0][:, None], axis=0)
    stat = jnp.transpose(pad_to(jnp.stack([factors[1], shifts[1]]), 128, 0))
    d_z, x_part_grad, d_low, d_bc, step_grad, vec_grads, decay_sum = scan_backward(
        slot, fixed, starts_int, d_comb_ssm, stat, y_total, z_gate, ssm_in, step_low, wide_bc, states,
        last_states, step_w, bias, rate2, skip, gain_ssm, unit_rows,
    )
    d_bc = jnp.transpose(
        d_bc[:, :, 0].reshape(units, 2, unit_rows, STATE), (0, 2, 1, 3)
    ).reshape(rows, 2 * STATE)
    d_select = all_sum(jnp.concatenate([d_low, d_bc.astype(BF16)], axis=1), devices)
    z_part_grad = dot_tn(normed, d_z).astype(BF16)
    d_query, d_keys, d_values = attn_backward(
        slot, low_block, pair, queries, attn, d_attn.astype(BF16), attn_stat, keys,
        jnp.transpose(keys), values, unit_rows,
    )
    d_qkv = jnp.concatenate([d_query, d_keys.astype(BF16), d_values.astype(BF16)], axis=1)
    qkv_part_grad = dot_tn(normed, d_qkv).astype(BF16)
    d_select = after(d_select, z_part_grad, qkv_part_grad)
    d_x, conv_grads, select_grad = conv_backward(
        slot, fixed, starts_int, d_select, x_part_grad, conv_out, x_in, ssm_in, conv_w, sel_w,
        unit_rows,
    )
    d_normed = rows_scatter(
        lambda a, b: (
            dot_nt(d_qkv[a:b], qkv_w) + dot_nt(d_x[a:b], x_w) + dot_nt(d_z[a:b], z_w)
        ).astype(BF16),
        rows, devices,
    )
    z_grad = lane_scatter(z_part_grad)
    in_grad = lane_scatter(qkv_part_grad)
    x_grad = lane_scatter(dot_tn(normed, d_x).astype(BF16))
    xz_grad = join_pairs(x_grad, z_grad, place, devices).astype(F32)
    spread = jnp.zeros((in_grad.shape[0], devices * head_width), BF16)
    spread = lax.dynamic_update_slice_in_dim(spread, in_grad[:, :head_width], place * head_width, 1)
    kv_zero = jnp.zeros((in_grad.shape[0], kv_room), BF16)
    qkv_full = jnp.concatenate(
        [
            spread[:, :query_width],
            lax.dynamic_update_slice_in_dim(
                kv_zero, in_grad[:, head_width : head_width + 2 * HEAD_SIZE],
                first_kv * HEAD_SIZE, 1,
            )[:, :kv_width],
            lax.dynamic_update_slice_in_dim(
                kv_zero, in_grad[:, head_width + 2 * HEAD_SIZE : qkv_width],
                first_kv * HEAD_SIZE, 1,
            )[:, :kv_width],
        ],
        axis=1,
    )
    part = query_key_value_weight.shape[1]
    qkv_blocks = jnp.transpose(qkv_full.reshape(-1, devices, part), (1, 0, 2))
    qkv_grad = lax.psum_scatter(
        qkv_blocks, "ctx", scatter_dimension=0, tiled=False
    ).astype(F32)

    d_norm_in, in_gain_part = norm_back(resid, in_factor, gain_in, d_normed)
    d_resid = d_mid + d_norm_in
    halves = [
        (my_start[i], d_resid[i * unit_rows : (i + 1) * unit_rows]) for i in range(2)
    ]
    tokens_grad = jnp.concatenate(
        [jnp.where(flag, 0.0, half).astype(BF16) for flag, half in halves], axis=0
    )[None]
    meta_sum = sum(jnp.where(flag, half, 0.0) for flag, half in halves)

    gain_rows = jnp.stack(
        [
            in_gain_part,
            ffn_gain_part,
            lax.dynamic_update_slice_in_dim(
                jnp.zeros((devices * head_width,), F32), attn_gain_part, place * head_width, 0
            )[:query_width],
        ]
    )
    by_lane = jnp.concatenate(
        [
            meta_sum.reshape(lanes, -1, model),
            jnp.broadcast_to(gain_rows[None], (lanes, 3, model)),
        ],
        axis=1,
    )
    count = by_lane.shape[1]
    packed = jnp.transpose(
        by_lane.reshape(lanes, count, devices, model_part), (0, 2, 1, 3)
    ).reshape(lanes * devices, count, model_part)
    totals = jnp.sum(
        lax.all_to_all(
            packed.astype(BF16), ("fsdp", "ctx"), split_axis=0, concat_axis=0, tiled=True
        ).astype(F32),
        axis=0,
    )
    counts = [CONV, select_grad.shape[0], DT_RANK, STATE]
    local = jnp.concatenate(
        [
            part.reshape(lanes, -1, width)
            for part in (conv_grads[:CONV], select_grad, step_grad, rate * decay_sum)
        ]
        + [jnp.broadcast_to(vec_grads[None, :3], (lanes, 3, width))],
        axis=1,
    )
    local = lane_small_scatter(local, lanes)
    ends = [sum(counts[:i]) // lanes for i in range(5)]
    piece = lambda i: local[ends[i] : ends[i + 1]]
    vec = lambda i: local[ends[4] + i]
    return (
        layer_out,
        tokens_grad,
        totals[: count - 3],
        totals[count - 3],
        qkv_grad,
        xz_grad,
        piece(0),
        piece(1),
        piece(2),
        vec(2),
        piece(3),
        vec(1),
        totals[count - 1],
        vec(0),
        out_grad,
        totals[count - 2],
        gate_grad,
        up_grad,
        down_grad,
    )


def solution(mesh):
    rows = P("fsdp", "ctx", None)
    index = P("fsdp", None)
    mat = P("fsdp", "ctx")
    vec = P("ctx")
    return jax.shard_map(
        shards,
        mesh=mesh,
        in_specs=(
            rows, rows, index, index, mat, vec, mat, mat, mat, mat, mat, vec, mat, vec, vec, vec,
            mat, vec, mat, mat, mat,
        ),
        out_specs=(
            rows, rows, mat, vec, mat, mat, mat, mat, mat, vec, mat, vec, vec, vec, mat, vec, mat,
            mat, mat,
        ),
        check_vma=False,
    )
```

time: 1630 us -> 1300 us (0.80)
  waiting for transfers between devices: 715 us -> 331 us
  local copies, waits for them, and re-layouts: 137 us -> 296 us
  blocking collectives: 133 us -> 0 us
  Pallas kernels: 347 us -> 232 us
  starting transfers between devices: 26.6 us -> 123 us
  matrix products: 182 us -> 215 us
  other arithmetic: 56.4 us -> 81.4 us
    ppermute x0 -> x99, waiting for transfers between devices: none -> 242 us  [the longest x90 218 us: swap(): return lax.ppermute(value, 'ctx', [(d, d ^ mask) for d in range(CUBE)])]
    reduce_scatter x5 -> x2, waiting for transfers between devices: 235 us -> 0.01 us  [the longest x1 0.01 us: offload_scatter(): lax.psum_scatter(blocks, 'ctx', scatter_dimension=0, tiled=False)]
    all_gather x6 -> x1, waiting for transfers between devices: 197 us -> 0.01 us  [offload_gather(): got = lax.all_gather(own, 'ctx', axis=0)]
    all_gather x5, waiting for transfers between devices: 166 us -> 34.9 us  [lane_gather(): return lax.all_gather(value, 'fsdp', axis=0, tiled=True)]
    ppermute x0 -> x99, starting transfers between devices: none -> 85 us  [the longest x90 73.8 us: swap(): return lax.ppermute(value, 'ctx', [(d, d ^ mask) for d in range(CUBE)])]
    all_to_all x2 -> x0, blocking collectives: 72.4 us -> none  [rows_to_columns(): got = lax.all_to_all(blocks, 'ctx', split_axis=0, concat_axis=0, tiled=True)]
    pallas_call x1, Pallas kernels: 145 us -> 74.9 us  [scan_backward(): pl.pallas_call(scan_kernel_bwd, out_shape=(jax.ShapeDtypeStruct((rows, wi...]
    all_gather x5 -> x0, blocking collectives: 60.8 us -> none  [the longest x1 18.8 us: shards(): small_all = lax.all_gather(small, 'fsdp', axis=0)]
  transfers between devices with their start and end apart: 31 -> 122, of which waited for: 18 -> 55; matrix products, arithmetic and copies ran while one was open for 18% -> 42% of each run, Pallas kernels for 12% -> 18%
where the time goes in v2:
time: 1300 us; the launch traced here: 1290 us
  waiting for transfers between devices  331 us (25%)
  local copies, waits for them, and re-layouts  296 us (23%)
  Pallas kernels  232 us (18%)
  matrix products  215 us (17%)
  starting transfers between devices  123 us (9%)
  other arithmetic  81.4 us (6%)
  between operations  16.6 us (1%)
    ppermute x90, waiting for transfers between devices, swap(): return lax.ppermute(value, 'ctx', [(d, d ^ mask) for d in range(CUBE)])  218 us
    dot_general x13, matrix products, dot_nt(): lax.dot_general(left, right, (((1,), (1,)), ((), ())), preferred_element_...  92.6 us
    unnamed x278, local copies, waits for them, and re-layouts  82.6 us
    pallas_call x1, Pallas kernels, scan_backward(): pl.pallas_call(scan_kernel_bwd, out_shape=(jax.ShapeDtypeStruct((rows, wi...  74.9 us
    ppermute x90, starting transfers between devices, swap(): return lax.ppermute(value, 'ctx', [(d, d ^ mask) for d in range(CUBE)])  73.8 us
    dot_general x10, matrix products, dot_nn(): lax.dot_general(left, right, (((1,), (0,)), ((), ())), preferred_element_...  70.2 us
    ppermute x24, local copies, waits for them, and re-layouts, swap(): return lax.ppermute(value, 'ctx', [(d, d ^ mask) for d in range(CUBE)])  58.4 us
    dot_general x7, matrix products, dot_tn(): lax.dot_general(left, right, (((0,), (0,)), ((), ())), preferred_element_...  51.7 us
  transfers between devices with their start and end apart: 122, of which 55 were waited for; matrix products, arithmetic and copies ran while one was open for 42% of the time, Pallas kernels for 18%

profile of v2, /device:TPU:0, one launch (start us, length us, event | category | flops | bytes accessed | tf_op | source)
XLA Modules:
  0.0 1294.8 jit_solution(3324392910131082453)
XLA Ops:
  10.6 6.9 collective-permute-done.1
  45.0 6.9 collective-permute-done.25
  78.5 9.3 collective-permute-done.28
  100.8 32.9 %all-gather.10.cloned.1.call-done = bf16[1600,912]{1,0:T(8,128)(2,1)} async-done(((bf16[400,912]{1,0:T(8,128)(2,1)}), bf16[1600,912]{1,0:T(8,128)(2,1)}) %all-gather.10.cloned.1.call-update) | async-done | bytes 2918416 | tf_op jit(solution)/shard_map/all_gather | solution.py:835
  139.7 8.7 collective-permute-done.14
  166.8 9.3 shard_map.366
  176.2 8.1 convolution_convert_fusion.12.xin_ref
  184.3 13.3 %shard_map.368 = (f32[2048,400]{1,0:T(8,128)}, bf16[2048,400]{1,0:T(8,128)(2,1)}, bf16[2048,132]{1,0:T(8,128)(2,1)}) custom-call(s32[16]{0:T(128)} %copy-done.71, s32[16]{0:T(128)} %copy-done.70, s32[16]{0:T(128)} %copy-done.68, bf16[2048,400]{1,0:T(8,128)(2,1)} %convolution_convert_fusion.12.xin_ref, f32[4,400]{1,0:T(4,128)} %fusion.61.w_ref, ...), custom_call_target="tpu_custom_call" | custom-call | flops 229376000 | bytes 6553600 | tf_op jit(solution)/shard_map/pallas_call | solution.py:135
  207.8 8.8 collective-permute-done.33
  222.6 9.6 collective-permute-done.32
  256.2 7.5 convolution_convert_fusion.13
  264.9 8.3 convolution_convert_fusion.11.z_ref
  273.2 45.9 %shard_map.369 = (f32[2048,400]{1,0:T(8,128)}, bf16[2048,400]{1,0:T(8,128)(2,1)}, f32[2048,128]{1,0:T(8,128)}, f32[16,128,32,128]{3,2,1,0:T(8,128)}, f32[16,128,...) custom-call(s32[16]{0:T(128)} %copy-done.71, s32[16]{0:T(128)} %copy-done.70, s32[16]{0:T(128)} %copy-done.68, ...), custom_call_target="tpu_custom_call" | custom-call | flops 104857600 | bytes 9830400 | tf_op jit(solution)/shard_map/pallas_call | solution.py:332
  327.6 33.9 %shard_map.367 = (f32[2048,256]{1,0:T(8,128)}, bf16[2048,256]{1,0:T(8,128)(2,1)}, f32[16,8,512]{2,1,0:T(8,128)}) custom-call(s32[16]{0:T(128)} %copy-done.71, s32[16]{0:T(128)} %and_select_fusion.1.low_block, s32[4]{0:T(128)} %subtract_clamp_fusion.pair, bf16[2048,256]{1,0:T(8,128)(2,1)} %slice.604.q_ref, bf16[2048,128]{1,0:T(8,128)(2,1)} %get-tuple-element.308.k_ref, ...), custom_call_target="tpu_custom_call" | custom-call | flops 2147483648 | bytes 4194304 | tf_op jit(solution)/shard_map/pallas_call | solution.py:618
  392.6 7.2 fusion.81
  415.2 7.8 collective-permute-done.51
  426.9 18.8 %collective-permute-done.44 = bf16[128,1600]{1,0:T(8,128)(2,1)S(1)} collective-permute-done((bf16[128,1600]{1,0:T(8,128)(2,1)S(1)}, bf16[128,1600]{1,0:T(8,128)(2,1)S(1)}, u32[]{:S(2)}, u32[]{:S(2)}) %collective-permute-start.44) | collective-permute-done | bytes 409632 | tf_op jit(solution)/shard_map/ppermute | solution.py:735
  450.2 8.3 collective-permute-done.52
  520.9 20.3 %collective-permute-done.58 = bf16[128,1600]{1,0:T(8,128)(2,1)} collective-permute-done((bf16[128,1600]{1,0:T(8,128)(2,1)}, bf16[128,1600]{1,0:T(8,128)(2,1)}, u32[]{:S(2)}, u32[]{:S(2)}) %collective-permute-start.58) | collective-permute-done | bytes 409632 | tf_op jit(solution)/shard_map/ppermute | solution.py:735
  564.2 10.9 fusion.6
  575.1 7.0 gather_fusion.5
  582.1 9.9 fusion.101
  592.0 15.0 %multiply_convert_fusion = (bf16[2048,688]{0,1:T(8,128)(2,1)S(1)}, bf16[2048,688]{0,1:T(8,128)(2,1)}, bf16[2048,688]{0,1:T(8,128)(2,1)}) fusion(f32[2048,688]{0,1:T(8,128)} %fusion.101, f32[2048,688]{0,1:T(8,128)} %fusion.6, bf16[2048,1600]{1,0:T(8,128)(2,1)} %constant_dynamic-update-slice_fusion.12, bf16[1600,1376]{1,0:T(8,128)(2,1)} %all-gather.14.cloned.1.call-done), kind=kOutput, calls=%fused_computation.16 | convolution fusion | flops 4530012160 | bytes 28999680 | tf_op jit(solution)/shard_map/dot_general | solution.py:30
  634.7 8.2 fusion.10
  642.9 9.4 convolution_convert_fusion.5
  652.3 10.6 all-to-all-done.4
  667.7 9.8 add_convert_fusion.1
  690.8 8.5 convolution_convert_fusion.6
  707.0 7.3 copy.765
  735.2 12.9 collective-permute-done.71
  793.2 36.6 %shard_map.370 = (bf16[2048,256]{1,0:T(8,128)(2,1)}, f32[2048,128]{1,0:T(8,128)}, f32[2048,128]{1,0:T(8,128)}) custom-call(s32[16]{0:T(128)} %copy-done.71, s32[16]{0:T(128)} %and_select_fusion.1.low_block, s32[4]{0:T(128)} %subtract_clamp_fusion.pair, bf16[2048,256]{1,0:T(8,128)(2,1)} %slice.604.q_ref, f32[2048,256]{1,0:T(8,128)} %get-tuple-element.67.o_ref, ...), custom_call_target="tpu_custom_call" | custom-call | flops 5368709120 | bytes 6291456 | tf_op jit(solution)/shard_map/pallas_call | solution.py:701
  839.2 9.4 fusion.102.dc_ref
  848.6 74.9 %shard_map.371 = (bf16[2048,400]{1,0:T(8,128)(2,1)}, f32[2048,400]{1,0:T(8,128)}, bf16[2048,100]{1,0:T(8,128)(2,1)}, f32[16,2,8,2048]{3,2,1,0:T(8,128)}, f32[100...) custom-call(s32[16]{0:T(128)} %copy-done.71, s32[16]{0:T(128)} %copy-done.70, s32[16]{0:T(128)} %copy-done.68, ...), custom_call_target="tpu_custom_call" | custom-call | flops 314572800 | bytes 19660800 | tf_op jit(solution)/shard_map/pallas_call | solution.py:489
  929.0 7.8 convolution_convert_fusion.14
  945.9 10.6 collective-permute-done.87
  960.3 10.7 collective-permute-done.90
  972.6 17.5 %shard_map.372 = (bf16[2048,400]{1,0:T(8,128)(2,1)}, f32[8,400]{1,0:T(8,128)}, f32[132,400]{1,0:T(8,128)}) custom-call(s32[16]{0:T(128)} %copy-done.71, s32[16]{0:T(128)} %copy-done.70, s32[16]{0:T(128)} %copy-done.68, bf16[2048,132]{1,0:T(8,128)(2,1)} %pad_maximum_fusion.10.dsel_ref, f32[2048,400]{1,0:T(8,128)} %get-tuple-element.79.part_ref, ...), custom_call_target="tpu_custom_call" | custom-call | flops 242483200 | bytes 9830400 | tf_op jit(solution)/shard_map/pallas_call | solution.py:202
  996.6 7.6 convolution_convert_fusion
  1014.0 9.7 copy.691
  1025.7 8.1 convolution_convert_fusion.8
  1058.8 25.4 %all-to-all-done.3 = bf16[8,656,200]{1,2,0:T(8,128)(2,1)S(1)} async-done(((bf16[8,656,200]{1,2,0:T(8,128)(2,1)}), bf16[8,656,200]{1,2,0:T(8,128)(2,1)S(1)}, u32[]{:S(2)}, u32[]{:S(2)}) %all-to-all-start.3) | async-done | bytes 2099232 | tf_op jit(solution)/shard_map/all_to_all | solution.py:800
  1096.1 9.5 add_convert_fusion.2
  1124.6 7.8 add_convert_fusion
  1132.4 7.3 collective-permute-done.102
  1209.8 13.6 %collective-permute-done.93 = bf16[128,1600]{1,0:T(8,128)(2,1)} collective-permute-done((bf16[128,1600]{1,0:T(8,128)(2,1)}, bf16[128,1600]{1,0:T(8,128)(2,1)}, u32[]{:S(2)}, u32[]{:S(2)}) %collective-permute-start.93) | collective-permute-done | bytes 409632 | tf_op jit(solution)/shard_map/ppermute | solution.py:735
  1236.1 9.8 collective-permute-done.94
  1255.8 13.0 %all-to-all-start.2 = ((bf16[32,35,200]{2,1,0:T(8,128)(2,1)}), bf16[32,35,200]{2,1,0:T(8,128)(2,1)S(1)}, u32[]{:S(2)}, u32[]{:S(2)}) async-start(bf16[32,35,200]{2,1,0:T(8,128)(2,1)} %copy.721), calls=%async_computation.3 | async-start | bytes 1310720 | tf_op jit(solution)/shard_map/all_to_all | solution.py:1220
  1275.7 11.0 all-to-all-done.2
  (789 shorter events, 606.3 us)
Async XLA Ops:
  7.2 55.1 %all-gather.12.cloned.1.call-start = ((), (), s32[]{:S(2)}) async-start(), calls=%async_computation.14 | async-start | bytes 2048000 | tf_op jit(solution)/shard_map/all_gather | solution.py:835
  18.4 115.4 %all-gather.10.cloned.1.call-start = ((), (), s32[]{:S(2)}) async-start(), calls=%async_computation.13 | async-start | bytes 4096000 | tf_op jit(solution)/shard_map/all_gather | solution.py:835
  60.2 175.2 %all-gather.18.cloned.1.call-start = ((), (), s32[]{:S(2)}) async-start(), calls=%async_computation.19 | async-start | bytes 2560000 | tf_op jit(solution)/shard_map/all_gather | solution.py:835
  62.3 309.5 %all-gather.14.cloned.1.call-start = ((), (), s32[]{:S(2)}) async-start(), calls=%async_computation.15 | async-start | bytes 5632000 | tf_op jit(solution)/shard_map/all_gather | solution.py:835
  62.3 34.9 %collective-permute-start.12 = (bf16[256,1600]{0,1:T(8,128)(2,1)}, bf16[256,1600]{0,1:T(8,128)(2,1)}, u32[]{:S(2)}, u32[]{:S(2)}) collective-permute-start(bf16[256,1600]{0,1:T(8,128)(2,1)} %bitcast.23), channel_id=1, source_target_pairs={{0,8},{4,12},{8,0},{12,4},{16,24},{20,28},{24,16},{28,20},{1,9},{5... | collective-permute-start | bytes 2457608 | tf_op jit(solution)/shard_map/ppermute | solution.py:735
  63.9 72.0 %collective-permute-start.13 = (bf16[256,1600]{0,1:T(8,128)(2,1)}, bf16[256,1600]{0,1:T(8,128)(2,1)}, u32[]{:S(2)}, u32[]{:S(2)}) collective-permute-start(bf16[256,1600]{0,1:T(8,128)(2,1)} %bitcast.23), channel_id=1, source_target_pairs={{0,16},{4,20},{8,24},{12,28},{16,0},{20,4},{24,8},{28,12},{1,17},{... | collective-permute-start | bytes 2457608 | tf_op jit(solution)/shard_map/ppermute | solution.py:735
  78.4 79.6 %collective-permute-start.16 = (bf16[256,1600]{0,1:T(8,128)(2,1)}, bf16[256,1600]{0,1:T(8,128)(2,1)}, u32[]{:S(2)}, u32[]{:S(2)}) collective-permute-start(bf16[256,1600]{0,1:T(8,128)(2,1)} %bitcast.23), channel_id=1, source_target_pairs={{0,4},{4,0},{8,12},{12,8},{16,20},{20,16},{24,28},{28,24},{1,5},{5... | collective-permute-start | bytes 2457608 | tf_op jit(solution)/shard_map/ppermute | solution.py:735
  93.7 41.5 %collective-permute-start.8 = (bf16[131,200]{1,0:T(8,128)(2,1)S(1)}, bf16[131,200]{1,0:T(8,128)(2,1)S(1)}, u32[]{:S(2)}, u32[]{:S(2)}) collective-permute-start(bf16[131,200]{1,0:T(8,128)(2,1)S(1)} %pad_maximum_fusion.16), channel_id=1, source_target_pairs={{0,4},{4,0},{8,12},{12,8},{16,20},{20,16},{24,28},{28,24},{1,5},{5... | collective-permute-start | bytes 157208 | tf_op jit(solution)/shard_map/ppermute | solution.py:735
  97.3 41.1 %collective-permute-start.9 = (bf16[131,200]{1,0:T(8,128)(2,1)S(1)}, bf16[131,200]{1,0:T(8,128)(2,1)S(1)}, u32[]{:S(2)}, u32[]{:S(2)}) collective-permute-start(bf16[131,200]{1,0:T(8,128)(2,1)S(1)} %pad_maximum_fusion.16), channel_id=1, source_target_pairs={{0,12},{4,8},{8,4},{12,0},{16,28},{20,24},{24,20},{28,16},{1,13},{... | collective-permute-start | bytes 157208 | tf_op jit(solution)/shard_map/ppermute | solution.py:735
  97.3 54.9 %collective-permute-start.10 = (bf16[131,200]{1,0:T(8,128)(2,1)S(1)}, bf16[131,200]{1,0:T(8,128)(2,1)S(1)}, u32[]{:S(2)}, u32[]{:S(2)}) collective-permute-start(bf16[131,200]{1,0:T(8,128)(2,1)S(1)} %pad_maximum_fusion.16), channel_id=1, source_target_pairs={{0,20},{4,16},{8,28},{12,24},{16,4},{20,0},{24,12},{28,8},{1,21},{... | collective-permute-start | bytes 157208 | tf_op jit(solution)/shard_map/ppermute | solution.py:735
  251.9 67.1 %all-to-all-start = ((bf16[8,656,200]{1,2,0:T(8,128)(2,1)}), bf16[8,656,200]{1,2,0:T(8,128)(2,1)S(1)}, u32[]{:S(2)}, u32[]{:S(2)}) async-start(bf16[8,656,200]{1,2,0:T(8,128)(2,1)} %pad_maximum_fusion.1), calls=%async_computation | async-start | bytes 4915200 | tf_op jit(solution)/shard_map/all_to_all | solution.py:800
  255.6 229.2 %all-gather.20.cloned.1.call-start = ((), (), s32[]{:S(2)}) async-start(), calls=%async_computation.20 | async-start | bytes 2816000 | tf_op jit(solution)/shard_map/all_gather | solution.py:835
  256.2 318.9 %all-gather.16.cloned.1.call-start = ((), (), s32[]{:S(2)}) async-start(), calls=%async_computation.18 | async-start | bytes 7667712 | tf_op jit(solution)/shard_map/all_gather | solution.py:786
  324.8 62.1 %collective-permute-start.49 = (bf16[1024,1600]{0,1:T(8,128)(2,1)}, bf16[1024,1600]{0,1:T(8,128)(2,1)}, u32[]{:S(2)}, u32[]{:S(2)}) collective-permute-start(bf16[1024,1600]{0,1:T(8,128)(2,1)} %convolution_convert_fusion.4), channel_id=1, source_target_pairs={{0,4},{4,0},{8,12},{12,8},{16,20},{20,16},{24,28},{28,24},{1,5},{5... | collective-permute-start | bytes 9830408 | tf_op jit(solution)/shard_map/ppermute | solution.py:735
  366.9 38.1 %collective-permute-start.42 = (bf16[1024,1600]{0,1:T(8,128)(2,1)}, bf16[1024,1600]{0,1:T(8,128)(2,1)}, u32[]{:S(2)}, u32[]{:S(2)}) collective-permute-start(bf16[1024,1600]{0,1:T(8,128)(2,1)} %convolution_convert_fusion.2), channel_id=1, source_target_pairs={{0,4},{4,0},{8,12},{12,8},{16,20},{20,16},{24,28},{28,24},{1,5},{5... | collective-permute-start | bytes 9830408 | tf_op jit(solution)/shard_map/ppermute | solution.py:735
  401.0 22.1 %collective-permute-start.51 = (bf16[128,1600]{1,0:T(8,128)(2,1)}, bf16[128,1600]{1,0:T(8,128)(2,1)}, u32[]{:S(2)}, u32[]{:S(2)}) collective-permute-start(bf16[128,1600]{1,0:T(8,128)(2,1)} %get-tuple-element.301), channel_id=1, source_target_pairs={{0,8},{4,12},{8,0},{12,4},{16,24},{20,28},{24,16},{28,20},{1,9},{5... | collective-permute-start | bytes 1228808 | tf_op jit(solution)/shard_map/ppermute | solution.py:735
  402.8 45.2 %collective-permute-start.50 = (bf16[128,1600]{1,0:T(8,128)(2,1)}, bf16[128,1600]{1,0:T(8,128)(2,1)}, u32[]{:S(2)}, u32[]{:S(2)}) collective-permute-start(bf16[128,1600]{1,0:T(8,128)(2,1)} %get-tuple-element.298), channel_id=1, source_target_pairs={{0,8},{4,12},{8,0},{12,4},{16,24},{20,28},{24,16},{28,20},{1,9},{5... | collective-permute-start | bytes 1228808 | tf_op jit(solution)/shard_map/ppermute | solution.py:735
  404.1 44.4 %collective-permute-start.55 = (bf16[128,1600]{1,0:T(8,128)(2,1)}, bf16[128,1600]{1,0:T(8,128)(2,1)}, u32[]{:S(2)}, u32[]{:S(2)}) collective-permute-start(bf16[128,1600]{1,0:T(8,128)(2,1)} %get-tuple-element.299), channel_id=1, source_target_pairs={{0,16},{4,20},{8,24},{12,28},{16,0},{20,4},{24,8},{28,12},{1,17},{... | collective-permute-start | bytes 1228808 | tf_op jit(solution)/shard_map/ppermute | solution.py:735
  413.5 32.2 %collective-permute-start.44 = (bf16[128,1600]{1,0:T(8,128)(2,1)S(1)}, bf16[128,1600]{1,0:T(8,128)(2,1)S(1)}, u32[]{:S(2)}, u32[]{:S(2)}) collective-permute-start(bf16[128,1600]{1,0:T(8,128)(2,1)S(1)} %get-tuple-element.297), channel_id=1, source_target_pairs={{0,8},{4,12},{8,0},{12,4},{16,24},{20,28},{24,16},{28,20},{1,9},{5... | collective-permute-start | bytes 1228808 | tf_op jit(solution)/shard_map/ppermute | solution.py:735
  423.1 24.4 %collective-permute-start.46 = (bf16[128,1600]{1,0:T(8,128)(2,1)S(1)}, bf16[128,1600]{1,0:T(8,128)(2,1)S(1)}, u32[]{:S(2)}, u32[]{:S(2)}) collective-permute-start(bf16[128,1600]{1,0:T(8,128)(2,1)S(1)} %get-tuple-element.296), channel_id=1, source_target_pairs={{0,16},{4,20},{8,24},{12,28},{16,0},{20,4},{24,8},{28,12},{1,17},{... | collective-permute-start | bytes 1228808 | tf_op jit(solution)/shard_map/ppermute | solution.py:735
  424.6 41.3 %collective-permute-start.43 = (bf16[128,1600]{1,0:T(8,128)(2,1)S(1)}, bf16[128,1600]{1,0:T(8,128)(2,1)S(1)}, u32[]{:S(2)}, u32[]{:S(2)}) collective-permute-start(bf16[128,1600]{1,0:T(8,128)(2,1)S(1)} %get-tuple-element.294), channel_id=1, source_target_pairs={{0,8},{4,12},{8,0},{12,4},{16,24},{20,28},{24,16},{28,20},{1,9},{5... | collective-permute-start | bytes 1228808 | tf_op jit(solution)/shard_map/ppermute | solution.py:735
  448.4 26.0 %collective-permute-start.45 = (bf16[128,1600]{1,0:T(8,128)(2,1)S(1)}, bf16[128,1600]{1,0:T(8,128)(2,1)S(1)}, u32[]{:S(2)}, u32[]{:S(2)}) collective-permute-start(bf16[128,1600]{1,0:T(8,128)(2,1)S(1)} %get-tuple-element.272), channel_id=1, source_target_pairs={{0,16},{4,20},{8,24},{12,28},{16,0},{20,4},{24,8},{28,12},{1,17},{... | collective-permute-start | bytes 1228808 | tf_op jit(solution)/shard_map/ppermute | solution.py:735
  483.1 25.4 %collective-permute-start.57 = (bf16[256,1600]{0,1:T(8,128)(2,1)}, bf16[256,1600]{0,1:T(8,128)(2,1)}, u32[]{:S(2)}, u32[]{:S(2)}) collective-permute-start(bf16[256,1600]{0,1:T(8,128)(2,1)} %copy.676), channel_id=1, source_target_pairs={{0,16},{4,20},{8,24},{12,28},{16,0},{20,4},{24,8},{28,12},{1,17},{... | collective-permute-start | bytes 2457608 | tf_op jit(solution)/shard_map/ppermute | solution.py:735
  484.8 29.6 %collective-permute-start.60 = (bf16[256,1600]{0,1:T(8,128)(2,1)}, bf16[256,1600]{0,1:T(8,128)(2,1)}, u32[]{:S(2)}, u32[]{:S(2)}) collective-permute-start(bf16[256,1600]{0,1:T(8,128)(2,1)} %copy.676), channel_id=1, source_target_pairs={{0,4},{4,0},{8,12},{12,8},{16,20},{20,16},{24,28},{28,24},{1,5},{5... | collective-permute-start | bytes 2457608 | tf_op jit(solution)/shard_map/ppermute | solution.py:735
  497.6 84.4 %all-to-all-start.1 = ((bf16[8,688,200]{1,2,0:T(8,128)(2,1)}), bf16[8,688,200]{1,2,0:T(8,128)(2,1)}, u32[]{:S(2)}, u32[]{:S(2)}) async-start(bf16[8,688,200]{1,2,0:T(8,128)(2,1)} %copy.689), calls=%async_computation.1 | async-start | bytes 4915200 | tf_op jit(solution)/shard_map/all_to_all | solution.py:800
  506.4 34.7 %collective-permute-start.58 = (bf16[128,1600]{1,0:T(8,128)(2,1)}, bf16[128,1600]{1,0:T(8,128)(2,1)}, u32[]{:S(2)}, u32[]{:S(2)}) collective-permute-start(bf16[128,1600]{1,0:T(8,128)(2,1)} %slice.648), channel_id=1, source_target_pairs={{0,16},{4,20},{8,24},{12,28},{16,0},{20,4},{24,8},{28,12},{1,17},{... | collective-permute-start | bytes 1228808 | tf_op jit(solution)/shard_map/ppermute | solution.py:735
  512.4 28.8 %collective-permute-start.59 = (bf16[128,1600]{1,0:T(8,128)(2,1)}, bf16[128,1600]{1,0:T(8,128)(2,1)}, u32[]{:S(2)}, u32[]{:S(2)}) collective-permute-start(bf16[128,1600]{1,0:T(8,128)(2,1)} %slice.649), channel_id=1, source_target_pairs={{0,8},{4,12},{8,0},{12,4},{16,24},{20,28},{24,16},{28,20},{1,9},{5... | collective-permute-start | bytes 1228808 | tf_op jit(solution)/shard_map/ppermute | solution.py:735
  513.9 37.3 %collective-permute-start.61 = (bf16[256,1600]{0,1:T(8,128)(2,1)}, bf16[256,1600]{0,1:T(8,128)(2,1)}, u32[]{:S(2)}, u32[]{:S(2)}) collective-permute-start(bf16[256,1600]{0,1:T(8,128)(2,1)} %collective-permute-done.56), channel_id=1, source_target_pairs={{0,4},{4,0},{8,12},{12,8},{16,20},{20,16},{24,28},{28,24},{1,5},{5... | collective-permute-start | bytes 2457608 | tf_op jit(solution)/shard_map/ppermute | solution.py:735
  513.9 39.5 %collective-permute-start.62 = (bf16[256,1600]{0,1:T(8,128)(2,1)}, bf16[256,1600]{0,1:T(8,128)(2,1)}, u32[]{:S(2)}, u32[]{:S(2)}) collective-permute-start(bf16[256,1600]{0,1:T(8,128)(2,1)} %collective-permute-done.57), channel_id=1, source_target_pairs={{0,4},{4,0},{8,12},{12,8},{16,20},{20,16},{24,28},{28,24},{1,5},{5... | collective-permute-start | bytes 2457608 | tf_op jit(solution)/shard_map/ppermute | solution.py:735
  616.5 61.0 %collective-permute-start.64 = (bf16[1024,1600]{0,1:T(8,128)(2,1)}, bf16[1024,1600]{0,1:T(8,128)(2,1)}, u32[]{:S(2)}, u32[]{:S(2)}) collective-permute-start(bf16[1024,1600]{0,1:T(8,128)(2,1)} %add_convert_fusion.3), channel_id=1, source_target_pairs={{0,4},{4,0},{8,12},{12,8},{16,20},{20,16},{24,28},{28,24},{1,5},{5... | collective-permute-start | bytes 9830408 | tf_op jit(solution)/shard_map/ppermute | solution.py:735
  628.0 34.9 %all-to-all-start.4 = ((bf16[8,688,200]{1,2,0:T(8,128)(2,1)}), bf16[8,688,200]{1,2,0:T(8,128)(2,1)}, u32[]{:S(2)}, u32[]{:S(2)}) async-start(bf16[8,688,200]{1,2,0:T(8,128)(2,1)} %bitcast.307), calls=%async_computation.6 | async-start | bytes 4915200 | tf_op jit(solution)/shard_map/all_to_all | solution.py:800
  632.4 485.0 %reduce-scatter.35.cloned.1.call-start = ((), (), s32[]{:S(2)}) async-start(), calls=%async_computation.26 | async-start | bytes 3522560
  667.4 481.3 %reduce-scatter.33.cloned.1.call-start = ((), (), s32[]{:S(2)}) async-start(), calls=%async_computation.25 | async-start | bytes 5632000
  714.4 445.8 %reduce-scatter.25.cloned.1.call-start = ((), (), s32[]{:S(2)}) async-start(), calls=%async_computation.21 | async-start | bytes 2048000 | tf_op jit(solution)/shard_map/reduce_scatter | solution.py:839
  728.8 30.8 %collective-permute-start.78 = (bf16[256,1600]{0,1:T(8,128)(2,1)S(1)}, bf16[256,1600]{0,1:T(8,128)(2,1)}, u32[]{:S(2)}, u32[]{:S(2)}) collective-permute-start(bf16[256,1600]{0,1:T(8,128)(2,1)S(1)} %copy.696), channel_id=1, source_target_pairs={{0,8},{4,12},{8,0},{12,4},{16,24},{20,28},{24,16},{28,20},{1,9},{5... | collective-permute-start | bytes 2457608 | tf_op jit(solution)/shard_map/ppermute | solution.py:735
  729.1 32.8 %collective-permute-start.79 = (bf16[256,1600]{0,1:T(8,128)(2,1)S(1)}, bf16[256,1600]{0,1:T(8,128)(2,1)}, u32[]{:S(2)}, u32[]{:S(2)}) collective-permute-start(bf16[256,1600]{0,1:T(8,128)(2,1)S(1)} %copy.696), channel_id=1, source_target_pairs={{0,16},{4,20},{8,24},{12,28},{16,0},{20,4},{24,8},{28,12},{1,17},{... | collective-permute-start | bytes 2457608 | tf_op jit(solution)/shard_map/ppermute | solution.py:735
  729.4 36.1 %collective-permute-start.82 = (bf16[256,1600]{0,1:T(8,128)(2,1)S(1)}, bf16[256,1600]{0,1:T(8,128)(2,1)}, u32[]{:S(2)}, u32[]{:S(2)}) collective-permute-start(bf16[256,1600]{0,1:T(8,128)(2,1)S(1)} %copy.696), channel_id=1, source_target_pairs={{0,4},{4,0},{8,12},{12,8},{16,20},{20,16},{24,28},{28,24},{1,5},{5... | collective-permute-start | bytes 2457608 | tf_op jit(solution)/shard_map/ppermute | solution.py:735
  837.5 348.2 %reduce-scatter.29.cloned.1.call-start = ((), (), s32[]{:S(2)}) async-start(), calls=%async_computation.23 | async-start | bytes 2048000 | tf_op jit(solution)/shard_map/reduce_scatter | solution.py:839
  940.3 245.5 %reduce-scatter.27.cloned.1.call-start = ((), (), s32[]{:S(2)}) async-start(), calls=%async_computation.22 | async-start | bytes 2048000 | tf_op jit(solution)/shard_map/reduce_scatter | solution.py:839
  996.6 208.7 %reduce-scatter.21.cloned.1.call-start = ((), (), s32[]{:S(2)}) async-start(), calls=%async_computation.16 | async-start | bytes 7667712 | tf_op jit(solution)/shard_map/reduce_scatter | solution.py:796
  1039.4 44.8 %all-to-all-start.3 = ((bf16[8,656,200]{1,2,0:T(8,128)(2,1)}), bf16[8,656,200]{1,2,0:T(8,128)(2,1)S(1)}, u32[]{:S(2)}, u32[]{:S(2)}) async-start(bf16[8,656,200]{1,2,0:T(8,128)(2,1)} %bitcast.306), calls=%async_computation.5 | async-start | bytes 4915200 | tf_op jit(solution)/shard_map/all_to_all | solution.py:800
  1043.3 228.2 %reduce-scatter.31.cloned.1.call-start = ((), (), s32[]{:S(2)}) async-start(), calls=%async_computation.24 | async-start | bytes 3072000
  1094.7 179.1 %reduce-scatter.23.cloned.1.call-start = ((), (), s32[]{:S(2)}) async-start(), calls=%async_computation.17 | async-start | bytes 2580480 | tf_op jit(solution)/shard_map/reduce_scatter | solution.py:1185
  1105.6 87.3 %collective-permute-start.91 = (bf16[1024,1600]{0,1:T(8,128)(2,1)}, bf16[1024,1600]{0,1:T(8,128)(2,1)}, u32[]{:S(2)}, u32[]{:S(2)}) collective-permute-start(bf16[1024,1600]{0,1:T(8,128)(2,1)} %add_convert_fusion.2), channel_id=1, source_target_pairs={{0,4},{4,0},{8,12},{12,8},{16,20},{20,16},{24,28},{28,24},{1,5},{5... | collective-permute-start | bytes 9830408 | tf_op jit(solution)/shard_map/ppermute | solution.py:735
  1187.8 41.4 %collective-permute-start.98 = (bf16[400,400]{1,0:T(8,128)(2,1)}, bf16[400,400]{1,0:T(8,128)(2,1)}, u32[]{:S(2)}, u32[]{:S(2)}) collective-permute-start(bf16[400,400]{1,0:T(8,128)(2,1)} %get-tuple-element.323), channel_id=1, source_target_pairs={{0,0},{8,4},{16,8},{24,12},{4,16},{12,20},{20,24},{28,28},{1,1},{9... | collective-permute-start | bytes 960008 | tf_op jit(solution)/shard_map/ppermute | solution.py:895
  1192.7 36.5 %collective-permute-start.99 = (bf16[400,400]{1,0:T(8,128)(2,1)}, bf16[400,400]{1,0:T(8,128)(2,1)}, u32[]{:S(2)}, u32[]{:S(2)}) collective-permute-start(bf16[400,400]{1,0:T(8,128)(2,1)} %get-tuple-element.324), channel_id=1, source_target_pairs={{4,0},{12,4},{20,8},{28,12},{0,16},{8,20},{16,24},{24,28},{5,1},{1... | collective-permute-start | bytes 960008 | tf_op jit(solution)/shard_map/ppermute | solution.py:896
  1208.5 26.2 %collective-permute-start.92 = (bf16[128,1600]{1,0:T(8,128)(2,1)S(1)}, bf16[128,1600]{1,0:T(8,128)(2,1)S(1)}, u32[]{:S(2)}, u32[]{:S(2)}) collective-permute-start(bf16[128,1600]{1,0:T(8,128)(2,1)S(1)} %get-tuple-element.286), channel_id=1, source_target_pairs={{0,8},{4,12},{8,0},{12,4},{16,24},{20,28},{24,16},{28,20},{1,9},{5... | collective-permute-start | bytes 1228808 | tf_op jit(solution)/shard_map/ppermute | solution.py:735
  1255.8 30.9 %all-to-all-start.2 = ((bf16[32,35,200]{2,1,0:T(8,128)(2,1)}), bf16[32,35,200]{2,1,0:T(8,128)(2,1)S(1)}, u32[]{:S(2)}, u32[]{:S(2)}) async-start(bf16[32,35,200]{2,1,0:T(8,128)(2,1)} %copy.721), calls=%async_computation.3 | async-start | bytes 1310720 | tf_op jit(solution)/shard_map/all_to_all | solution.py:1220
  (182 other events, 2931.1 us)
Sparse Core Ops, SparseCore 0:
  18.5 43.7 all-gather.11
  64.4 69.3 all-gather.9
  135.4 43.8 all-gather.17
  181.2 84.6 all-gather.13
  267.3 47.2 all-gather.19
  372.0 61.7 all-gather.15
  667.5 54.1 reduce-scatter.34
  724.2 81.7 reduce-scatter.32
  837.6 37.4 reduce-scatter.24
  940.4 37.3 reduce-scatter.28
  996.7 37.1 reduce-scatter.26
  1037.5 73.0 reduce-scatter.20
  1113.0 58.9 reduce-scatter.30
  1185.8 57.9 reduce-scatter.22

commit v3 on v2

--- a/solution.py
+++ b/solution.py
@@ -3,6 +3,7 @@
 import jax.numpy as jnp
 from jax import lax
 from jax.experimental import pallas as pl
+from jax.experimental.layout import Layout, with_layout_constraint
 from jax.experimental.pallas import tpu as pltpu
 from jax.sharding import PartitionSpec as P
 
@@ -18,6 +19,7 @@
 LN2 = 0.6931471805599453
 VMEM_LIMIT = 56 * 1024 * 1024
 STEP_GROUP = 8
+SMALL_COST = pl.CostEstimate(flops=1, bytes_accessed=1, transcendentals=0)
 F32 = jnp.float32
 BF16 = jnp.bfloat16
 
@@ -48,6 +50,32 @@
 def whole_spec(shape):
     zeros = (0,) * len(shape)
     return pl.BlockSpec(shape, lambda *_: zeros)
+
+
+def later(kernel, before, deps):
+    if not deps:
+        return kernel
+    count = len(deps)
+    return lambda *refs: kernel(*refs[:before], *refs[before + count :])
+
+
+def wait_specs(deps):
+    return [pl.BlockSpec(memory_space=pl.ANY)] * len(deps)
+
+
+def hold_kernel(in_ref, out_ref):
+    out_ref[...] = in_ref[...]
+
+
+def hold(value, *deps):
+    return pl.pallas_call(
+        later(hold_kernel, 1, deps),
+        out_shape=jax.ShapeDtypeStruct(value.shape, value.dtype),
+        in_specs=[pl.BlockSpec(memory_space=pltpu.VMEM)] + wait_specs(deps),
+        out_specs=pl.BlockSpec(memory_space=pltpu.VMEM),
+        compiler_params=pltpu.CompilerParams(vmem_limit_bytes=VMEM_LIMIT),
+        cost_estimate=SMALL_COST,
+    )(value, *deps)
 
 
 def params():
@@ -69,15 +97,15 @@
     for piece in pieces:
         for i in range(piece.shape[0] // unit_rows):
             out_ref[unit * unit_rows : (unit + 1) * unit_rows, :] = norm_unit(
-                piece[i * unit_rows : (i + 1) * unit_rows, :], meta_ref[...], gain_ref[...],
-                begins[unit],
+                piece[i * unit_rows : (i + 1) * unit_rows, : meta_ref.shape[1]], meta_ref[...],
+                gain_ref[...], begins[unit],
             )
             unit += 1
 
 
 def norm_rows_kernel(begins, meta_ref, gain_ref, in_ref, out_ref):
     out_ref[...] = norm_unit(
-        in_ref[...], meta_ref[...], gain_ref[...], begins[pl.program_id(0)]
+        in_ref[:, : meta_ref.shape[1]], meta_ref[...], gain_ref[...], begins[pl.program_id(0)]
     )
 
 
@@ -94,15 +122,15 @@
             out_specs=pl.BlockSpec(memory_space=pltpu.VMEM),
             compiler_params=pltpu.CompilerParams(vmem_limit_bytes=VMEM_LIMIT),
         )(begins, meta, gain, *pieces)
-    by_unit = pl.BlockSpec((unit_rows, width), lambda u, *_: (u, 0))
+    by_unit = lambda size: pl.BlockSpec((unit_rows, size), lambda u, *_: (u, 0))
     return pl.pallas_call(
         norm_rows_kernel,
         out_shape=shape,
         grid_spec=pltpu.PrefetchScalarGridSpec(
             num_scalar_prefetch=1,
             grid=(rows // unit_rows,),
-            in_specs=[whole_spec((unit_rows, width)), whole_spec((1, width)), by_unit],
-            out_specs=by_unit,
+            in_specs=[whole_spec((unit_rows, width)), whole_spec((1, width)), by_unit(pieces[0].shape[1])],
+            out_specs=by_unit(width),
         ),
         compiler_params=params(),
     )(begins, meta, gain, pieces[0])
@@ -155,9 +183,7 @@
             scratch_shapes=[pltpu.VMEM((unit_rows + 8, width), F32)],
         ),
         compiler_params=params(),
-        cost_estimate=pl.CostEstimate(
-            flops=2 * rows * width * (sel_rows + 8), bytes_accessed=rows * width * 8, transcendentals=rows * width
-        ),
+        cost_estimate=SMALL_COST,
     )(slot, fixed, start, xin, conv_w, sel_w)
 
 
@@ -195,12 +221,12 @@
         gw_ref[k : k + 1, :] += jnp.sum(dext[off : off + rows, :] * xin, axis=0, keepdims=True)
 
 
-def conv_backward(slot, fixed, start, dsel, part, xc, xin, xs, conv_w, sel_w, unit_rows):
+def conv_backward(slot, fixed, start, dsel, part, xc, xin, xs, conv_w, sel_w, unit_rows, deps=()):
     rows, width = xin.shape
     units = rows // unit_rows
     sel_rows = sel_w.shape[0]
     return pl.pallas_call(
-        conv_kernel_bwd,
+later(        conv_kernel_bwd, 10, deps),
         out_shape=(
             jax.ShapeDtypeStruct((rows, width), BF16),
             jax.ShapeDtypeStruct((8, width), F32),
@@ -217,7 +243,7 @@
                 unit_spec(unit_rows, width, units),
                 whole_spec((CONV, width)),
                 whole_spec((sel_rows, width)),
-            ],
+            ] + wait_specs(deps),
             out_specs=[
                 unit_spec(unit_rows, width, units),
                 whole_spec((8, width)),
@@ -226,10 +252,8 @@
             scratch_shapes=[pltpu.VMEM((unit_rows + 8, width), F32)],
         ),
         compiler_params=params(),
-        cost_estimate=pl.CostEstimate(
-            flops=2 * rows * width * (sel_rows + 16), bytes_accessed=rows * width * 12, transcendentals=rows * width
-        ),
-    )(slot, fixed, start, dsel, part, xc, xin, xs, conv_w, sel_w)
+        cost_estimate=SMALL_COST,
+    )(slot, fixed, start, dsel, part, xc, xin, xs, conv_w, sel_w, *deps)
 
 
 def step_sizes(low_ref, step_ref, bias_ref):
@@ -324,13 +348,13 @@
     square_ref[...] = jnp.broadcast_to(jnp.sum(ys * ys, axis=1, keepdims=True), square_ref.shape)
 
 
-def scan_forward(slot, fixed, start, xs, z, low, bc, step_w, bias, rate2, skip, gain, unit_rows):
+def scan_forward(slot, fixed, start, xs, z, low, bc, step_w, bias, rate2, skip, gain, unit_rows, deps=()):
     rows, width = xs.shape
     units = rows // unit_rows
     rank = low.shape[1]
     count = -(-width // 128)
     return pl.pallas_call(
-        scan_kernel_fwd,
+later(        scan_kernel_fwd, 12, deps),
         out_shape=(
             jax.ShapeDtypeStruct((rows, width), F32),
             jax.ShapeDtypeStruct((rows, width), BF16),
@@ -354,7 +378,7 @@
                 whole_spec((STATE, width)),
                 whole_spec((1, width)),
                 whole_spec((1, width)),
-            ],
+            ] + wait_specs(deps),
             out_specs=[
                 unit_spec(unit_rows, width),
                 unit_spec(unit_rows, width),
@@ -371,11 +395,8 @@
             ],
         ),
         compiler_params=params(),
-        cost_estimate=pl.CostEstimate(
-            flops=rows * width * STATE * 8, bytes_accessed=rows * width * 12,
-            transcendentals=rows * width * STATE,
-        ),
-    )(slot, fixed, start, xs, z, low, bc, step_w, bias, rate2, skip, gain)
+        cost_estimate=SMALL_COST,
+    )(slot, fixed, start, xs, z, low, bc, step_w, bias, rate2, skip, gain, *deps)
 
 
 def scan_kernel_bwd(
@@ -479,7 +500,7 @@
 
 
 def scan_backward(
-    slot, fixed, start, dc, stat, y, z, xs, low, wide, before, final, step_w, bias, rate2, skip, gain, unit_rows
+    slot, fixed, start, dc, stat, y, z, xs, low, wide, before, final, step_w, bias, rate2, skip, gain, unit_rows, deps=()
 ):
     rows, width = xs.shape
     units = rows // unit_rows
@@ -487,7 +508,7 @@
     count = -(-width // 128)
     last = units - 1
     return pl.pallas_call(
-        scan_kernel_bwd,
+        later(scan_kernel_bwd, 3 + 14, deps),
         out_shape=(
             jax.ShapeDtypeStruct((rows, width), BF16),
             jax.ShapeDtypeStruct((rows, width), F32),
@@ -517,7 +538,7 @@
                 whole_spec((STATE, width)),
                 whole_spec((1, width)),
                 whole_spec((1, width)),
-            ],
+            ] + wait_specs(deps),
             out_specs=[
                 unit_spec(unit_rows, width, units),
                 unit_spec(unit_rows, width, units),
@@ -542,11 +563,8 @@
             ],
         ),
         compiler_params=params(),
-        cost_estimate=pl.CostEstimate(
-            flops=rows * width * STATE * 24, bytes_accessed=rows * width * 24,
-            transcendentals=rows * width * STATE,
-        ),
-    )(slot, fixed, start, dc, stat, y, z, xs, low, wide, before, final, step_w, bias, rate2, skip, gain)
+        cost_estimate=SMALL_COST,
+    )(slot, fixed, start, dc, stat, y, z, xs, low, wide, before, final, step_w, bias, rate2, skip, gain, *deps)
 
 
 PAIR_WIDTH = 2 * HEAD_SIZE
@@ -611,12 +629,12 @@
     )[0:1]
 
 
-def attn_forward(slot, low_block, pair, q, k, vt, gain, unit_rows):
+def attn_forward(slot, low_block, pair, q, k, vt, gain, unit_rows, deps=()):
     rows, width = q.shape
     units = rows // unit_rows
     lanes = width // HEAD_SIZE * unit_rows
     return pl.pallas_call(
-        attn_kernel_fwd,
+later(        attn_kernel_fwd, 7, deps),
         out_shape=(
             jax.ShapeDtypeStruct((rows, width), F32),
             jax.ShapeDtypeStruct((rows, width), BF16),
@@ -630,7 +648,7 @@
                 whole_spec(k.shape),
                 whole_spec(vt.shape),
                 whole_spec((1, width)),
-            ],
+            ] + wait_specs(deps),
             out_specs=[
                 unit_spec(unit_rows, width),
                 unit_spec(unit_rows, width),
@@ -638,11 +656,8 @@
             ],
         ),
         compiler_params=params(),
-        cost_estimate=pl.CostEstimate(
-            flops=2 * rows * rows * width, bytes_accessed=rows * width * 8,
-            transcendentals=rows * rows * (width // HEAD_SIZE) // 2,
-        ),
-    )(slot, low_block, pair, q, k, vt, gain)
+        cost_estimate=SMALL_COST,
+    )(slot, low_block, pair, q, k, vt, gain, *deps)
 
 
 def attn_kernel_bwd(
@@ -694,12 +709,12 @@
     dq_ref[...] = (unstack_heads(dq, pair, rows) * HEAD_SIZE**-0.5).astype(BF16)
 
 
-def attn_backward(slot, low_block, pair, q, o, do, stat, k, kt, v, unit_rows):
+def attn_backward(slot, low_block, pair, q, o, do, stat, k, kt, v, unit_rows, deps=()):
     rows, width = q.shape
     units = rows // unit_rows
     lanes = width // HEAD_SIZE * unit_rows
     return pl.pallas_call(
-        attn_kernel_bwd,
+later(        attn_kernel_bwd, 10, deps),
         out_shape=(
             jax.ShapeDtypeStruct((rows, width), BF16),
             jax.ShapeDtypeStruct(k.shape, F32),
@@ -716,23 +731,314 @@
                 whole_spec(k.shape),
                 whole_spec(kt.shape),
                 whole_spec(v.shape),
-            ],
+            ] + wait_specs(deps),
             out_specs=[unit_spec(unit_rows, width), whole_spec(k.shape), whole_spec(v.shape)],
         ),
         compiler_params=params(),
-        cost_estimate=pl.CostEstimate(
-            flops=5 * rows * rows * width, bytes_accessed=rows * width * 12,
-            transcendentals=rows * rows * (width // HEAD_SIZE) // 2,
-        ),
-    )(slot, low_block, pair, q, o, do, stat, k, kt, v)
+        cost_estimate=SMALL_COST,
+    )(slot, low_block, pair, q, o, do, stat, k, kt, v, *deps)
+
+
+def fill_width(width):
+    return -(-width // 128) * 128
+
+
+def piece_specs(pieces, block_rows):
+    if len(pieces) == 1:
+        return [pl.BlockSpec((block_rows, pieces[0].shape[1]), lambda i, *_: (i, 0))]
+    return [whole_spec(piece.shape) for piece in pieces]
+
+
+def take_piece(refs, buf):
+    if len(refs) == 1:
+        buf[...] = refs[0][...]
+        return
+    step = pl.program_id(0)
+    for k, ref in enumerate(refs):
+
+        @pl.when(step == k)
+        def _(ref=ref):
+            buf[...] = ref[...]
+
+
+def store_filled(ref, value):
+    width = value.shape[1]
+    ref[:, :width] = value.astype(ref.dtype)
+    if ref.shape[1] > width:
+        ref[:, width:] = jnp.zeros((ref.shape[0], ref.shape[1] - width), ref.dtype)
+
+
+def whole_call(kernel, out_shape, *values, deps=()):
+    return pl.pallas_call(
+        later(kernel, len(values), deps),
+        out_shape=out_shape,
+        in_specs=[pl.BlockSpec(memory_space=pltpu.VMEM)] * len(values) + wait_specs(deps),
+        out_specs=[pl.BlockSpec(memory_space=pltpu.VMEM)] * len(out_shape),
+        compiler_params=pltpu.CompilerParams(vmem_limit_bytes=VMEM_LIMIT),
+        cost_estimate=SMALL_COST,
+    )(*values, *deps)
+
+
+def chip_sum_kernel(mine, mate, own, to_x, to_y, keep_x, keep_y):
+    size = own.shape[0]
+    half = size // 2
+    block = lambda i, a, b: (
+        mine[i * size + a : i * size + b, :].astype(F32)
+        + mate[i * size + a : i * size + b, :].astype(F32)
+    )
+    own[...] = block(0, 0, size)
+    to_x[:half, :] = block(1, 0, half).astype(BF16)
+    to_x[half:, :] = block(3, 0, half).astype(BF16)
+    to_y[:half, :] = block(2, half, size).astype(BF16)
+    to_y[half:, :] = block(3, half, size).astype(BF16)
+    keep_x[...] = block(1, half, size)
+    keep_y[...] = block(2, 0, half)
+
+
+def near_sum_kernel(own, keep_x, keep_y, by_x, by_y, part, to_x, to_y):
+    half = keep_x.shape[0]
+    part[:half, :] = own[:half, :] + by_x[:half, :].astype(F32)
+    part[half:, :] = own[half:, :] + by_y[:half, :].astype(F32)
+    to_x[...] = (keep_x[...] + by_y[half:, :].astype(F32)).astype(BF16)
+    to_y[...] = (keep_y[...] + by_x[half:, :].astype(F32)).astype(BF16)
+
+
+def far_sum_kernel(part, by_y, by_x, out):
+    half = by_y.shape[0]
+    out[:half, :] = part[:half, :] + by_y[...].astype(F32)
+    out[half:, :] = part[half:, :] + by_x[...].astype(F32)
+
+
+def join_qkv_kernel(queries, keys, values, out):
+    at = 0
+    for ref in (queries, keys, values):
+        out[:, at : at + ref.shape[1]] = ref[...].astype(BF16)
+        at += ref.shape[1]
+
+
+def cross_kernel(by_x, by_y, to_y, to_x):
+    half = to_x.shape[0]
+    to_y[...] = by_x[:half, :]
+    to_x[...] = by_y[half:, :]
+
+
+def join_kernel(left, right, out):
+    out[:, : left.shape[1]] = left[...]
+    out[:, left.shape[1] :] = right[...]
+
+
+def two_sums_kernel(top, by_x, end, by_y, out_top, out_end):
+    out_top[...] = (top[...].astype(F32) + by_x[...].astype(F32)).astype(BF16)
+    out_end[...] = (end[...].astype(F32) + by_y[...].astype(F32)).astype(BF16)
+
+
+def move_kernel(moves, in_ref, out_ref):
+    out_ref[...] = jnp.zeros_like(out_ref)
+    for a, lo, b, to, size in moves:
+        out_ref[b, :, to : to + size] = in_ref[a, :, lo : lo + size]
+
+
+def move_columns(value, moves, blocks, width, deps=()):
+    return pl.pallas_call(
+later(        functools.partial(move_kernel, tuple(moves)), 1, deps),
+        out_shape=jax.ShapeDtypeStruct((blocks, value.shape[1], width), value.dtype),
+        in_specs=[pl.BlockSpec(memory_space=pltpu.VMEM)] + wait_specs(deps),
+        out_specs=pl.BlockSpec(memory_space=pltpu.VMEM),
+        compiler_params=pltpu.CompilerParams(vmem_limit_bytes=VMEM_LIMIT),
+    )(value, *deps)
+
+
+def pick_kernel(cases, place_ref, in_ref, out_ref):
+    out_ref[...] = jnp.zeros_like(out_ref)
+    for place, moves in enumerate(cases):
+
+        @pl.when(place_ref[0] == place)
+        def _(moves=moves):
+            for a, lo, _, to, size in moves:
+                out_ref[:, to : to + size] = in_ref[a, :, lo : lo + size]
+
+
+def pick_columns(value, place, cases, width, deps=()):
+    return pl.pallas_call(
+later(        functools.partial(pick_kernel, tuple(tuple(moves) for moves in cases)), 2, deps),
+        out_shape=jax.ShapeDtypeStruct((value.shape[1], width), value.dtype),
+        in_specs=[
+            pl.BlockSpec(memory_space=pltpu.SMEM), pl.BlockSpec(memory_space=pltpu.VMEM),
+        ] + wait_specs(deps),
+        out_specs=pl.BlockSpec(memory_space=pltpu.VMEM),
+        compiler_params=pltpu.CompilerParams(vmem_limit_bytes=VMEM_LIMIT),
+    )(place.astype(jnp.int32).reshape(1), value, *deps)
+
+
+def runs(spans, each):
+    out = []
+    for column, block, to, size in spans:
+        while size > 0:
+            part, lo = divmod(column, each)
+            some = min(size, each - lo)
+            out.append((part, lo, block, to, some))
+            column, to, size = column + some, to + some, size - some
+    return out
+
+
+def project_kernel(count, added, cuts, half, *refs):
+    lefts, weights = refs[:count], refs[count : 2 * count]
+    outs = refs[2 * count + added :]
+    total = None
+    for left, weight, (lo, hi) in zip(lefts, weights, cuts):
+        part = dot_nt(left[...], weight[:, lo:hi])
+        total = part if total is None else total + part
+    if added:
+        total = total + refs[2 * count][:, : total.shape[1]].astype(F32)
+    if half == 0:
+        store_filled(outs[0], total)
+        return
+
+    @pl.when(pl.program_id(0) < half)
+    def _():
+        store_filled(outs[0], total)
+
+    @pl.when(pl.program_id(0) >= half)
+    def _():
+        store_filled(outs[1], total)
+
+
+def project(lefts, weights, cuts, block_rows, split=False, addend=None, deps=()):
+    size = weights[0].shape[0]
+    rows = lefts[0].shape[0]
+    blocks = rows // block_rows
+    half = blocks // 2 if split else 0
+    by_rows_spec = lambda width: pl.BlockSpec(
+        (block_rows, width), lambda i: ((i + half) % blocks, 0)
+    )
+    extra = [] if addend is None else [addend]
+    shape = jax.ShapeDtypeStruct((rows // 2 if split else rows, fill_width(size)), BF16)
+    block = (block_rows, fill_width(size))
+    if split:
+        out_shape = (shape, shape)
+        out_specs = (
+            pl.BlockSpec(block, lambda i: (jnp.minimum(i, half - 1), 0)),
+            pl.BlockSpec(block, lambda i: (jnp.maximum(i - half, 0), 0)),
+        )
+    else:
+        out_shape, out_specs = (shape,), (pl.BlockSpec(block, lambda i: (i, 0)),)
+    return pl.pallas_call(
+        later(
+            functools.partial(project_kernel, len(lefts), bool(extra), cuts, half),
+            2 * len(lefts) + len(extra), deps,
+        ),
+        out_shape=out_shape,
+        grid=(blocks,),
+        in_specs=[by_rows_spec(left.shape[1]) for left in lefts]
+        + [whole_spec(weight.shape) for weight in weights]
+        + [by_rows_spec(part.shape[1]) for part in extra]
+        + wait_specs(deps),
+        out_specs=out_specs,
+        compiler_params=params(),
+        cost_estimate=SMALL_COST,
+    )(*lefts, *weights, *extra, *deps)
+
+
+def ffn_kernel(count, model, order, *refs):
+    x_refs, c_ref = refs[:count], refs[count]
+    gate_ref, up_ref, down_ref = refs[count + 1 : count + 4]
+    x_out, c_out, hidden_ref, dgate_ref, dup_ref, back_ref, out_ref, x_buf = refs[-8:]
+    take_piece(x_refs, x_buf)
+    x = x_buf[:, :model]
+    c = c_ref[...]
+    x_out[...] = x
+    c_out[...] = c
+    gate = dot_nn(x, gate_ref[...])
+    up = dot_nn(x, up_ref[...])
+    sig = sigmoid(gate)
+    act = gate * sig
+    hidden = (act * up).astype(BF16)
+    d_hidden = dot_nn(c, down_ref[...])
+    d_gate = (d_hidden * up * (sig * (1.0 + gate * (1.0 - sig)))).astype(BF16)
+    d_up = (d_hidden * act).astype(BF16)
+    hidden_ref[...] = hidden
+    dgate_ref[...] = d_gate
+    dup_ref[...] = d_up
+    store_filled(back_ref, dot_nt(d_gate, gate_ref[...]) + dot_nt(d_up, up_ref[...]))
+    store_filled(out_ref, dot_nt(hidden, down_ref[...]))
+
+
+def ffn(order, x_pieces, cot, gate_w, up_w, down_wt, first, rows, block_rows, earlier=None):
+    model, hidden = gate_w.shape
+    all_rows = cot.shape[0]
+    filled = x_pieces[0].shape[1]
+    count = len(x_pieces)
+    begin = first // block_rows
+    carried = [model, model, hidden, hidden, hidden]
+    extra = [] if earlier is None else list(earlier)
+    in_count = count + 5
+    place_spec = lambda width: pl.BlockSpec((block_rows, width), lambda i, *_: (begin + i, 0))
+    own_spec = pl.BlockSpec((block_rows, fill_width(model)), lambda i, *_: (i, 0))
+    return pl.pallas_call(
+        functools.partial(ffn_kernel, count, model),
+        out_shape=[jax.ShapeDtypeStruct((all_rows, width), BF16) for width in carried]
+        + [jax.ShapeDtypeStruct((rows, fill_width(model)), BF16)] * 2,
+        grid_spec=pltpu.PrefetchScalarGridSpec(
+            num_scalar_prefetch=1,
+            grid=(rows // block_rows,),
+            in_specs=piece_specs(x_pieces, block_rows)
+            + [pl.BlockSpec((block_rows, model), lambda i, order: (order[begin + i], 0))]
+            + [whole_spec(gate_w.shape)] * 3
+            + [pl.BlockSpec(memory_space=pl.ANY)] * len(extra),
+            out_specs=[place_spec(width) for width in carried] + [own_spec] * 2,
+            scratch_shapes=[pltpu.VMEM((block_rows, filled), BF16)],
+        ),
+        input_output_aliases={in_count + i: i for i in range(len(extra))},
+        compiler_params=params(),
+        cost_estimate=SMALL_COST,
+    )(order, *x_pieces, cot, gate_w, up_w, down_wt, *extra)
+
+
+def branch_kernel(count, model, split, *refs):
+    pieces, weight_ref = refs[:count], refs[count]
+    d_out, attn_ref, ssm_ref, buf = refs[count + 1 :]
+    take_piece(pieces, buf)
+    d = buf[:, :model]
+    d_out[...] = d
+    ssm_ref[...] = dot_nn(d, weight_ref[:, split:])
+    attn_ref[...] = dot_nn(d, weight_ref[:, :split])
+
+
+def branch(pieces, weight, split, block_rows):
+    model, depth = weight.shape
+    rows = sum(piece.shape[0] for piece in pieces)
+    spec = lambda width: pl.BlockSpec((block_rows, width), lambda i: (i, 0))
+    return pl.pallas_call(
+        functools.partial(branch_kernel, len(pieces), model, split),
+        out_shape=(
+            jax.ShapeDtypeStruct((rows, model), BF16),
+            jax.ShapeDtypeStruct((rows, split), F32),
+            jax.ShapeDtypeStruct((rows, depth - split), F32),
+        ),
+        grid=(rows // block_rows,),
+        in_specs=piece_specs(pieces, block_rows) + [whole_spec(weight.shape)],
+        out_specs=(spec(model), spec(split), spec(depth - split)),
+        scratch_shapes=[pltpu.VMEM((block_rows, pieces[0].shape[1]), BF16)],
+        compiler_params=params(),
+        cost_estimate=SMALL_COST,
+    )(*pieces, weight)
 
 
 ORDER = (0, 2, 4, 6, 1, 3, 5, 7)
 CUBE = len(ORDER)
 
 
+def by_rows(value):
+    return with_layout_constraint(value, Layout(major_to_minor=tuple(range(value.ndim))))
+
+
 def swap(value, mask):
     return lax.ppermute(value, "ctx", [(d, d ^ mask) for d in range(CUBE)])
+
+
+def fill_lanes(value):
+    more = -value.shape[1] % 128
+    return jnp.pad(value.astype(BF16), ((0, 0), (0, more)))
 
 
 def block_order(place, devices):
@@ -748,52 +1054,65 @@
     return owner
 
 
-def rows_gather(own, devices):
-    pieces = gather_pieces(own, devices)
-    return pieces[0] if len(pieces) == 1 else jnp.concatenate(pieces, axis=0)
-
-
 def gather_pieces(own, devices):
     if devices != CUBE:
         return [lax.all_gather(own, "ctx", axis=0, tiled=True)]
-    half = own.shape[0] // 2
     by_x, by_y, mate = swap(own, 2), swap(own, 4), swap(own, 1)
-    far = jnp.concatenate([swap(by_x[:half], 4), swap(by_y[half:], 2)], axis=0)
-    mates = [mate, swap(by_x, 1), swap(by_y, 1), swap(far, 1)]
-    return [own, by_x, by_y, far] + mates
-
-
-def rows_scatter(make, rows, devices):
+    part = jax.ShapeDtypeStruct((own.shape[0] // 2, own.shape[1]), own.dtype)
+    to_y, to_x = whole_call(cross_kernel, [part, part], by_x, by_y)
+    far = jnp.concatenate([swap(to_y, 4), swap(to_x, 2)], axis=0)
+    return [own, by_x, by_y, far, mate, swap(by_x, 1), swap(by_y, 1), swap(far, 1)]
+
+
+def row_halves(rows, devices):
+    return [(rows // 2, rows // 2), (0, rows // 2)] if devices == CUBE else [(0, rows)]
+
+
+def scatter_begin(part, devices):
+    return swap(part, 1) if devices == CUBE else part
+
+
+def scatter_chip(mine, from_mate, devices, deps=()):
     if devices != CUBE:
-        return lax.psum_scatter(make(0, rows), "ctx", scatter_dimension=0, tiled=True).astype(F32)
-    size = rows // CUBE
-    half = size // 2
-    from_mate = swap(make(rows // 2, rows), 1)
-    total = make(0, rows // 2).astype(F32) + from_mate.astype(F32)
-    cut = lambda i, a, b: total[i * size + a : i * size + b]
-    far_x = swap(cut(3, 0, half).astype(BF16), 2)
-    far_y = swap(cut(3, half, size).astype(BF16), 4)
-    x_top = swap(cut(1, 0, half).astype(BF16), 2)
-    y_end = swap(cut(2, half, size).astype(BF16), 4)
-    x_end = swap((cut(1, half, size) + far_y.astype(F32)).astype(BF16), 2)
-    y_top = swap((cut(2, 0, half) + far_x.astype(F32)).astype(BF16), 4)
-    top = cut(0, 0, half) + x_top.astype(F32) + y_top.astype(F32)
-    end = cut(0, half, size) + x_end.astype(F32) + y_end.astype(F32)
-    return jnp.concatenate([top, end], axis=0)
-
-
-def offload_gather(own, place, devices):
-    got = lax.all_gather(own, "ctx", axis=0)
-    if devices == CUBE:
-        got = got[block_order(place, devices)]
-    return got.reshape(-1, own.shape[1])
-
-
-def offload_scatter(value, place, devices):
-    blocks = value.reshape(devices, -1, value.shape[1])
-    if devices == CUBE:
-        blocks = blocks[block_index(jnp.arange(CUBE, dtype=jnp.int32), place, devices)]
-    return lax.psum_scatter(blocks, "ctx", scatter_dimension=0, tiled=False).astype(F32)
+        return (mine,)
+    size, width = mine.shape[0] * 2 // CUBE, mine.shape[1]
+    shape = lambda rows, kind: jax.ShapeDtypeStruct((rows, width), kind)
+    whole, half = shape(size, F32), shape(size // 2, F32)
+    send = shape(size, BF16)
+    return whole_call(
+        chip_sum_kernel, [whole, send, send, half, half], mine, from_mate, deps=deps
+    )
+
+
+def scatter_links(parts, devices, deps=()):
+    if devices != CUBE:
+        return parts
+    own, to_x, to_y, keep_x, keep_y = parts
+    low = jax.ShapeDtypeStruct(keep_x.shape, BF16)
+    return whole_call(
+        near_sum_kernel, [jax.ShapeDtypeStruct(own.shape, F32), low, low],
+        own, keep_x, keep_y, swap(to_x, 2), swap(to_y, 4), deps=deps,
+    )
+
+
+def scatter_near(mine, from_mate, devices):
+    return scatter_links(scatter_chip(mine, from_mate, devices), devices)
+
+
+def scatter_far(parts, width, devices, deps=()):
+    if devices != CUBE:
+        total = lax.psum_scatter(parts[0], "ctx", scatter_dimension=0, tiled=True)
+        return total[:, :width].astype(F32)
+    part, to_x, to_y = parts
+    shape = jax.ShapeDtypeStruct(part.shape, F32)
+    total = whole_call(
+        far_sum_kernel, [shape], part, swap(to_y, 4), swap(to_x, 2), deps=deps
+    )[0]
+    return total[:, :width]
+
+
+def scatter_end(mine, from_mate, width, devices):
+    return scatter_far(scatter_near(mine, from_mate, devices), width, devices)
 
 
 def exchange(blocks):
@@ -812,23 +1131,42 @@
     return jnp.stack([swap(value, k) if k else value for k in ORDER])
 
 
-def place_gather(value, place, devices):
-    got = small_gather(value, place, devices)
+def in_places(got, place, devices):
     if devices != CUBE:
         return got
+    got = jnp.stack(got)
     return got[block_index(jnp.arange(CUBE, dtype=jnp.int32), place, devices)]
 
 
-def all_sum(value, devices):
+def place_gather(value, place, devices, ordered=True):
     if devices != CUBE:
-        return lax.psum(value, "ctx")
-    add = lambda a, b: (a.astype(F32) + b.astype(F32)).astype(BF16)
-    value = add(value, swap(value, 1))
+        return lax.all_gather(value, "ctx", axis=0)
+    got = [swap(value, k) if k else value for k in ORDER]
+    return in_places(got, place, devices) if ordered else got
+
+
+def add_low(a, b):
+    return (a.astype(F32) + b.astype(F32)).astype(BF16)
+
+
+def all_sum_core(value, devices):
+    return add_low(value, swap(value, 1)) if devices == CUBE else value
+
+
+def all_sum_near(value, devices, deps=()):
+    if devices != CUBE:
+        return (value,)
     half = value.shape[0] // 2
     top, end = value[:half], value[half:]
-    top, end = add(top, swap(top, 2)), add(end, swap(end, 4))
-    top, end = add(top, swap(top, 4)), add(end, swap(end, 2))
-    return jnp.concatenate([top, end], axis=0)
+    shape = jax.ShapeDtypeStruct(top.shape, top.dtype)
+    return whole_call(two_sums_kernel, [shape, shape], top, swap(top, 2), end, swap(end, 4), deps=deps)
+
+
+def all_sum_far(parts, devices):
+    if devices != CUBE:
+        return lax.psum(parts[0], "ctx")
+    top, end = parts
+    return jnp.concatenate([add_low(top, swap(top, 4)), add_low(end, swap(end, 2))], axis=0)
 
 
 def lane_gather(value):
@@ -849,26 +1187,22 @@
     return got[(lane - jnp.arange(lanes, dtype=jnp.int32)) % lanes]
 
 
-def lane_small_scatter(blocks, lanes):
+def lane_small_exchange(blocks, lanes):
     lane = lax.axis_index("fsdp")
     pick = lambda k: lax.dynamic_index_in_dim(blocks, (lane + k) % lanes, 0, False)
-    return pick(0) + sum(lane_shift(pick(k), lanes, k) for k in range(1, lanes))
+    return tuple(lane_shift(pick(k), lanes, k) if k else pick(0) for k in range(lanes))
+
+
+def lane_small_scatter(blocks, lanes):
+    return sum(part.astype(F32) for part in lane_small_exchange(blocks, lanes))
 
 
 def after(value, *earlier):
     return lax.optimization_barrier((value,) + earlier)[0]
 
 
-def columns_to_rows(value, devices):
-    width = value.shape[1]
-    got = exchange(value.reshape(devices, -1, width))
-    return jnp.transpose(got, (1, 0, 2)).reshape(-1, devices * width)
-
-
-def rows_to_columns(value, devices):
-    rows = value.shape[0]
-    blocks = jnp.transpose(value.reshape(rows, devices, -1), (1, 0, 2))
-    return exchange(blocks).reshape(devices * rows, -1)
+def back(moves):
+    return [(b, to, a, lo, size) for a, lo, b, to, size in moves]
 
 
 def pair_routes(devices):
@@ -954,7 +1288,10 @@
     x_part, z_part = split_pairs(w_xz, place, devices)
 
     small = after(
-        jnp.concatenate([conv_kernel, state_proj, step_proj, decay_log], axis=0), x_part
+        jnp.concatenate(
+            [conv_kernel, state_proj, step_proj, decay_log, meta_tokens.reshape(-1, width)], axis=0
+        ),
+        x_part,
     )
     small_all = lane_small_gather(small, lanes)
     marks = [conv_kernel.shape[0], state_proj.shape[0], step_proj.shape[0], decay_log.shape[0]]
@@ -962,10 +1299,10 @@
     conv_w = small_all[:, : ends[0]].reshape(-1, width).astype(F32)
     sel_w = small_all[:, ends[0] : ends[1]].reshape(-1, width)
     step_w = small_all[:, ends[1] : ends[2]].reshape(-1, width)
-    decay = small_all[:, ends[2] :].reshape(-1, width).astype(F32)
+    decay = small_all[:, ends[2] : ends[3]].reshape(-1, width).astype(F32)
     rate = -jnp.exp(decay)
     rate2 = rate * LOG2E
-    meta_part = lane_small_gather(after(meta_tokens, x_part), lanes).reshape(-1, model_part)
+    meta_part = small_all[:, ends[3] :].reshape(-1, model_part)
     meta_rows = meta_part.shape[0]
     wide = jnp.concatenate(
         [meta_part, input_gain[None], ffn_gain[None], attn_gain[None]], axis=0
@@ -982,82 +1319,100 @@
     skip = skip_gain.astype(F32)[None]
     gain_ssm = ssm_gain.astype(F32)[None]
 
-    first_kv = (place * heads) // group
-    qkv_row = place_gather(after(query_key_value_weight, x_part), place, devices)
-    qkv_row = jnp.transpose(qkv_row, (1, 0, 2)).reshape(qkv_row.shape[1], -1)
-    q_part = lax.dynamic_slice_in_dim(
-        pad_to(qkv_row[:, :query_width], devices * head_width, 1), place * head_width, head_width, 1
-    )
-    kv_room = (devices * heads // group + 3) * HEAD_SIZE
-    k_part = lax.dynamic_slice_in_dim(
-        pad_to(qkv_row[:, query_width : query_width + kv_width], kv_room, 1),
-        first_kv * HEAD_SIZE, 2 * HEAD_SIZE, 1,
-    )
-    v_part = lax.dynamic_slice_in_dim(
-        pad_to(qkv_row[:, query_width + kv_width :], kv_room, 1),
-        first_kv * HEAD_SIZE, 2 * HEAD_SIZE, 1,
-    )
-    pair = jnp.clip(
-        (place * heads + jnp.arange(heads, dtype=jnp.int32)) // group - first_kv, 0, 1
-    ).astype(jnp.int32)
-    qkv_width = head_width + 4 * HEAD_SIZE
-    x_w = lane_gather(x_part)
-    qkvz_w = lane_gather(jnp.concatenate([q_part, k_part, v_part, z_part], axis=1))
-    qkv_w = qkvz_w[:, :qkv_width]
-    z_w = qkvz_w[:, qkv_width:]
-    out_cols = lane_gather(after(out_proj, x_w))
-    gate_up_w = lane_gather(jnp.concatenate([after(w_gate, qkvz_w), w_up], axis=1))
-    gate_w = gate_up_w[:, :hidden_width]
-    up_w = gate_up_w[:, hidden_width:]
-    down_cols = lane_gather(after(w_down, out_cols))
-    blocks = jnp.concatenate(
-        [
-            pad_to(out_cols[:query_width], devices * head_width, 0).reshape(
-                devices, head_width, model_part
-            ),
-            out_cols[query_width:].reshape(devices, width, model_part),
-        ],
-        axis=1,
-    )
-    out_w = columns_to_rows(blocks.reshape(-1, model_part), devices)
-    down_w = columns_to_rows(down_cols, devices)
+    xz_w = lane_gather(jnp.concatenate([x_part, z_part], axis=1))
+    x_w, z_w = xz_w[:, :width], xz_w[:, width:]
+    out_held = hold(jnp.transpose(out_proj), small_all)
+    out_cols = lax.all_gather(out_held, "fsdp", axis=0)
+    order = block_order(place, devices)
+    piece_rows = min(256, own_rows)
 
     own_tok = tokens[0]
+    pieces = gather_pieces(fill_lanes(after(own_tok, x_part)), devices)
     slot_start = jnp.sum(
         jnp.where(slot[None, :] == slot_ids[:, None], starts_int[None, :], 0), axis=1
     ).astype(jnp.int32)
-    normed = norm_all(slot_start, meta, gain_in[None], gather_pieces(own_tok, devices))
+    normed = norm_all(slot_start, meta, gain_in[None], pieces)
+    qkv_all = lax.all_gather(hold(query_key_value_weight, normed, out_held), "ctx", axis=0)
     resid = jnp.where(
         my_start[:, None, None], meta[None], own_tok.reshape(2, unit_rows, model).astype(F32)
     ).reshape(own_rows, model)
     in_factor = rms_factor(resid)
 
     x_in = dot_nn(normed, x_w).astype(BF16)
-    cot = offload_gather(after(cotangent[0], gate_up_w), place, devices)
+
     conv_out, ssm_in, select = conv_forward(
         slot, fixed, starts_int, x_in, conv_w, sel_w, unit_rows
     )
-    select = all_sum(select, devices).astype(F32)
+    select = all_sum_core(select, devices)
+    z_gate = dot_nn(normed, z_w).astype(BF16)
+    near = all_sum_near(select, devices, (z_gate,))
+    select = all_sum_far(near, devices).astype(F32)
+    first_kv = (place * heads) // group
+    kv_room = (devices * heads // group + 3) * HEAD_SIZE
+    cases = []
+    for d in range(devices):
+        some = max(0, min(head_width, query_width - d * head_width))
+        spans = [(d * head_width, 0, 0, some)]
+        low_kv = d * heads // group * HEAD_SIZE
+        some = max(0, min(PAIR_WIDTH, kv_width - low_kv))
+        for i in range(2):
+            begin = query_width + i * kv_width + low_kv
+            spans.append((begin, 0, head_width + i * PAIR_WIDTH, some))
+        cases.append(runs(spans, query_key_value_weight.shape[1]))
+    qkv_width = head_width + 2 * PAIR_WIDTH
+    qkv_part = pick_columns(qkv_all, place, cases, qkv_width, (near[0],))
+    qkv_w = lane_gather(qkv_part)
+    pair = jnp.clip(
+        (place * heads + jnp.arange(heads, dtype=jnp.int32)) // group - first_kv, 0, 1
+    ).astype(jnp.int32)
+    cot_own = hold(cotangent[0], qkv_part)
+    cot = lax.all_gather(cot_own, "ctx", axis=0, tiled=True)
+    down_held = hold(jnp.transpose(w_down), cot_own)
+    down_cols = lax.all_gather(down_held, "fsdp", axis=0)
+    gate_held = hold(w_gate, down_held)
+    gate_w = lane_gather(gate_held)
+    up_held = hold(w_up, gate_held)
+    up_w = lane_gather(up_held)
+    spans = []
+    for d in range(devices):
+        some = max(0, min(head_width, query_width - d * head_width))
+        spans += [(d * head_width, d, 0, some), (query_width + d * width, d, head_width, width)]
+    out_moves = runs(spans, out_proj.shape[0])
+    out_blocks = move_columns(out_cols, out_moves, devices, head_width + width, (select,))
+    out_wt = exchange(out_blocks).reshape(model, -1)
+    down_moves = runs(
+        [(d * hidden_width, d, 0, hidden_width) for d in range(devices)], w_down.shape[0]
+    )
+    step_low = select[:, :DT_RANK].astype(BF16)
+    bc = jnp.transpose(select[:, DT_RANK:].reshape(units, unit_rows, 2 * STATE), (0, 2, 1))
+    y_total, ssm_comb, ssm_square, wide_bc, states, last_states = scan_forward(
+        slot, fixed, starts_int, ssm_in, z_gate, step_low, bc, step_w, bias, rate2, skip, gain_ssm,
+        unit_rows, (out_blocks, up_held),
+    )
+
+    cube = devices == CUBE
+
+    def out_term(comb, lo, hi, *deps):
+        return project([comb], [out_wt], [(lo, hi)], piece_rows, cube, None, deps)
+
+    ssm_terms = out_term(ssm_comb, head_width, head_width + width)
+    ssm_mate = scatter_begin(ssm_terms[0], devices)
     qkv = dot_nn(normed, qkv_w).astype(BF16)
+    ssm_chip = scatter_chip(ssm_terms[-1], ssm_mate, devices, (qkv,))
+    down_blocks = move_columns(down_cols, down_moves, devices, hidden_width, (ssm_chip[0],))
+    down_wt = exchange(down_blocks).reshape(model, -1)
     queries = qkv[:, :head_width]
     keys = qkv[:, head_width : head_width + PAIR_WIDTH]
     values = qkv[:, head_width + PAIR_WIDTH :]
     attn, attn_comb, attn_stat = attn_forward(
-        slot, low_block, pair, queries, keys, jnp.transpose(values), gain_attn, unit_rows
-    )
-    attn_out = rows_scatter(
-        lambda a, b: dot_nn(attn_comb[a:b], out_w[:head_width]).astype(BF16), rows, devices
-    )
-    z_gate = dot_nn(normed, z_w).astype(BF16)
-    step_low = select[:, :DT_RANK].astype(BF16)
-    bc = jnp.transpose(select[:, DT_RANK:].reshape(units, unit_rows, 2 * STATE), (0, 2, 1))
-    y_total, ssm_comb, ssm_square, wide_bc, states, last_states = scan_forward(
-        slot, fixed, starts_int, ssm_in, z_gate, step_low, bc, step_w, bias, rate2, skip, gain_ssm,
-        unit_rows,
-    )
-    ssm_out = rows_scatter(
-        lambda a, b: dot_nn(ssm_comb[a:b], out_w[head_width:]).astype(BF16), rows, devices
-    )
+        slot, low_block, pair, queries, keys, jnp.transpose(values), gain_attn, unit_rows,
+        (ssm_chip[0], down_blocks),
+    )
+    ssm_near = scatter_links(ssm_chip, devices, (attn_comb,))
+    attn_terms = out_term(attn_comb, 0, head_width, down_wt, ssm_near[0])
+    ssm_out = scatter_far(ssm_near, model, devices)
+    attn_mate = scatter_begin(attn_terms[0], devices)
+    attn_out = scatter_end(attn_terms[-1], attn_mate, model, devices)
     squares = jnp.stack(
         [
             attn_stat[:, 1, :unit_rows].reshape(devices, own_rows),
@@ -1073,35 +1428,36 @@
         + 0.5 * own_factors[1][:, None] * ssm_out
     )
     mid_factor = rms_factor(mid)
-    ffn_in = rows_gather((mid * mid_factor * gain_ffn).astype(BF16), devices)
-
-    gate = dot_nn(ffn_in, gate_w)
-    up = dot_nn(ffn_in, up_w)
-    sig = jax.nn.sigmoid(gate)
-    act = gate * sig
-    hidden = (act * up).astype(BF16)
-    d_hidden = dot_nt(cot, down_w)
-    d_gate = (d_hidden * up * (sig * (1.0 + gate * (1.0 - sig)))).astype(BF16)
-    d_up = (d_hidden * act).astype(BF16)
-    d_ffn = rows_scatter(
-        lambda a, b: (dot_nt(d_gate[a:b], gate_w) + dot_nt(d_up[a:b], up_w)).astype(BF16),
-        rows, devices,
-    )
-    ffn_out = offload_scatter(dot_nn(hidden, down_w).astype(BF16), place, devices)
-    layer_out = (mid + ffn_out).astype(BF16)[None]
-    down_part = dot_tn(hidden, cot).astype(BF16)
-    gate_up_part = jnp.concatenate(
-        [dot_tn(ffn_in, d_gate).astype(BF16), dot_tn(ffn_in, d_up).astype(BF16)], axis=1
-    )
-    down_grad = lane_scatter(rows_to_columns(down_part, devices)).astype(F32)
-    gate_up_grad = lane_scatter(gate_up_part).astype(F32)
-    gate_grad, up_grad = gate_up_grad[:, :hidden_width], gate_up_grad[:, hidden_width:]
-    d_ffn = after(d_ffn, gate_up_part, down_part)
+    x_pieces = gather_pieces(fill_lanes(mid * mid_factor * gain_ffn), devices)
+
+    carried = None
+    back_terms, ffn_terms = [], []
+    for first, count in row_halves(rows, devices):
+        some = slice(first // own_rows, (first + count) // own_rows)
+        x_some = x_pieces[some] if devices == CUBE else x_pieces
+        *carried, back_term, ffn_term = ffn(
+            order, x_some, cot, gate_w, up_w, down_wt, first, count, piece_rows, carried
+        )
+        back_terms.append(back_term)
+        ffn_terms.append(ffn_term)
+    ffn_in, cot_rows, hidden, d_gate, d_up = carried
+    back_mate = scatter_begin(back_terms[0], devices)
+    ffn_in = after(ffn_in, back_mate)
+    gate_part = dot_tn(ffn_in, d_gate).astype(BF16)
+    gate_grad = lane_scatter(gate_part)
+    d_ffn = after(scatter_end(back_terms[-1], back_mate, model, devices), gate_part)
 
     d_mid_norm, ffn_gain_part = norm_back(mid, mid_factor, gain_ffn, d_ffn)
     d_mid = cotangent[0].astype(F32) + d_mid_norm
     d_branch_own = d_mid.astype(BF16)
-    d_branch = rows_gather(d_branch_own, devices)
+    d_pieces = gather_pieces(fill_lanes(d_branch_own), devices)
+    up_part = dot_tn(ffn_in, after(d_up, d_branch_own)).astype(BF16)
+    up_grad = lane_scatter(up_part)
+    down_part = dot_tn(cot_rows, after(hidden, d_branch_own)).astype(BF16)
+    d_pieces[-1] = after(d_pieces[-1], up_part, down_part)
+    down_back = exchange(after(down_part, d_pieces[-1]).reshape(devices, model_part, -1))
+    ffn_mate = scatter_begin(ffn_terms[0], devices)
+    ffn_chip = scatter_chip(ffn_terms[-1], ffn_mate, devices)
     branch_f = d_branch_own.astype(F32)
     dots = jnp.stack(
         [
@@ -1114,55 +1470,82 @@
     spread_rows = jnp.transpose(spread_rows, (1, 0, 2)).reshape(4, rows)
     factors, shifts = spread_rows[:2], spread_rows[2:]
 
-    d_comb_attn = dot_nt(d_branch, out_w[:head_width])
-    d_comb_ssm = dot_nt(d_branch, out_w[head_width:])
+    d_branch, d_comb_attn, d_comb_ssm = branch(d_pieces, out_wt, head_width, piece_rows)
+    stat = jnp.transpose(pad_to(jnp.stack([factors[1], shifts[1]]), 128, 0))
+    d_z, x_part_grad, d_low, d_bc, step_grad, vec_grads, decay_sum = scan_backward(
+        slot, fixed, starts_int, d_comb_ssm, stat, y_total, z_gate, ssm_in, step_low, wide_bc,
+        states, last_states, step_w, bias, rate2, skip, gain_ssm, unit_rows,
+        (ffn_chip[0],),
+    )
+    d_bc = jnp.transpose(
+        d_bc[:, :, 0].reshape(units, 2, unit_rows, STATE), (0, 2, 1, 3)
+    ).reshape(rows, 2 * STATE)
+    ffn_near = scatter_links(ffn_chip, devices, (d_low,))
+    down_back = move_columns(
+        down_back, back(down_moves), lanes, w_down.shape[0], (ffn_near[0],)
+    )
+    down_grad = lax.psum_scatter(down_back, "fsdp", scatter_dimension=0, tiled=False)
+    d_select = whole_call(
+        join_kernel, [jax.ShapeDtypeStruct((rows, DT_RANK + 2 * STATE), BF16)],
+        d_low, d_bc.astype(BF16), deps=(down_back,),
+    )[0]
     attn_mixed = (attn * (0.5 * factors[0][:, None] * gain_attn)).astype(BF16)
     ssm_mixed = (ssm_comb.astype(F32) * (0.5 * factors[1][:, None])).astype(BF16)
-    out_part = dot_tn(jnp.concatenate([attn_mixed, ssm_mixed], axis=1), d_branch).astype(BF16)
-    out_back = rows_to_columns(out_part, devices).reshape(devices, -1, model_part)
-    out_grad = lane_scatter(
-        jnp.concatenate(
-            [
-                out_back[:, :head_width].reshape(-1, model_part)[:query_width],
-                out_back[:, head_width:].reshape(-1, model_part),
-            ],
-            axis=0,
-        )
-    ).astype(F32)
+    d_select = all_sum_core(d_select, devices)
+    mixed = after(jnp.concatenate([attn_mixed, ssm_mixed], axis=1), d_select)
+    out_part = dot_tn(d_branch, mixed).astype(BF16)
+    d_near = all_sum_near(d_select, devices)
+    d_near = lax.optimization_barrier(tuple(d_near) + (out_part,))[:-1]
+    d_far = all_sum_far(d_near, devices)
+    z_part_grad = dot_tn(normed, after(d_z, *d_near)).astype(BF16)
+    d_far = after(d_far, z_part_grad)
+    out_back = exchange(hold(out_part, d_far).reshape(devices, model_part, -1))
+    if devices == CUBE:
+        ffn_near = (ffn_near[0], hold(ffn_near[1], d_far), hold(ffn_near[2], d_far))
     half = 0.5 * d_comb_attn
     d_attn = factors[0][:, None] * (half * gain_attn) - attn * shifts[0][:, None]
     attn_gain_part = jnp.sum(half * attn * factors[0][:, None], axis=0)
-    stat = jnp.transpose(pad_to(jnp.stack([factors[1], shifts[1]]), 128, 0))
-    d_z, x_part_grad, d_low, d_bc, step_grad, vec_grads, decay_sum = scan_backward(
-        slot, fixed, starts_int, d_comb_ssm, stat, y_total, z_gate, ssm_in, step_low, wide_bc, states,
-        last_states, step_w, bias, rate2, skip, gain_ssm, unit_rows,
-    )
-    d_bc = jnp.transpose(
-        d_bc[:, :, 0].reshape(units, 2, unit_rows, STATE), (0, 2, 1, 3)
-    ).reshape(rows, 2 * STATE)
-    d_select = all_sum(jnp.concatenate([d_low, d_bc.astype(BF16)], axis=1), devices)
-    z_part_grad = dot_tn(normed, d_z).astype(BF16)
     d_query, d_keys, d_values = attn_backward(
-        slot, low_block, pair, queries, attn, d_attn.astype(BF16), attn_stat, keys,
-        jnp.transpose(keys), values, unit_rows,
-    )
-    d_qkv = jnp.concatenate([d_query, d_keys.astype(BF16), d_values.astype(BF16)], axis=1)
+        slot, low_block, pair, queries, attn, d_attn.astype(BF16), attn_stat,
+        keys, jnp.transpose(keys), values, unit_rows, (d_far, out_part),
+    )
+    out_back = move_columns(
+        out_back, back(out_moves), lanes, out_proj.shape[0], (d_query,)
+    )
+    layer_out = mid + scatter_far(ffn_near, model, devices, (out_back,))
+    d_qkv = whole_call(
+        join_qkv_kernel, [jax.ShapeDtypeStruct((rows, qkv_width), BF16)],
+        d_query, d_keys, d_values, deps=(layer_out,),
+    )[0]
+    layer_out = layer_out.astype(BF16)[None]
     qkv_part_grad = dot_tn(normed, d_qkv).astype(BF16)
-    d_select = after(d_select, z_part_grad, qkv_part_grad)
-    d_x, conv_grads, select_grad = conv_backward(
-        slot, fixed, starts_int, d_select, x_part_grad, conv_out, x_in, ssm_in, conv_w, sel_w,
-        unit_rows,
-    )
-    d_normed = rows_scatter(
-        lambda a, b: (
-            dot_nt(d_qkv[a:b], qkv_w) + dot_nt(d_x[a:b], x_w) + dot_nt(d_z[a:b], z_w)
-        ).astype(BF16),
-        rows, devices,
+    early = project(
+        [d_qkv, after(d_z, d_qkv)], [qkv_w, z_w], [(0, qkv_width), (0, width)], piece_rows,
+        False, None, (qkv_part_grad, z_part_grad),
+    )[0]
+    out_grad = lax.psum_scatter(
+        out_back, "fsdp", scatter_dimension=0, tiled=False
     )
     z_grad = lane_scatter(z_part_grad)
     in_grad = lane_scatter(qkv_part_grad)
-    x_grad = lane_scatter(dot_tn(normed, d_x).astype(BF16))
-    xz_grad = join_pairs(x_grad, z_grad, place, devices).astype(F32)
+    d_x, conv_grads, select_grad = conv_backward(
+        slot, fixed, starts_int, d_far, x_part_grad, conv_out, x_in, ssm_in, conv_w, sel_w, unit_rows,
+        (early, layer_out, out_back, down_back),
+    )
+    in_terms = project([d_x], [x_w], [(0, width)], piece_rows, cube, early)
+    in_mate = scatter_begin(in_terms[0], devices)
+    x_part_sum = dot_tn(after(normed, in_mate), d_x).astype(BF16)
+    in_chip = scatter_chip(in_terms[-1], in_mate, devices)
+    in_near = scatter_links(in_chip, devices)
+    d_normed = scatter_far(in_near, model, devices)
+    sums = (down_grad, out_grad, gate_grad, up_grad, z_grad, in_grad, conv_grads, select_grad)
+    sums += (step_grad, vec_grads, decay_sum)
+    sums = lax.optimization_barrier(sums + tuple(in_near))[: len(sums)]
+    down_grad, out_grad, gate_grad, up_grad, z_grad, in_grad, conv_grads, select_grad = sums[:8]
+    step_grad, vec_grads, decay_sum = sums[8:]
+    gate_grad, up_grad = gate_grad.astype(F32), up_grad.astype(F32)
+    x_grad = lane_scatter(x_part_sum)
+    in_grad = hold(in_grad, d_normed)
     spread = jnp.zeros((in_grad.shape[0], devices * head_width), BF16)
     spread = lax.dynamic_update_slice_in_dim(spread, in_grad[:, :head_width], place * head_width, 1)
     kv_zero = jnp.zeros((in_grad.shape[0], kv_room), BF16)
@@ -1222,6 +1605,12 @@
         ).astype(F32),
         axis=0,
     )
+    xz_grad = join_pairs(x_grad, z_grad, place, devices).astype(F32)
+    packed_low = packed.astype(BF16)
+    down_grad, out_grad = (
+        jnp.transpose(hold(part, packed_low).astype(F32)) for part in (down_grad, out_grad)
+    )
+    select_grad = hold(select_grad, packed_low)
     counts = [CONV, select_grad.shape[0], DT_RANK, STATE]
     local = jnp.concatenate(
         [

time: 1300 us -> 1100 us (0.85)
  Pallas kernels: 232 us -> 459 us
  local copies, waits for them, and re-layouts: 296 us -> 124 us
  matrix products: 215 us -> 89.4 us
  waiting for transfers between devices: 331 us -> 223 us
  other arithmetic: 81.4 us -> 60.4 us
    pallas_call x5 -> x52, Pallas kernels: 209 us -> 437 us  [the longest x22 82.2 us: whole_call(): pl.pallas_call(later(kernel, len(values), deps), out_shape=out_shape, in_...]
    dot_general x13 -> x0, matrix products: 92.6 us -> none  [dot_nt(): lax.dot_general(left, right, (((1,), (1,)), ((), ())), preferred_element_...]
    ppermute x24 -> x2, local copies, waits for them, and re-layouts: 58.4 us -> 2.54 us  [swap(): return lax.ppermute(value, 'ctx', [(d, d ^ mask) for d in range(CUBE)])]
    ppermute x90 -> x80, waiting for transfers between devices: 218 us -> 171 us  [swap(): return lax.ppermute(value, 'ctx', [(d, d ^ mask) for d in range(CUBE)])]
    dot_general x10 -> x3, matrix products: 70.2 us -> 25.8 us  [dot_nn(): lax.dot_general(left, right, (((1,), (0,)), ((), ())), preferred_element_...]
    all_to_all x4, waiting for transfers between devices: 36 us -> 0.01 us  [exchange(): lax.all_to_all(blocks, 'ctx', split_axis=0, concat_axis=0, tiled=True)]
    all_gather x5 -> x4, waiting for transfers between devices: 34.9 us -> 0.04 us  [lane_gather(): return lax.all_gather(value, 'fsdp', axis=0, tiled=True)]
    unnamed x278 -> x270, local copies, waits for them, and re-layouts: 82.6 us -> 48.3 us
  transfers between devices with their start and end apart: 122 -> 111, of which waited for: 55 -> 42; matrix products, arithmetic and copies ran while one was open for 42% -> 23% of each run, Pallas kernels for 18% -> 40%
where the time goes in v3:
time: 1100 us; the launch traced here: 1090 us
  Pallas kernels  459 us (42%)
  waiting for transfers between devices  223 us (20%)
  local copies, waits for them, and re-layouts  124 us (11%)
  starting transfers between devices  114 us (10%)
  matrix products  89.4 us (8%)
  other arithmetic  60.4 us (5%)
  between operations  15.8 us (1%)
    ppermute x80, waiting for transfers between devices, swap(): return lax.ppermute(value, 'ctx', [(d, d ^ mask) for d in range(CUBE)])  171 us
    pallas_call x22, Pallas kernels, whole_call(): pl.pallas_call(later(kernel, len(values), deps), out_shape=out_shape, in_...  82.2 us
    pallas_call x1, Pallas kernels, scan_backward(): pl.pallas_call(later(scan_kernel_bwd, 3 + 14, deps), out_shape=(jax.Shape...  74.9 us
    ppermute x80, starting transfers between devices, swap(): return lax.ppermute(value, 'ctx', [(d, d ^ mask) for d in range(CUBE)])  63.6 us
    dot_general x7, matrix products, dot_tn(): lax.dot_general(left, right, (((0,), (0,)), ((), ())), preferred_element_...  63.6 us
    pallas_call x2, Pallas kernels, ffn(): pl.pallas_call(functools.partial(ffn_kernel, count, model), out_shape=[ja...  54.1 us
    unnamed x270, local copies, waits for them, and re-layouts  48.3 us
    pallas_call x1, Pallas kernels, scan_forward(): pl.pallas_call(later(scan_kernel_fwd, 12, deps), out_shape=(jax.ShapeDtyp...  45.8 us
  transfers between devices with their start and end apart: 111, of which 42 were waited for; matrix products, arithmetic and copies ran while one was open for 23% of the time, Pallas kernels for 40%

profile of v3, /device:TPU:0, one launch (start us, length us, event | category | flops | bytes accessed | tf_op | source)
XLA Modules:
  0.0 1086.4 jit_solution(1705114821395380607)
XLA Ops:
  14.3 9.6 collective-permute-done.1
  62.7 9.5 collective-permute-done.14
  87.8 9.2 shard_map.367.refs_1_
  102.5 8.8 convolution_convert_fusion.9.xin_ref.refs_6_
  111.3 13.2 %shard_map.370 = (f32[2048,400]{1,0:T(8,128)}, bf16[2048,400]{1,0:T(8,128)(2,1)}, bf16[2048,132]{1,0:T(8,128)(2,1)}) custom-call(s32[16]{0:T(128)} %copy-done.86, s32[16]{0:T(128)} %copy-done.96, s32[16]{0:T(128)} %copy-done.88, bf16[2048,400]{1,0:T(8,128)(2,1)} %convolution_convert_fusion.9.xin_ref.refs_6_, f32[4,400]{1,0:T(4,128)} %fusion.6.w_ref.refs_8_, ...), custom_call_target="tpu_custom_call" | custom-call | flops 1 | bytes 1 | tf_op jit(solution)/shard_map/pallas_call | solution.py:163
  132.7 8.4 convolution_convert_fusion.8.refs_4_.refs_6_
  168.1 11.7 %collective-permute-done.24 = bf16[1024,132]{1,0:T(8,128)(2,1)S(1)} collective-permute-done((bf16[1024,132]{1,0:T(8,128)(2,1)S(1)}, bf16[1024,132]{1,0:T(8,128)(2,1)S(1)}, u32[]{:S(2)}, u32[]{:S(2)}) %collective-permute-start.24) | collective-permute-done | bytes 270368 | tf_op jit(solution)/shard_map/ppermute | solution.py:1036
  203.6 45.8 %shard_map.378 = (f32[2048,400]{1,0:T(8,128)}, bf16[2048,400]{1,0:T(8,128)(2,1)}, f32[2048,128]{1,0:T(8,128)}, f32[16,128,32,128]{3,2,1,0:T(8,128)}, f32[16,128,...) custom-call(s32[16]{0:T(128)} %copy-done.86, s32[16]{0:T(128)} %copy-done.96, s32[16]{0:T(128)} %copy-done.88, ...), custom_call_target="tpu_custom_call" | custom-call | flops 1 | bytes 1 | tf_op jit(solution)/shard_map/pallas_call | solution.py:356
  250.9 10.5 shard_map.379
  261.8 8.7 convolution_convert_fusion.7.refs_2_
  270.5 5.6 shard_map.380
  295.2 30.0 %shard_map.382 = (f32[2048,256]{1,0:T(8,128)}, bf16[2048,256]{1,0:T(8,128)(2,1)}, f32[16,8,512]{2,1,0:T(8,128)}) custom-call(s32[16]{0:T(128)} %copy-done.86, s32[16]{0:T(128)} %and_select_fusion.1.refs_1_, s32[4]{0:T(128)} %subtract_clamp_fusion.refs_2_, bf16[2048,256]{1,0:T(8,128)(2,1)} %slice.326.refs_3_, ...), custom_call_target="tpu_custom_call" | custom-call | flops 1 | bytes 1 | tf_op jit(solution)/shard_map/pallas_call | solution.py:636
  325.2 6.4 collective-permute-done.33.refs_3_
  337.1 9.3 shard_map.384
  346.4 6.4 collective-permute-done.35.mate
  352.7 5.6 shard_map.385
  365.6 14.1 %collective-permute-done.26 = f32[2,256]{1,0:T(2,128)S(1)} collective-permute-done((f32[2,256]{1,0:T(2,128)S(1)}, f32[2,256]{1,0:T(2,128)S(1)}, u32[]{:S(2)}, u32[]{:S(2)}) %collective-permute-start.26) | collective-permute-done | bytes 2080 | tf_op jit(solution)/shard_map/ppermute | solution.py:1036
  392.0 12.2 %collective-permute-done.40.by_y = bf16[128,1664]{1,0:T(8,128)(2,1)S(1)} collective-permute-done((bf16[128,1664]{1,0:T(8,128)(2,1)S(1)}, bf16[128,1664]{1,0:T(8,128)(2,1)S(1)}, u32[]{:S(2)}, u32[]{:S(2)}) %collective-permute-start.40) | collective-permute-done | bytes 426016 | tf_op jit(solution)/shard_map/ppermute | solution.py:1036
  408.7 12.5 %collective-permute-done.38.by_y = bf16[128,1664]{1,0:T(8,128)(2,1)S(1)} collective-permute-done((bf16[128,1664]{1,0:T(8,128)(2,1)}, bf16[128,1664]{1,0:T(8,128)(2,1)S(1)}, u32[]{:S(2)}, u32[]{:S(2)}) %collective-permute-start.38) | collective-permute-done | bytes 426016 | tf_op jit(solution)/shard_map/ppermute | solution.py:1036
  429.9 19.4 %collective-permute-done.42.by_x.refs_1_ = bf16[256,1664]{1,0:T(8,128)(2,1)S(1)} collective-permute-done((bf16[256,1664]{1,0:T(8,128)(2,1)S(1)}, bf16[256,1664]{1,0:T(8,128)(2,1)S(1)}, u32[]{:S(2)}, u32[]{:S(2)}) %collective-permute-start.42) | collective-permute-done | bytes 852000 | tf_op jit(solution)/shard_map/ppermute | solution.py:1036
  456.0 9.1 collective-permute-done.44
  468.9 26.8 %shard_map.390 = (bf16[2048,1600]{1,0:T(8,128)(2,1)}, bf16[2048,1600]{1,0:T(8,128)(2,1)}, bf16[2048,688]{1,0:T(8,128)(2,1)}, bf16[2048,688]{1,0:T(8,128)(2,1)}, ...) custom-call(s32[8]{0:T(128)} %broadcast_xor_fusion.order, ...), custom_call_target="tpu_custom_call" | custom-call | flops 1 | bytes 1 | tf_op jit(solution)/shard_map/pallas_call | solution.py:977
  496.3 27.3 %shard_map.391 = (bf16[2048,1600]{1,0:T(8,128)(2,1)}, bf16[2048,1600]{1,0:T(8,128)(2,1)}, bf16[2048,688]{1,0:T(8,128)(2,1)}, bf16[2048,688]{1,0:T(8,128)(2,1)}, ...) custom-call(s32[8]{0:T(128)} %broadcast_xor_fusion.order, ...), custom_call_target="tpu_custom_call", output_to_operand_aliasing={{0}: (9, {}), {1}: (10, {}), {2}: (11, {}), {3}: (12, {}), ... | custom-call | flops 1 | bytes 1 | tf_op jit(solution)/shard_map/pallas_call | solution.py:977
  523.6 5.5 shard_map.393
  532.4 5.5 shard_map.392
  540.5 10.6 collective-permute-done.54.by_x
  558.8 9.6 convolution_convert_fusion.3
  589.6 10.1 convolution_convert_fusion.2
  599.7 7.2 collective-permute-done.58.by_x.refs_1_
  611.7 10.1 convolution_convert_fusion.1
  650.4 12.7 %shard_map.397 = (bf16[2048,1600]{1,0:T(8,128)(2,1)}, f32[2048,256]{1,0:T(8,128)}, f32[2048,400]{1,0:T(8,128)}) custom-call(bf16[256,1664]{1,0:T(8,128)(2,1)} %pad.21.refs_0_, bf16[256,1664]{1,0:T(8,128)(2,1)} %collective-permute-done.58.by_x.refs_1_, bf16[256,1664]{1,0:T(8,128)(2,1)} %collective-permute-done.59.by_y.refs_2_, bf16[256,1664]{1,0:T(8,128)(2,1)} %copy-done.46, ...), custom_call_target="tpu_custom_call" | custom-call | flops 1 | bytes 1 | tf_op jit(solution)/shard_map/pallas_call | solution.py:1011
  663.2 74.9 %shard_map.398 = (bf16[2048,400]{1,0:T(8,128)(2,1)}, f32[2048,400]{1,0:T(8,128)}, bf16[2048,100]{1,0:T(8,128)(2,1)}, f32[16,2,8,2048]{3,2,1,0:T(8,128)}, f32[100...) custom-call(s32[16]{0:T(128)} %copy-done.86, s32[16]{0:T(128)} %copy-done.96, s32[16]{0:T(128)} %copy-done.88, ...), custom_call_target="tpu_custom_call" | custom-call | flops 1 | bytes 1 | tf_op jit(solution)/shard_map/pallas_call | solution.py:510
  766.4 9.8 convolution_convert_fusion.refs_0_.refs_11_
  782.1 7.8 convolution_convert_fusion.6.refs_5_
  793.5 10.4 collective-permute-done.76
  822.1 32.6 %shard_map.406 = (bf16[2048,256]{1,0:T(8,128)(2,1)}, f32[2048,128]{1,0:T(8,128)}, f32[2048,128]{1,0:T(8,128)}) custom-call(s32[16]{0:T(128)} %copy-done.86, s32[16]{0:T(128)} %and_select_fusion.1.refs_1_, s32[4]{0:T(128)} %subtract_clamp_fusion.refs_2_, bf16[2048,256]{1,0:T(8,128)(2,1)} %slice.326.refs_3_, f32[2048,256]{1,0:T(8,128)} %get-tuple-element.224.refs_4_, ...), custom_call_target="tpu_custom_call" | custom-call | flops 1 | bytes 1 | tf_op jit(solution)/shard_map/pallas_call | solution.py:716
  869.3 8.4 convolution_convert_fusion.5.refs_4_
  882.3 12.9 %shard_map.410.refs_10_.refs_2_ = bf16[2048,1664]{1,0:T(8,128)(2,1)} custom-call(bf16[2048,512]{1,0:T(8,128)(2,1)} %shard_map.409.refs_0_, bf16[2048,400]{1,0:T(8,128)(2,1)} %get-tuple-element.238.refs_1_, bf16[1600,512]{1,0:T(8,128)(2,1)} %all-gather.15.cloned.1.call-done.refs_2_, bf16[1600,400]{1,0:T(8,128)(2,1)} %get-tuple-element.362.refs_3_, ...), custom_call_target="tpu_custom_call" | custom-call | flops 1 | bytes 1 | tf_op jit(solution)/shard_map/pallas_call | solution.py:925
  895.2 17.4 %shard_map.411 = (bf16[2048,400]{1,0:T(8,128)(2,1)}, f32[8,400]{1,0:T(8,128)}, f32[132,400]{1,0:T(8,128)}) custom-call(s32[16]{0:T(128)} %copy-done.86, s32[16]{0:T(128)} %copy-done.96, s32[16]{0:T(128)} %copy-done.88, bf16[2048,132]{1,0:T(8,128)(2,1)} %pad_maximum_fusion.3.refs_1_.refs_10_.refs_3_, f32[2048,400]{1,0:T(8,128)} %get-tuple-element.234.refs_4_, ...), custom_call_target="tpu_custom_call" | custom-call | flops 1 | bytes 1 | tf_op jit(solution)/shard_map/pallas_call | solution.py:228
  912.7 11.7 %shard_map.412 = (bf16[1024,1664]{1,0:T(8,128)(2,1)}, bf16[1024,1664]{1,0:T(8,128)(2,1)}) custom-call(bf16[2048,400]{1,0:T(8,128)(2,1)} %get-tuple-element.239.refs_0_, bf16[1600,400]{1,0:T(8,128)(2,1)} %get-tuple-element.361.refs_1_, bf16[2048,1664]{1,0:T(8,128)(2,1)} %shard_map.410.refs_10_.refs_2_), custom_call_target="tpu_custom_call" | custom-call | flops 1 | bytes 1 | tf_op jit(solution)/shard_map/pallas_call | solution.py:925
  924.7 6.1 collective-permute-done.80.mate
  930.8 5.6 shard_map.413
  950.6 7.1 collective-permute-done.81.by_x
  964.1 7.8 convolution_convert_fusion.4
  994.7 9.8 all-to-all-start.4
  1030.2 6.9 collective-permute-done.88
  1048.0 20.4 %collective-permute-done.86 = bf16[400,400]{1,0:T(8,128)(2,1)S(1)} collective-permute-done((bf16[400,400]{1,0:T(8,128)(2,1)S(1)}, bf16[400,400]{1,0:T(8,128)(2,1)S(1)}, u32[]{:S(2)}, u32[]{:S(2)}) %collective-permute-start.86) | collective-permute-done | bytes 320032 | tf_op jit(solution)/shard_map/ppermute | solution.py:1230
  1069.7 8.0 reduce-scatter.21.cloned.1.call-done
  (705 shorter events, 421.4 us)
Async XLA Ops:
  7.2 95.3 %all-gather.13.cloned.1.call-start = ((), (), s32[]{:S(2)}) async-start(), calls=%async_computation.13 | async-start | bytes 3584000 | tf_op jit(solution)/shard_map/all_gather | solution.py:1173
  25.2 124.4 %all-gather.27.cloned.1.call-start = ((), (), s32[]{:S(2)}) async-start(), calls=%async_computation.25 | async-start | bytes 2580480 | tf_op jit(solution)/shard_map/all_gather | solution.py:1335
  29.1 25.8 %collective-permute-start.12 = (bf16[256,1664]{1,0:T(8,128)(2,1)}, bf16[256,1664]{1,0:T(8,128)(2,1)S(1)}, u32[]{:S(2)}, u32[]{:S(2)}) collective-permute-start(bf16[256,1664]{1,0:T(8,128)(2,1)} %pad.18.refs_0_), channel_id=1, source_target_pairs={{0,8},{4,12},{8,0},{12,4},{16,24},{20,28},{24,16},{28,20},{1,9},{5... | collective-permute-start | bytes 2555912 | tf_op jit(solution)/shard_map/ppermute | solution.py:1036
  30.9 26.0 %collective-permute-start.13 = (bf16[256,1664]{1,0:T(8,128)(2,1)}, bf16[256,1664]{1,0:T(8,128)(2,1)S(1)}, u32[]{:S(2)}, u32[]{:S(2)}) collective-permute-start(bf16[256,1664]{1,0:T(8,128)(2,1)} %pad.18.refs_0_), channel_id=1, source_target_pairs={{0,16},{4,20},{8,24},{12,28},{16,0},{20,4},{24,8},{28,12},{1,17},{... | collective-permute-start | bytes 2555912 | tf_op jit(solution)/shard_map/ppermute | solution.py:1036
  39.6 48.1 %collective-permute-start.16 = (bf16[256,1664]{1,0:T(8,128)(2,1)}, bf16[256,1664]{1,0:T(8,128)(2,1)}, u32[]{:S(2)}, u32[]{:S(2)}) collective-permute-start(bf16[256,1664]{1,0:T(8,128)(2,1)} %pad.18.refs_0_), channel_id=1, source_target_pairs={{0,4},{4,0},{8,12},{12,8},{16,20},{20,16},{24,28},{28,24},{1,5},{5... | collective-permute-start | bytes 2555912 | tf_op jit(solution)/shard_map/ppermute | solution.py:1036
  100.6 82.5 %all-gather.23.cloned.1.call-start = ((), (), s32[]{:S(2)}) async-start(), calls=%async_computation.23 | async-start | bytes 2560000 | tf_op jit(solution)/shard_map/all_gather | solution.py:1325
  102.1 159.7 %all-gather.15.cloned.1.call-start = ((), (), s32[]{:S(2)}) async-start(), calls=%async_computation.14 | async-start | bytes 2048000 | tf_op jit(solution)/shard_map/all_gather | solution.py:1173
  156.8 119.3 %all-gather.25.cloned.1.call-start = ((), (), s32[]{:S(2)}) async-start(), calls=%async_computation.24 | async-start | bytes 2816000 | tf_op jit(solution)/shard_map/all_gather | solution.py:1371
  162.3 304.8 %all-gather.21.cloned.1.call-start = ((), (), s32[]{:S(2)}) async-start(), calls=%async_computation.17 | async-start | bytes 3072000 | tf_op jit(solution)/shard_map/all_gather | solution.py:1173
  186.6 62.8 %all-to-all-start = ((bf16[8,200,656]{2,1,0:T(8,128)(2,1)}), bf16[8,200,656]{2,1,0:T(8,128)(2,1)S(1)}, u32[]{:S(2)}, u32[]{:S(2)}) async-start(bf16[8,200,656]{2,1,0:T(8,128)(2,1)} %shard_map.373.refs_12_), calls=%async_computation | async-start | bytes 4915200 | tf_op jit(solution)/shard_map/all_to_all | solution.py:1119
  190.4 276.7 %all-gather.19.cloned.1.call-start = ((), (), s32[]{:S(2)}) async-start(), calls=%async_computation.16 | async-start | bytes 3072000 | tf_op jit(solution)/shard_map/all_gather | solution.py:1173
  191.1 275.9 %all-gather.17.cloned.1.call-start = ((), (), s32[]{:S(2)}) async-start(), calls=%async_computation.15 | async-start | bytes 7667712 | tf_op jit(solution)/shard_map/all_gather | solution.py:1369
  279.6 56.0 %all-to-all-start.1 = ((bf16[8,200,688]{2,1,0:T(8,128)(2,1)}), bf16[8,200,688]{2,1,0:T(8,128)(2,1)S(1)}, u32[]{:S(2)}, u32[]{:S(2)}) async-start(bf16[8,200,688]{2,1,0:T(8,128)(2,1)} %shard_map.381.refs_8_), calls=%async_computation.1 | async-start | bytes 4915200 | tf_op jit(solution)/shard_map/all_to_all | solution.py:1119
  283.6 661.4 %reduce-scatter.25.cloned.1.call-start = ((), (), s32[]{:S(2)}) async-start(), calls=%async_computation.26 | async-start | bytes 3072000
  284.1 47.6 %collective-permute-start.33 = (bf16[256,1664]{1,0:T(8,128)(2,1)}, bf16[256,1664]{1,0:T(8,128)(2,1)}, u32[]{:S(2)}, u32[]{:S(2)}) collective-permute-start(bf16[256,1664]{1,0:T(8,128)(2,1)} %get-tuple-element.160), channel_id=1, source_target_pairs={{0,8},{4,12},{8,0},{12,4},{16,24},{20,28},{24,16},{28,20},{1,9},{5... | collective-permute-start | bytes 2555912 | tf_op jit(solution)/shard_map/ppermute | solution.py:1036
  286.1 45.5 %collective-permute-start.34 = (bf16[256,1664]{1,0:T(8,128)(2,1)}, bf16[256,1664]{1,0:T(8,128)(2,1)}, u32[]{:S(2)}, u32[]{:S(2)}) collective-permute-start(bf16[256,1664]{1,0:T(8,128)(2,1)} %get-tuple-element.161), channel_id=1, source_target_pairs={{0,16},{4,20},{8,24},{12,28},{16,0},{20,4},{24,8},{28,12},{1,17},{... | collective-permute-start | bytes 2555912 | tf_op jit(solution)/shard_map/ppermute | solution.py:1036
  358.4 22.8 %collective-permute-start.36 = (bf16[256,1664]{1,0:T(8,128)(2,1)}, bf16[256,1664]{1,0:T(8,128)(2,1)S(1)}, u32[]{:S(2)}, u32[]{:S(2)}) collective-permute-start(bf16[256,1664]{1,0:T(8,128)(2,1)} %get-tuple-element.168), channel_id=1, source_target_pairs={{0,8},{4,12},{8,0},{12,4},{16,24},{20,28},{24,16},{28,20},{1,9},{5... | collective-permute-start | bytes 2555912 | tf_op jit(solution)/shard_map/ppermute | solution.py:1036
  359.7 22.9 %collective-permute-start.37 = (bf16[256,1664]{1,0:T(8,128)(2,1)}, bf16[256,1664]{1,0:T(8,128)(2,1)S(1)}, u32[]{:S(2)}, u32[]{:S(2)}) collective-permute-start(bf16[256,1664]{1,0:T(8,128)(2,1)} %get-tuple-element.169), channel_id=1, source_target_pairs={{0,16},{4,20},{8,24},{12,28},{16,0},{20,4},{24,8},{28,12},{1,17},{... | collective-permute-start | bytes 2555912 | tf_op jit(solution)/shard_map/ppermute | solution.py:1036
  364.1 23.7 %collective-permute-start.28 = (f32[2,256]{1,0:T(2,128)S(1)}, f32[2,256]{1,0:T(2,128)S(1)}, u32[]{:S(2)}, u32[]{:S(2)}) collective-permute-start(f32[2,256]{1,0:T(2,128)S(1)} %bitcast.279), channel_id=1, source_target_pairs={{0,24},{4,28},{8,16},{12,20},{16,8},{20,12},{24,0},{28,4},{1,25},{... | collective-permute-start | bytes 6152 | tf_op jit(solution)/shard_map/ppermute | solution.py:1036
  390.1 31.2 %collective-permute-start.38 = (bf16[128,1664]{1,0:T(8,128)(2,1)}, bf16[128,1664]{1,0:T(8,128)(2,1)S(1)}, u32[]{:S(2)}, u32[]{:S(2)}) collective-permute-start(bf16[128,1664]{1,0:T(8,128)(2,1)} %get-tuple-element.171), channel_id=1, source_target_pairs={{0,16},{4,20},{8,24},{12,28},{16,0},{20,4},{24,8},{28,12},{1,17},{... | collective-permute-start | bytes 1277960 | tf_op jit(solution)/shard_map/ppermute | solution.py:1036
  391.1 30.1 %collective-permute-start.39 = (bf16[128,1664]{1,0:T(8,128)(2,1)}, bf16[128,1664]{1,0:T(8,128)(2,1)S(1)}, u32[]{:S(2)}, u32[]{:S(2)}) collective-permute-start(bf16[128,1664]{1,0:T(8,128)(2,1)} %get-tuple-element.172), channel_id=1, source_target_pairs={{0,8},{4,12},{8,0},{12,4},{16,24},{20,28},{24,16},{28,20},{1,9},{5... | collective-permute-start | bytes 1277960 | tf_op jit(solution)/shard_map/ppermute | solution.py:1036
  427.8 21.5 %collective-permute-start.42 = (bf16[256,1664]{1,0:T(8,128)(2,1)S(1)}, bf16[256,1664]{1,0:T(8,128)(2,1)S(1)}, u32[]{:S(2)}, u32[]{:S(2)}) collective-permute-start(bf16[256,1664]{1,0:T(8,128)(2,1)S(1)} %pad.20.refs_0_), channel_id=1, source_target_pairs={{0,8},{4,12},{8,0},{12,4},{16,24},{20,28},{24,16},{28,20},{1,9},{5... | collective-permute-start | bytes 2555912 | tf_op jit(solution)/shard_map/ppermute | solution.py:1036
  429.4 20.4 %collective-permute-start.43 = (bf16[256,1664]{1,0:T(8,128)(2,1)S(1)}, bf16[256,1664]{1,0:T(8,128)(2,1)S(1)}, u32[]{:S(2)}, u32[]{:S(2)}) collective-permute-start(bf16[256,1664]{1,0:T(8,128)(2,1)S(1)} %pad.20.refs_0_), channel_id=1, source_target_pairs={{0,16},{4,20},{8,24},{12,28},{16,0},{20,4},{24,8},{28,12},{1,17},{... | collective-permute-start | bytes 2555912 | tf_op jit(solution)/shard_map/ppermute | solution.py:1036
  495.8 27.8 %collective-permute-start.53 = (bf16[1024,1664]{1,0:T(8,128)(2,1)}, bf16[1024,1664]{1,0:T(8,128)(2,1)}, u32[]{:S(2)}, u32[]{:S(2)}) collective-permute-start(bf16[1024,1664]{1,0:T(8,128)(2,1)} %get-tuple-element.190), channel_id=1, source_target_pairs={{0,4},{4,0},{8,12},{12,8},{16,20},{20,16},{24,28},{28,24},{1,5},{5... | collective-permute-start | bytes 10223624 | tf_op jit(solution)/shard_map/ppermute | solution.py:1036
  496.0 34.6 %collective-permute-start.50 = (bf16[1024,1664]{1,0:T(8,128)(2,1)}, bf16[1024,1664]{1,0:T(8,128)(2,1)S(1)}, u32[]{:S(2)}, u32[]{:S(2)}) collective-permute-start(bf16[1024,1664]{1,0:T(8,128)(2,1)} %get-tuple-element.183), channel_id=1, source_target_pairs={{0,4},{4,0},{8,12},{12,8},{16,20},{20,16},{24,28},{28,24},{1,5},{5... | collective-permute-start | bytes 10223624 | tf_op jit(solution)/shard_map/ppermute | solution.py:1036
  529.2 22.0 %collective-permute-start.54 = (bf16[256,1664]{1,0:T(8,128)(2,1)}, bf16[256,1664]{1,0:T(8,128)(2,1)S(1)}, u32[]{:S(2)}, u32[]{:S(2)}) collective-permute-start(bf16[256,1664]{1,0:T(8,128)(2,1)} %get-tuple-element.194), channel_id=1, source_target_pairs={{0,8},{4,12},{8,0},{12,4},{16,24},{20,28},{24,16},{28,20},{1,9},{5... | collective-permute-start | bytes 2555912 | tf_op jit(solution)/shard_map/ppermute | solution.py:1036
  529.8 22.0 %collective-permute-start.55 = (bf16[256,1664]{1,0:T(8,128)(2,1)}, bf16[256,1664]{1,0:T(8,128)(2,1)S(1)}, u32[]{:S(2)}, u32[]{:S(2)}) collective-permute-start(bf16[256,1664]{1,0:T(8,128)(2,1)} %get-tuple-element.195), channel_id=1, source_target_pairs={{0,16},{4,20},{8,24},{12,28},{16,0},{20,4},{24,8},{28,12},{1,17},{... | collective-permute-start | bytes 2555912 | tf_op jit(solution)/shard_map/ppermute | solution.py:1036
  537.9 200.1 %collective-permute-start.51 = (bf16[256,1664]{1,0:T(8,128)(2,1)}, bf16[256,1664]{1,0:T(8,128)(2,1)}, u32[]{:S(2)}, u32[]{:S(2)}) collective-permute-start(bf16[256,1664]{1,0:T(8,128)(2,1)} %get-tuple-element.187), channel_id=1, source_target_pairs={{0,8},{4,12},{8,0},{12,4},{16,24},{20,28},{24,16},{28,20},{1,9},{5... | collective-permute-start | bytes 2555912 | tf_op jit(solution)/shard_map/ppermute | solution.py:1036
  539.0 199.0 %collective-permute-start.52 = (bf16[256,1664]{1,0:T(8,128)(2,1)}, bf16[256,1664]{1,0:T(8,128)(2,1)}, u32[]{:S(2)}, u32[]{:S(2)}) collective-permute-start(bf16[256,1664]{1,0:T(8,128)(2,1)} %get-tuple-element.188), channel_id=1, source_target_pairs={{0,16},{4,20},{8,24},{12,28},{16,0},{20,4},{24,8},{28,12},{1,17},{... | collective-permute-start | bytes 2555912 | tf_op jit(solution)/shard_map/ppermute | solution.py:1036
  556.8 21.2 %collective-permute-start.56 = (bf16[128,1664]{1,0:T(8,128)(2,1)}, bf16[128,1664]{1,0:T(8,128)(2,1)S(1)}, u32[]{:S(2)}, u32[]{:S(2)}) collective-permute-start(bf16[128,1664]{1,0:T(8,128)(2,1)} %get-tuple-element.197), channel_id=1, source_target_pairs={{0,16},{4,20},{8,24},{12,28},{16,0},{20,4},{24,8},{28,12},{1,17},{... | collective-permute-start | bytes 1277960 | tf_op jit(solution)/shard_map/ppermute | solution.py:1036
  557.7 20.4 %collective-permute-start.57 = (bf16[128,1664]{1,0:T(8,128)(2,1)}, bf16[128,1664]{1,0:T(8,128)(2,1)S(1)}, u32[]{:S(2)}, u32[]{:S(2)}) collective-permute-start(bf16[128,1664]{1,0:T(8,128)(2,1)} %get-tuple-element.198), channel_id=1, source_target_pairs={{0,8},{4,12},{8,0},{12,4},{16,24},{20,28},{24,16},{28,20},{1,9},{5... | collective-permute-start | bytes 1277960 | tf_op jit(solution)/shard_map/ppermute | solution.py:1036
  572.9 374.3 %reduce-scatter.27.cloned.1.call-start = ((), (), s32[]{:S(2)}) async-start(), calls=%async_computation.27 | async-start | bytes 3072000
  588.7 40.5 %collective-permute-start.66 = (f32[4,256]{1,0:T(4,128)S(1)}, f32[4,256]{1,0:T(4,128)S(1)}, u32[]{:S(2)}, u32[]{:S(2)}) collective-permute-start(f32[4,256]{1,0:T(4,128)S(1)} %pad_maximum_fusion.8), channel_id=1, source_target_pairs={{0,8},{4,12},{8,0},{12,4},{16,24},{20,28},{24,16},{28,20},{1,9},{5... | collective-permute-start | bytes 12296 | tf_op jit(solution)/shard_map/ppermute | solution.py:1036
  640.3 105.9 %all-to-all-start.2 = ((bf16[8,200,688]{2,1,0:T(8,128)(2,1)}), bf16[8,200,688]{2,1,0:T(8,128)(2,1)}, u32[]{:S(2)}, u32[]{:S(2)}) async-start(bf16[8,200,688]{2,1,0:T(8,128)(2,1)} %bitcast.235), calls=%async_computation.2 | async-start | bytes 4915200 | tf_op jit(solution)/shard_map/all_to_all | solution.py:1119
  644.7 327.3 %reduce-scatter.17.cloned.1.call-start = ((), (), s32[]{:S(2)}) async-start(), calls=%async_computation.19 | async-start | bytes 2048000 | tf_op jit(solution)/shard_map/reduce_scatter | solution.py:1177
  790.0 182.1 %reduce-scatter.29.cloned.1.call-start = ((), (), s32[]{:S(2)}) async-start(), calls=%async_computation.28 | async-start | bytes 2816000
  809.7 45.1 %all-to-all-start.3 = ((bf16[8,200,656]{2,1,0:T(8,128)(2,1)}), bf16[8,200,656]{2,1,0:T(8,128)(2,1)}, u32[]{:S(2)}, u32[]{:S(2)}) async-start(bf16[8,200,656]{2,1,0:T(8,128)(2,1)} %bitcast.236), calls=%async_computation.3 | async-start | bytes 4915200 | tf_op jit(solution)/shard_map/all_to_all | solution.py:1119
  814.1 158.0 %reduce-scatter.19.cloned.1.call-start = ((), (), s32[]{:S(2)}) async-start(), calls=%async_computation.20 | async-start | bytes 2048000 | tf_op jit(solution)/shard_map/reduce_scatter | solution.py:1177
  816.0 42.3 %collective-permute-start.79 = (bf16[128,1664]{1,0:T(8,128)(2,1)}, bf16[128,1664]{1,0:T(8,128)(2,1)S(1)}, u32[]{:S(2)}, u32[]{:S(2)}) collective-permute-start(bf16[128,1664]{1,0:T(8,128)(2,1)} %shard_map.404), channel_id=1, source_target_pairs={{0,8},{4,12},{8,0},{12,4},{16,24},{20,28},{24,16},{28,20},{1,9},{5... | collective-permute-start | bytes 1277960 | tf_op jit(solution)/shard_map/ppermute | solution.py:1036
  819.6 38.6 %collective-permute-start.78 = (bf16[128,1664]{1,0:T(8,128)(2,1)}, bf16[128,1664]{1,0:T(8,128)(2,1)S(1)}, u32[]{:S(2)}, u32[]{:S(2)}) collective-permute-start(bf16[128,1664]{1,0:T(8,128)(2,1)} %shard_map.403), channel_id=1, source_target_pairs={{0,16},{4,20},{8,24},{12,28},{16,0},{20,4},{24,8},{28,12},{1,17},{... | collective-permute-start | bytes 1277960 | tf_op jit(solution)/shard_map/ppermute | solution.py:1036
  877.7 95.2 %reduce-scatter.15.cloned.1.call-start = ((), (), s32[]{:S(2)}) async-start(), calls=%async_computation.18 | async-start | bytes 2560000 | tf_op jit(solution)/shard_map/reduce_scatter | solution.py:1526
  924.4 116.3 %reduce-scatter.23.cloned.1.call-start = ((), (), s32[]{:S(2)}) async-start(), calls=%async_computation.22 | async-start | bytes 2048000 | tf_op jit(solution)/shard_map/reduce_scatter | solution.py:1177
  936.4 21.3 %collective-permute-start.81 = (bf16[256,1664]{1,0:T(8,128)(2,1)}, bf16[256,1664]{1,0:T(8,128)(2,1)}, u32[]{:S(2)}, u32[]{:S(2)}) collective-permute-start(bf16[256,1664]{1,0:T(8,128)(2,1)} %get-tuple-element.245), channel_id=1, source_target_pairs={{0,8},{4,12},{8,0},{12,4},{16,24},{20,28},{24,16},{28,20},{1,9},{5... | collective-permute-start | bytes 2555912 | tf_op jit(solution)/shard_map/ppermute | solution.py:1036
  936.9 21.0 %collective-permute-start.82 = (bf16[256,1664]{1,0:T(8,128)(2,1)}, bf16[256,1664]{1,0:T(8,128)(2,1)}, u32[]{:S(2)}, u32[]{:S(2)}) collective-permute-start(bf16[256,1664]{1,0:T(8,128)(2,1)} %get-tuple-element.246), channel_id=1, source_target_pairs={{0,16},{4,20},{8,24},{12,28},{16,0},{20,4},{24,8},{28,12},{1,17},{... | collective-permute-start | bytes 2555912 | tf_op jit(solution)/shard_map/ppermute | solution.py:1036
  994.7 51.9 %all-to-all-start.4 = ((bf16[32,35,200]{2,1,0:T(8,128)(2,1)}), bf16[32,35,200]{2,1,0:T(8,128)(2,1)S(1)}, u32[]{:S(2)}, u32[]{:S(2)}) async-start(bf16[32,35,200]{2,1,0:T(8,128)(2,1)} %bitcast.76.refs_1_), calls=%async_computation.4 | async-start | bytes 1310720 | tf_op jit(solution)/shard_map/all_to_all | solution.py:1603
  1004.5 73.2 %reduce-scatter.21.cloned.1.call-start = ((), (), s32[]{:S(2)}) async-start(), calls=%async_computation.21 | async-start | bytes 2580480 | tf_op jit(solution)/shard_map/reduce_scatter | solution.py:1568
  1014.3 22.8 %collective-permute-start.88 = (f32[66,400]{1,0:T(8,128)}, f32[66,400]{1,0:T(8,128)}, u32[]{:S(2)}, u32[]{:S(2)}) collective-permute-start(f32[66,400]{1,0:T(8,128)} %get-tuple-element.385), channel_id=1, source_target_pairs={{0,2},{1,3},{2,0},{3,1},{4,6},{5,7},{6,4},{7,5},{8,10},{9,11},{10,... | collective-permute-start | bytes 316808 | tf_op jit(solution)/shard_map/ppermute | solution.py:1181
  1042.4 25.9 %collective-permute-start.86 = (bf16[400,400]{1,0:T(8,128)(2,1)S(1)}, bf16[400,400]{1,0:T(8,128)(2,1)S(1)}, u32[]{:S(2)}, u32[]{:S(2)}) collective-permute-start(bf16[400,400]{1,0:T(8,128)(2,1)S(1)} %get-tuple-element.378), channel_id=1, source_target_pairs={{4,0},{12,4},{20,8},{28,12},{0,16},{8,20},{16,24},{24,28},{5,1},{1... | collective-permute-start | bytes 960008 | tf_op jit(solution)/shard_map/ppermute | solution.py:1230
  (181 other events, 2250.8 us)
Sparse Core Ops, SparseCore 0:
  25.3 64.4 all-gather.12
  100.7 32.3 all-gather.26
  134.7 44.9 all-gather.22
  181.1 36.9 all-gather.14
  220.1 47.5 all-gather.24
  269.7 50.9 all-gather.20
  322.8 50.8 all-gather.18
  376.2 57.2 all-gather.16
  573.0 54.4 reduce-scatter.24
  629.6 51.2 reduce-scatter.26
  790.1 41.9 reduce-scatter.16
  834.4 44.6 reduce-scatter.28
  881.4 37.8 reduce-scatter.18
  924.5 48.3 reduce-scatter.14
  975.0 43.4 reduce-scatter.22
  1025.8 51.8 reduce-scatter.20

commit v4 on v3

--- a/solution.py
+++ b/solution.py
@@ -1225,11 +1225,13 @@
 
 def join_pairs(left, right, place, devices):
     first, second = pair_routes(devices)
-    even = place % 2 == 0
-    got_a = lax.ppermute(jnp.where(even, left, right), "ctx", [(b, a) for a, b in first])
-    got_b = lax.ppermute(jnp.where(even, right, left), "ctx", [(b, a) for a, b in second])
+    send = lambda value, routes, odd: lax.ppermute(
+        value, "ctx", [(b, a) for a, b in routes if b % 2 == odd]
+    )
     early = place < devices // 2
-    return jnp.concatenate([jnp.where(early, got_a, got_b), jnp.where(early, got_b, got_a)], axis=1)
+    low = jnp.where(early, send(left, first, 0), send(right, second, 0))
+    high = jnp.where(early, send(left, second, 1), send(right, first, 1))
+    return jnp.concatenate([low, high], axis=1)
 
 
 def pad_to(value, size, axis):

time: 1100 us -> 1090 us (level)
  waiting for transfers between devices: 223 us -> 206 us
    ppermute x2 -> x4, waiting for transfers between devices: 20.4 us -> 1.29 us  [join_pairs(): lax.ppermute(value, 'ctx', [(b, a) for a, b in routes if b % 2 == odd])]
    unnamed x270 -> x272, local copies, waits for them, and re-layouts: 48.3 us -> 48.1 us
  transfers between devices with their start and end apart: 111 -> 113, of which waited for: 42 -> 39; matrix products, arithmetic and copies ran while one was open for 23% -> 23% of each run, Pallas kernels for 40% -> 41%
where the time goes in v4:
time: 1090 us; the launch traced here: 1070 us
  Pallas kernels  462 us (42%)
  waiting for transfers between devices  206 us (19%)
  local copies, waits for them, and re-layouts  125 us (11%)
  starting transfers between devices  115 us (11%)
  matrix products  89.4 us (8%)
  other arithmetic  59.1 us (5%)
  between operations  15.8 us (1%)
    ppermute x80, waiting for transfers between devices, swap(): return lax.ppermute(value, 'ctx', [(d, d ^ mask) for d in range(CUBE)])  169 us
    pallas_call x22, Pallas kernels, whole_call(): pl.pallas_call(later(kernel, len(values), deps), out_shape=out_shape, in_...  82.3 us
    pallas_call x1, Pallas kernels, scan_backward(): pl.pallas_call(later(scan_kernel_bwd, 3 + 14, deps), out_shape=(jax.Shape...  74.8 us
    dot_general x7, matrix products, dot_tn(): lax.dot_general(left, right, (((0,), (0,)), ((), ())), preferred_element_...  63.6 us
    ppermute x80, starting transfers between devices, swap(): return lax.ppermute(value, 'ctx', [(d, d ^ mask) for d in range(CUBE)])  63.4 us
    pallas_call x2, Pallas kernels, ffn(): pl.pallas_call(functools.partial(ffn_kernel, count, model), out_shape=[ja...  54.1 us
    unnamed x272, local copies, waits for them, and re-layouts  48.1 us
    pallas_call x1, Pallas kernels, scan_forward(): pl.pallas_call(later(scan_kernel_fwd, 12, deps), out_shape=(jax.ShapeDtyp...  45.8 us
  transfers between devices with their start and end apart: 113, of which 39 were waited for; matrix products, arithmetic and copies ran while one was open for 23% of the time, Pallas kernels for 41%

profile of v4, /device:TPU:0, one launch (start us, length us, event | category | flops | bytes accessed | tf_op | source)
XLA Modules:
  0.0 1072.1 jit_solution(9433860375738186643)
XLA Ops:
  14.3 9.6 collective-permute-done.1
  39.6 5.4 collective-permute-done.3
  62.7 9.5 collective-permute-done.14
  87.8 9.2 shard_map.367.refs_1_
  102.7 8.8 convolution_convert_fusion.9.xin_ref.refs_6_
  111.5 13.3 %shard_map.370 = (f32[2048,400]{1,0:T(8,128)}, bf16[2048,400]{1,0:T(8,128)(2,1)}, bf16[2048,132]{1,0:T(8,128)(2,1)}) custom-call(s32[16]{0:T(128)} %copy-done.85, s32[16]{0:T(128)} %copy-done.97, s32[16]{0:T(128)} %copy-done.89, bf16[2048,400]{1,0:T(8,128)(2,1)} %convolution_convert_fusion.9.xin_ref.refs_6_, f32[4,400]{1,0:T(4,128)} %fusion.6.w_ref.refs_8_, ...), custom_call_target="tpu_custom_call" | custom-call | flops 1 | bytes 1 | tf_op jit(solution)/shard_map/pallas_call | solution.py:163
  132.8 8.4 convolution_convert_fusion.8.refs_4_.refs_6_
  168.3 12.0 %collective-permute-done.24 = bf16[1024,132]{1,0:T(8,128)(2,1)S(1)} collective-permute-done((bf16[1024,132]{1,0:T(8,128)(2,1)S(1)}, bf16[1024,132]{1,0:T(8,128)(2,1)S(1)}, u32[]{:S(2)}, u32[]{:S(2)}) %collective-permute-start.24) | collective-permute-done | bytes 270368 | tf_op jit(solution)/shard_map/ppermute | solution.py:1036
  203.7 45.8 %shard_map.378 = (f32[2048,400]{1,0:T(8,128)}, bf16[2048,400]{1,0:T(8,128)(2,1)}, f32[2048,128]{1,0:T(8,128)}, f32[16,128,32,128]{3,2,1,0:T(8,128)}, f32[16,128,...) custom-call(s32[16]{0:T(128)} %copy-done.85, s32[16]{0:T(128)} %copy-done.97, s32[16]{0:T(128)} %copy-done.89, ...), custom_call_target="tpu_custom_call" | custom-call | flops 1 | bytes 1 | tf_op jit(solution)/shard_map/pallas_call | solution.py:356
  251.0 10.5 shard_map.379
  262.0 8.6 convolution_convert_fusion.7.refs_2_
  270.6 5.6 shard_map.380
  295.3 31.0 %shard_map.382 = (f32[2048,256]{1,0:T(8,128)}, bf16[2048,256]{1,0:T(8,128)(2,1)}, f32[16,8,512]{2,1,0:T(8,128)}) custom-call(s32[16]{0:T(128)} %copy-done.85, s32[16]{0:T(128)} %and_select_fusion.1.refs_1_, s32[4]{0:T(128)} %subtract_clamp_fusion.refs_2_, bf16[2048,256]{1,0:T(8,128)(2,1)} %slice.326.refs_3_, ...), custom_call_target="tpu_custom_call" | custom-call | flops 1 | bytes 1 | tf_op jit(solution)/shard_map/pallas_call | solution.py:636
  326.3 5.5 collective-permute-done.33.refs_3_
  337.2 9.3 shard_map.384
  346.5 6.4 collective-permute-done.35.mate
  352.8 5.6 shard_map.385
  365.7 14.1 %collective-permute-done.26 = f32[2,256]{1,0:T(2,128)S(1)} collective-permute-done((f32[2,256]{1,0:T(2,128)S(1)}, f32[2,256]{1,0:T(2,128)S(1)}, u32[]{:S(2)}, u32[]{:S(2)}) %collective-permute-start.26) | collective-permute-done | bytes 2080 | tf_op jit(solution)/shard_map/ppermute | solution.py:1036
  392.0 12.2 %collective-permute-done.40.by_y = bf16[128,1664]{1,0:T(8,128)(2,1)S(1)} collective-permute-done((bf16[128,1664]{1,0:T(8,128)(2,1)S(1)}, bf16[128,1664]{1,0:T(8,128)(2,1)S(1)}, u32[]{:S(2)}, u32[]{:S(2)}) %collective-permute-start.40) | collective-permute-done | bytes 426016 | tf_op jit(solution)/shard_map/ppermute | solution.py:1036
  408.7 12.0 %collective-permute-done.38.by_y = bf16[128,1664]{1,0:T(8,128)(2,1)S(1)} collective-permute-done((bf16[128,1664]{1,0:T(8,128)(2,1)}, bf16[128,1664]{1,0:T(8,128)(2,1)S(1)}, u32[]{:S(2)}, u32[]{:S(2)}) %collective-permute-start.38) | collective-permute-done | bytes 426016 | tf_op jit(solution)/shard_map/ppermute | solution.py:1036
  429.3 20.0 %collective-permute-done.42.by_x.refs_1_ = bf16[256,1664]{1,0:T(8,128)(2,1)S(1)} collective-permute-done((bf16[256,1664]{1,0:T(8,128)(2,1)S(1)}, bf16[256,1664]{1,0:T(8,128)(2,1)S(1)}, u32[]{:S(2)}, u32[]{:S(2)}) %collective-permute-start.42) | collective-permute-done | bytes 852000 | tf_op jit(solution)/shard_map/ppermute | solution.py:1036
  456.0 9.2 collective-permute-done.44
  469.0 26.8 %shard_map.390 = (bf16[2048,1600]{1,0:T(8,128)(2,1)}, bf16[2048,1600]{1,0:T(8,128)(2,1)}, bf16[2048,688]{1,0:T(8,128)(2,1)}, bf16[2048,688]{1,0:T(8,128)(2,1)}, ...) custom-call(s32[8]{0:T(128)} %broadcast_xor_fusion.order, ...), custom_call_target="tpu_custom_call" | custom-call | flops 1 | bytes 1 | tf_op jit(solution)/shard_map/pallas_call | solution.py:977
  496.4 27.3 %shard_map.391 = (bf16[2048,1600]{1,0:T(8,128)(2,1)}, bf16[2048,1600]{1,0:T(8,128)(2,1)}, bf16[2048,688]{1,0:T(8,128)(2,1)}, bf16[2048,688]{1,0:T(8,128)(2,1)}, ...) custom-call(s32[8]{0:T(128)} %broadcast_xor_fusion.order, ...), custom_call_target="tpu_custom_call", output_to_operand_aliasing={{0}: (9, {}), {1}: (10, {}), {2}: (11, {}), {3}: (12, {}), ... | custom-call | flops 1 | bytes 1 | tf_op jit(solution)/shard_map/pallas_call | solution.py:977
  523.7 5.5 shard_map.393
  532.5 5.5 shard_map.392
  540.6 10.6 collective-permute-done.54.by_x
  558.9 9.6 convolution_convert_fusion.3
  590.3 10.0 convolution_convert_fusion.2
  600.3 7.1 collective-permute-done.58.by_x.refs_1_
  612.0 10.1 convolution_convert_fusion.1
  650.9 12.8 %shard_map.397 = (bf16[2048,1600]{1,0:T(8,128)(2,1)}, f32[2048,256]{1,0:T(8,128)}, f32[2048,400]{1,0:T(8,128)}) custom-call(bf16[256,1664]{1,0:T(8,128)(2,1)} %pad.21.refs_0_, bf16[256,1664]{1,0:T(8,128)(2,1)} %collective-permute-done.58.by_x.refs_1_, bf16[256,1664]{1,0:T(8,128)(2,1)} %collective-permute-done.59.by_y.refs_2_, bf16[256,1664]{1,0:T(8,128)(2,1)} %copy-done.46, ...), custom_call_target="tpu_custom_call" | custom-call | flops 1 | bytes 1 | tf_op jit(solution)/shard_map/pallas_call | solution.py:1011
  663.6 74.8 %shard_map.398 = (bf16[2048,400]{1,0:T(8,128)(2,1)}, f32[2048,400]{1,0:T(8,128)}, bf16[2048,100]{1,0:T(8,128)(2,1)}, f32[16,2,8,2048]{3,2,1,0:T(8,128)}, f32[100...) custom-call(s32[16]{0:T(128)} %copy-done.85, s32[16]{0:T(128)} %copy-done.97, s32[16]{0:T(128)} %copy-done.89, ...), custom_call_target="tpu_custom_call" | custom-call | flops 1 | bytes 1 | tf_op jit(solution)/shard_map/pallas_call | solution.py:510
  766.9 9.8 convolution_convert_fusion.refs_0_.refs_11_
  782.6 7.8 convolution_convert_fusion.6.refs_5_
  794.0 10.3 collective-permute-done.76
  822.5 33.6 %shard_map.406 = (bf16[2048,256]{1,0:T(8,128)(2,1)}, f32[2048,128]{1,0:T(8,128)}, f32[2048,128]{1,0:T(8,128)}) custom-call(s32[16]{0:T(128)} %copy-done.85, s32[16]{0:T(128)} %and_select_fusion.1.refs_1_, s32[4]{0:T(128)} %subtract_clamp_fusion.refs_2_, bf16[2048,256]{1,0:T(8,128)(2,1)} %slice.326.refs_3_, f32[2048,256]{1,0:T(8,128)} %get-tuple-element.224.refs_4_, ...), custom_call_target="tpu_custom_call" | custom-call | flops 1 | bytes 1 | tf_op jit(solution)/shard_map/pallas_call | solution.py:716
  870.7 8.4 convolution_convert_fusion.5.refs_4_
  883.7 12.9 %shard_map.410.refs_10_.refs_2_ = bf16[2048,1664]{1,0:T(8,128)(2,1)} custom-call(bf16[2048,512]{1,0:T(8,128)(2,1)} %shard_map.409.refs_0_, bf16[2048,400]{1,0:T(8,128)(2,1)} %get-tuple-element.238.refs_1_, bf16[1600,512]{1,0:T(8,128)(2,1)} %all-gather.15.cloned.1.call-done.refs_2_, bf16[1600,400]{1,0:T(8,128)(2,1)} %get-tuple-element.362.refs_3_, ...), custom_call_target="tpu_custom_call" | custom-call | flops 1 | bytes 1 | tf_op jit(solution)/shard_map/pallas_call | solution.py:925
  896.6 17.5 %shard_map.411 = (bf16[2048,400]{1,0:T(8,128)(2,1)}, f32[8,400]{1,0:T(8,128)}, f32[132,400]{1,0:T(8,128)}) custom-call(s32[16]{0:T(128)} %copy-done.85, s32[16]{0:T(128)} %copy-done.97, s32[16]{0:T(128)} %copy-done.89, bf16[2048,132]{1,0:T(8,128)(2,1)} %pad_maximum_fusion.3.refs_1_.refs_10_.refs_3_, f32[2048,400]{1,0:T(8,128)} %get-tuple-element.234.refs_4_, ...), custom_call_target="tpu_custom_call" | custom-call | flops 1 | bytes 1 | tf_op jit(solution)/shard_map/pallas_call | solution.py:228
  914.1 11.7 %shard_map.412 = (bf16[1024,1664]{1,0:T(8,128)(2,1)}, bf16[1024,1664]{1,0:T(8,128)(2,1)}) custom-call(bf16[2048,400]{1,0:T(8,128)(2,1)} %get-tuple-element.239.refs_0_, bf16[1600,400]{1,0:T(8,128)(2,1)} %get-tuple-element.361.refs_1_, bf16[2048,1664]{1,0:T(8,128)(2,1)} %shard_map.410.refs_10_.refs_2_), custom_call_target="tpu_custom_call" | custom-call | flops 1 | bytes 1 | tf_op jit(solution)/shard_map/pallas_call | solution.py:925
  926.1 6.1 collective-permute-done.80.mate
  932.2 6.0 shard_map.413
  952.9 6.5 collective-permute-done.81.by_x
  965.6 7.8 convolution_convert_fusion.4
  1001.1 7.6 all-to-all-start.4
  1035.9 5.6 collective-permute-done.90
  1052.0 11.5 %reduce-scatter.21.cloned.1.call-done = bf16[1,400,280]{1,2,0:T(8,128)(2,1)} async-done(((bf16[8,400,280]{1,2,0:T(8,128)(2,1)}), bf16[1,400,280]{1,2,0:T(8,128)(2,1)}) %reduce-scatter.21.cloned.1.call-update) | async-done | bytes 224016 | tf_op jit(solution)/shard_map/reduce_scatter | solution.py:1570
  (711 shorter events, 421.0 us)
Async XLA Ops:
  7.2 95.5 %all-gather.13.cloned.1.call-start = ((), (), s32[]{:S(2)}) async-start(), calls=%async_computation.13 | async-start | bytes 3584000 | tf_op jit(solution)/shard_map/all_gather | solution.py:1173
  25.2 124.7 %all-gather.27.cloned.1.call-start = ((), (), s32[]{:S(2)}) async-start(), calls=%async_computation.25 | async-start | bytes 2580480 | tf_op jit(solution)/shard_map/all_gather | solution.py:1337
  29.1 25.8 %collective-permute-start.12 = (bf16[256,1664]{1,0:T(8,128)(2,1)}, bf16[256,1664]{1,0:T(8,128)(2,1)S(1)}, u32[]{:S(2)}, u32[]{:S(2)}) collective-permute-start(bf16[256,1664]{1,0:T(8,128)(2,1)} %pad.18.refs_0_), channel_id=1, source_target_pairs={{0,8},{4,12},{8,0},{12,4},{16,24},{20,28},{24,16},{28,20},{1,9},{5... | collective-permute-start | bytes 2555912 | tf_op jit(solution)/shard_map/ppermute | solution.py:1036
  30.9 26.0 %collective-permute-start.13 = (bf16[256,1664]{1,0:T(8,128)(2,1)}, bf16[256,1664]{1,0:T(8,128)(2,1)S(1)}, u32[]{:S(2)}, u32[]{:S(2)}) collective-permute-start(bf16[256,1664]{1,0:T(8,128)(2,1)} %pad.18.refs_0_), channel_id=1, source_target_pairs={{0,16},{4,20},{8,24},{12,28},{16,0},{20,4},{24,8},{28,12},{1,17},{... | collective-permute-start | bytes 2555912 | tf_op jit(solution)/shard_map/ppermute | solution.py:1036
  39.6 48.1 %collective-permute-start.16 = (bf16[256,1664]{1,0:T(8,128)(2,1)}, bf16[256,1664]{1,0:T(8,128)(2,1)}, u32[]{:S(2)}, u32[]{:S(2)}) collective-permute-start(bf16[256,1664]{1,0:T(8,128)(2,1)} %pad.18.refs_0_), channel_id=1, source_target_pairs={{0,4},{4,0},{8,12},{12,8},{16,20},{20,16},{24,28},{28,24},{1,5},{5... | collective-permute-start | bytes 2555912 | tf_op jit(solution)/shard_map/ppermute | solution.py:1036
  100.6 82.9 %all-gather.23.cloned.1.call-start = ((), (), s32[]{:S(2)}) async-start(), calls=%async_computation.23 | async-start | bytes 2560000 | tf_op jit(solution)/shard_map/all_gather | solution.py:1327
  102.1 159.8 %all-gather.15.cloned.1.call-start = ((), (), s32[]{:S(2)}) async-start(), calls=%async_computation.14 | async-start | bytes 2048000 | tf_op jit(solution)/shard_map/all_gather | solution.py:1173
  157.2 119.0 %all-gather.25.cloned.1.call-start = ((), (), s32[]{:S(2)}) async-start(), calls=%async_computation.24 | async-start | bytes 2816000 | tf_op jit(solution)/shard_map/all_gather | solution.py:1373
  162.6 304.4 %all-gather.21.cloned.1.call-start = ((), (), s32[]{:S(2)}) async-start(), calls=%async_computation.17 | async-start | bytes 3072000 | tf_op jit(solution)/shard_map/all_gather | solution.py:1173
  187.1 62.4 %all-to-all-start = ((bf16[8,200,656]{2,1,0:T(8,128)(2,1)}), bf16[8,200,656]{2,1,0:T(8,128)(2,1)S(1)}, u32[]{:S(2)}, u32[]{:S(2)}) async-start(bf16[8,200,656]{2,1,0:T(8,128)(2,1)} %shard_map.373.refs_12_), calls=%async_computation | async-start | bytes 4915200 | tf_op jit(solution)/shard_map/all_to_all | solution.py:1119
  190.9 276.2 %all-gather.19.cloned.1.call-start = ((), (), s32[]{:S(2)}) async-start(), calls=%async_computation.16 | async-start | bytes 3072000 | tf_op jit(solution)/shard_map/all_gather | solution.py:1173
  191.6 275.5 %all-gather.17.cloned.1.call-start = ((), (), s32[]{:S(2)}) async-start(), calls=%async_computation.15 | async-start | bytes 7667712 | tf_op jit(solution)/shard_map/all_gather | solution.py:1371
  279.8 56.0 %all-to-all-start.1 = ((bf16[8,200,688]{2,1,0:T(8,128)(2,1)}), bf16[8,200,688]{2,1,0:T(8,128)(2,1)S(1)}, u32[]{:S(2)}, u32[]{:S(2)}) async-start(bf16[8,200,688]{2,1,0:T(8,128)(2,1)} %shard_map.381.refs_8_), calls=%async_computation.1 | async-start | bytes 4915200 | tf_op jit(solution)/shard_map/all_to_all | solution.py:1119
  283.8 663.5 %reduce-scatter.25.cloned.1.call-start = ((), (), s32[]{:S(2)}) async-start(), calls=%async_computation.26 | async-start | bytes 3072000
  284.3 47.5 %collective-permute-start.33 = (bf16[256,1664]{1,0:T(8,128)(2,1)}, bf16[256,1664]{1,0:T(8,128)(2,1)}, u32[]{:S(2)}, u32[]{:S(2)}) collective-permute-start(bf16[256,1664]{1,0:T(8,128)(2,1)} %get-tuple-element.160), channel_id=1, source_target_pairs={{0,8},{4,12},{8,0},{12,4},{16,24},{20,28},{24,16},{28,20},{1,9},{5... | collective-permute-start | bytes 2555912 | tf_op jit(solution)/shard_map/ppermute | solution.py:1036
  286.3 45.5 %collective-permute-start.34 = (bf16[256,1664]{1,0:T(8,128)(2,1)}, bf16[256,1664]{1,0:T(8,128)(2,1)}, u32[]{:S(2)}, u32[]{:S(2)}) collective-permute-start(bf16[256,1664]{1,0:T(8,128)(2,1)} %get-tuple-element.161), channel_id=1, source_target_pairs={{0,16},{4,20},{8,24},{12,28},{16,0},{20,4},{24,8},{28,12},{1,17},{... | collective-permute-start | bytes 2555912 | tf_op jit(solution)/shard_map/ppermute | solution.py:1036
  358.5 22.8 %collective-permute-start.36 = (bf16[256,1664]{1,0:T(8,128)(2,1)}, bf16[256,1664]{1,0:T(8,128)(2,1)S(1)}, u32[]{:S(2)}, u32[]{:S(2)}) collective-permute-start(bf16[256,1664]{1,0:T(8,128)(2,1)} %get-tuple-element.168), channel_id=1, source_target_pairs={{0,8},{4,12},{8,0},{12,4},{16,24},{20,28},{24,16},{28,20},{1,9},{5... | collective-permute-start | bytes 2555912 | tf_op jit(solution)/shard_map/ppermute | solution.py:1036
  359.8 22.9 %collective-permute-start.37 = (bf16[256,1664]{1,0:T(8,128)(2,1)}, bf16[256,1664]{1,0:T(8,128)(2,1)S(1)}, u32[]{:S(2)}, u32[]{:S(2)}) collective-permute-start(bf16[256,1664]{1,0:T(8,128)(2,1)} %get-tuple-element.169), channel_id=1, source_target_pairs={{0,16},{4,20},{8,24},{12,28},{16,0},{20,4},{24,8},{28,12},{1,17},{... | collective-permute-start | bytes 2555912 | tf_op jit(solution)/shard_map/ppermute | solution.py:1036
  364.2 23.7 %collective-permute-start.28 = (f32[2,256]{1,0:T(2,128)S(1)}, f32[2,256]{1,0:T(2,128)S(1)}, u32[]{:S(2)}, u32[]{:S(2)}) collective-permute-start(f32[2,256]{1,0:T(2,128)S(1)} %bitcast.279), channel_id=1, source_target_pairs={{0,24},{4,28},{8,16},{12,20},{16,8},{20,12},{24,0},{28,4},{1,25},{... | collective-permute-start | bytes 6152 | tf_op jit(solution)/shard_map/ppermute | solution.py:1036
  390.1 30.5 %collective-permute-start.38 = (bf16[128,1664]{1,0:T(8,128)(2,1)}, bf16[128,1664]{1,0:T(8,128)(2,1)S(1)}, u32[]{:S(2)}, u32[]{:S(2)}) collective-permute-start(bf16[128,1664]{1,0:T(8,128)(2,1)} %get-tuple-element.171), channel_id=1, source_target_pairs={{0,16},{4,20},{8,24},{12,28},{16,0},{20,4},{24,8},{28,12},{1,17},{... | collective-permute-start | bytes 1277960 | tf_op jit(solution)/shard_map/ppermute | solution.py:1036
  391.2 29.5 %collective-permute-start.39 = (bf16[128,1664]{1,0:T(8,128)(2,1)}, bf16[128,1664]{1,0:T(8,128)(2,1)S(1)}, u32[]{:S(2)}, u32[]{:S(2)}) collective-permute-start(bf16[128,1664]{1,0:T(8,128)(2,1)} %get-tuple-element.172), channel_id=1, source_target_pairs={{0,8},{4,12},{8,0},{12,4},{16,24},{20,28},{24,16},{28,20},{1,9},{5... | collective-permute-start | bytes 1277960 | tf_op jit(solution)/shard_map/ppermute | solution.py:1036
  427.2 22.1 %collective-permute-start.42 = (bf16[256,1664]{1,0:T(8,128)(2,1)S(1)}, bf16[256,1664]{1,0:T(8,128)(2,1)S(1)}, u32[]{:S(2)}, u32[]{:S(2)}) collective-permute-start(bf16[256,1664]{1,0:T(8,128)(2,1)S(1)} %pad.20.refs_0_), channel_id=1, source_target_pairs={{0,8},{4,12},{8,0},{12,4},{16,24},{20,28},{24,16},{28,20},{1,9},{5... | collective-permute-start | bytes 2555912 | tf_op jit(solution)/shard_map/ppermute | solution.py:1036
  495.8 27.9 %collective-permute-start.53 = (bf16[1024,1664]{1,0:T(8,128)(2,1)}, bf16[1024,1664]{1,0:T(8,128)(2,1)}, u32[]{:S(2)}, u32[]{:S(2)}) collective-permute-start(bf16[1024,1664]{1,0:T(8,128)(2,1)} %get-tuple-element.190), channel_id=1, source_target_pairs={{0,4},{4,0},{8,12},{12,8},{16,20},{20,16},{24,28},{28,24},{1,5},{5... | collective-permute-start | bytes 10223624 | tf_op jit(solution)/shard_map/ppermute | solution.py:1036
  496.0 34.8 %collective-permute-start.50 = (bf16[1024,1664]{1,0:T(8,128)(2,1)}, bf16[1024,1664]{1,0:T(8,128)(2,1)S(1)}, u32[]{:S(2)}, u32[]{:S(2)}) collective-permute-start(bf16[1024,1664]{1,0:T(8,128)(2,1)} %get-tuple-element.183), channel_id=1, source_target_pairs={{0,4},{4,0},{8,12},{12,8},{16,20},{20,16},{24,28},{28,24},{1,5},{5... | collective-permute-start | bytes 10223624 | tf_op jit(solution)/shard_map/ppermute | solution.py:1036
  529.2 22.0 %collective-permute-start.54 = (bf16[256,1664]{1,0:T(8,128)(2,1)}, bf16[256,1664]{1,0:T(8,128)(2,1)S(1)}, u32[]{:S(2)}, u32[]{:S(2)}) collective-permute-start(bf16[256,1664]{1,0:T(8,128)(2,1)} %get-tuple-element.194), channel_id=1, source_target_pairs={{0,8},{4,12},{8,0},{12,4},{16,24},{20,28},{24,16},{28,20},{1,9},{5... | collective-permute-start | bytes 2555912 | tf_op jit(solution)/shard_map/ppermute | solution.py:1036
  529.9 22.0 %collective-permute-start.55 = (bf16[256,1664]{1,0:T(8,128)(2,1)}, bf16[256,1664]{1,0:T(8,128)(2,1)S(1)}, u32[]{:S(2)}, u32[]{:S(2)}) collective-permute-start(bf16[256,1664]{1,0:T(8,128)(2,1)} %get-tuple-element.195), channel_id=1, source_target_pairs={{0,16},{4,20},{8,24},{12,28},{16,0},{20,4},{24,8},{28,12},{1,17},{... | collective-permute-start | bytes 2555912 | tf_op jit(solution)/shard_map/ppermute | solution.py:1036
  538.1 200.4 %collective-permute-start.51 = (bf16[256,1664]{1,0:T(8,128)(2,1)}, bf16[256,1664]{1,0:T(8,128)(2,1)}, u32[]{:S(2)}, u32[]{:S(2)}) collective-permute-start(bf16[256,1664]{1,0:T(8,128)(2,1)} %get-tuple-element.187), channel_id=1, source_target_pairs={{0,8},{4,12},{8,0},{12,4},{16,24},{20,28},{24,16},{28,20},{1,9},{5... | collective-permute-start | bytes 2555912 | tf_op jit(solution)/shard_map/ppermute | solution.py:1036
  539.1 199.3 %collective-permute-start.52 = (bf16[256,1664]{1,0:T(8,128)(2,1)}, bf16[256,1664]{1,0:T(8,128)(2,1)}, u32[]{:S(2)}, u32[]{:S(2)}) collective-permute-start(bf16[256,1664]{1,0:T(8,128)(2,1)} %get-tuple-element.188), channel_id=1, source_target_pairs={{0,16},{4,20},{8,24},{12,28},{16,0},{20,4},{24,8},{28,12},{1,17},{... | collective-permute-start | bytes 2555912 | tf_op jit(solution)/shard_map/ppermute | solution.py:1036
  556.9 21.2 %collective-permute-start.56 = (bf16[128,1664]{1,0:T(8,128)(2,1)}, bf16[128,1664]{1,0:T(8,128)(2,1)S(1)}, u32[]{:S(2)}, u32[]{:S(2)}) collective-permute-start(bf16[128,1664]{1,0:T(8,128)(2,1)} %get-tuple-element.197), channel_id=1, source_target_pairs={{0,16},{4,20},{8,24},{12,28},{16,0},{20,4},{24,8},{28,12},{1,17},{... | collective-permute-start | bytes 1277960 | tf_op jit(solution)/shard_map/ppermute | solution.py:1036
  573.0 376.5 %reduce-scatter.27.cloned.1.call-start = ((), (), s32[]{:S(2)}) async-start(), calls=%async_computation.27 | async-start | bytes 3072000
  589.2 40.2 %collective-permute-start.66 = (f32[4,256]{1,0:T(4,128)S(1)}, f32[4,256]{1,0:T(4,128)S(1)}, u32[]{:S(2)}, u32[]{:S(2)}) collective-permute-start(f32[4,256]{1,0:T(4,128)S(1)} %pad_maximum_fusion.8), channel_id=1, source_target_pairs={{0,8},{4,12},{8,0},{12,4},{16,24},{20,28},{24,16},{28,20},{1,9},{5... | collective-permute-start | bytes 12296 | tf_op jit(solution)/shard_map/ppermute | solution.py:1036
  640.8 105.9 %all-to-all-start.2 = ((bf16[8,200,688]{2,1,0:T(8,128)(2,1)}), bf16[8,200,688]{2,1,0:T(8,128)(2,1)}, u32[]{:S(2)}, u32[]{:S(2)}) async-start(bf16[8,200,688]{2,1,0:T(8,128)(2,1)} %bitcast.235), calls=%async_computation.2 | async-start | bytes 4915200 | tf_op jit(solution)/shard_map/all_to_all | solution.py:1119
  645.2 328.3 %reduce-scatter.17.cloned.1.call-start = ((), (), s32[]{:S(2)}) async-start(), calls=%async_computation.19 | async-start | bytes 2048000 | tf_op jit(solution)/shard_map/reduce_scatter | solution.py:1177
  790.4 183.1 %reduce-scatter.29.cloned.1.call-start = ((), (), s32[]{:S(2)}) async-start(), calls=%async_computation.28 | async-start | bytes 2816000
  810.0 46.0 %all-to-all-start.3 = ((bf16[8,200,656]{2,1,0:T(8,128)(2,1)}), bf16[8,200,656]{2,1,0:T(8,128)(2,1)}, u32[]{:S(2)}, u32[]{:S(2)}) async-start(bf16[8,200,656]{2,1,0:T(8,128)(2,1)} %bitcast.236), calls=%async_computation.3 | async-start | bytes 4915200 | tf_op jit(solution)/shard_map/all_to_all | solution.py:1119
  814.4 159.1 %reduce-scatter.19.cloned.1.call-start = ((), (), s32[]{:S(2)}) async-start(), calls=%async_computation.20 | async-start | bytes 2048000 | tf_op jit(solution)/shard_map/reduce_scatter | solution.py:1177
  816.3 43.4 %collective-permute-start.79 = (bf16[128,1664]{1,0:T(8,128)(2,1)}, bf16[128,1664]{1,0:T(8,128)(2,1)S(1)}, u32[]{:S(2)}, u32[]{:S(2)}) collective-permute-start(bf16[128,1664]{1,0:T(8,128)(2,1)} %shard_map.404), channel_id=1, source_target_pairs={{0,8},{4,12},{8,0},{12,4},{16,24},{20,28},{24,16},{28,20},{1,9},{5... | collective-permute-start | bytes 1277960 | tf_op jit(solution)/shard_map/ppermute | solution.py:1036
  820.0 39.7 %collective-permute-start.78 = (bf16[128,1664]{1,0:T(8,128)(2,1)}, bf16[128,1664]{1,0:T(8,128)(2,1)S(1)}, u32[]{:S(2)}, u32[]{:S(2)}) collective-permute-start(bf16[128,1664]{1,0:T(8,128)(2,1)} %shard_map.403), channel_id=1, source_target_pairs={{0,16},{4,20},{8,24},{12,28},{16,0},{20,4},{24,8},{28,12},{1,17},{... | collective-permute-start | bytes 1277960 | tf_op jit(solution)/shard_map/ppermute | solution.py:1036
  879.1 94.4 %reduce-scatter.15.cloned.1.call-start = ((), (), s32[]{:S(2)}) async-start(), calls=%async_computation.18 | async-start | bytes 2560000 | tf_op jit(solution)/shard_map/reduce_scatter | solution.py:1528
  925.8 119.2 %reduce-scatter.23.cloned.1.call-start = ((), (), s32[]{:S(2)}) async-start(), calls=%async_computation.22 | async-start | bytes 2048000 | tf_op jit(solution)/shard_map/reduce_scatter | solution.py:1177
  938.1 21.3 %collective-permute-start.81 = (bf16[256,1664]{1,0:T(8,128)(2,1)}, bf16[256,1664]{1,0:T(8,128)(2,1)}, u32[]{:S(2)}, u32[]{:S(2)}) collective-permute-start(bf16[256,1664]{1,0:T(8,128)(2,1)} %get-tuple-element.245), channel_id=1, source_target_pairs={{0,8},{4,12},{8,0},{12,4},{16,24},{20,28},{24,16},{28,20},{1,9},{5... | collective-permute-start | bytes 2555912 | tf_op jit(solution)/shard_map/ppermute | solution.py:1036
  938.3 21.1 %collective-permute-start.82 = (bf16[256,1664]{1,0:T(8,128)(2,1)}, bf16[256,1664]{1,0:T(8,128)(2,1)}, u32[]{:S(2)}, u32[]{:S(2)}) collective-permute-start(bf16[256,1664]{1,0:T(8,128)(2,1)} %get-tuple-element.246), channel_id=1, source_target_pairs={{0,16},{4,20},{8,24},{12,28},{16,0},{20,4},{24,8},{28,12},{1,17},{... | collective-permute-start | bytes 2555912 | tf_op jit(solution)/shard_map/ppermute | solution.py:1036
  963.6 23.2 %collective-permute-start.83 = (bf16[128,1664]{1,0:T(8,128)(2,1)}, bf16[128,1664]{1,0:T(8,128)(2,1)}, u32[]{:S(2)}, u32[]{:S(2)}) collective-permute-start(bf16[128,1664]{1,0:T(8,128)(2,1)} %get-tuple-element.248), channel_id=1, source_target_pairs={{0,16},{4,20},{8,24},{12,28},{16,0},{20,4},{24,8},{28,12},{1,17},{... | collective-permute-start | bytes 1277960 | tf_op jit(solution)/shard_map/ppermute | solution.py:1036
  963.8 22.9 %collective-permute-start.84 = (bf16[128,1664]{1,0:T(8,128)(2,1)}, bf16[128,1664]{1,0:T(8,128)(2,1)}, u32[]{:S(2)}, u32[]{:S(2)}) collective-permute-start(bf16[128,1664]{1,0:T(8,128)(2,1)} %get-tuple-element.249), channel_id=1, source_target_pairs={{0,8},{4,12},{8,0},{12,4},{16,24},{20,28},{24,16},{28,20},{1,9},{5... | collective-permute-start | bytes 1277960 | tf_op jit(solution)/shard_map/ppermute | solution.py:1036
  973.5 75.7 %collective-permute-start.86 = (bf16[400,400]{1,0:T(8,128)(2,1)}, bf16[400,400]{1,0:T(8,128)(2,1)}, u32[]{:S(2)}, u32[]{:S(2)}) collective-permute-start(bf16[400,400]{1,0:T(8,128)(2,1)} %reduce-scatter.17.cloned.1.call-done), channel_id=1, source_target_pairs={{0,16},{8,20},{16,24},{24,28},{1,17},{9,21},{17,25},{25,29},{2,18}... | collective-permute-start | bytes 960008 | tf_op jit(solution)/shard_map/ppermute | solution.py:1228
  978.1 71.2 %collective-permute-start.88 = (bf16[400,400]{1,0:T(8,128)(2,1)}, bf16[400,400]{1,0:T(8,128)(2,1)}, u32[]{:S(2)}, u32[]{:S(2)}) collective-permute-start(bf16[400,400]{1,0:T(8,128)(2,1)} %reduce-scatter.17.cloned.1.call-done), channel_id=1, source_target_pairs={{4,16},{12,20},{20,24},{28,28},{5,17},{13,21},{21,25},{29,29},{6,1... | collective-permute-start | bytes 960008 | tf_op jit(solution)/shard_map/ppermute | solution.py:1228
  1001.1 45.5 %all-to-all-start.4 = ((bf16[32,35,200]{2,1,0:T(8,128)(2,1)}), bf16[32,35,200]{2,1,0:T(8,128)(2,1)S(1)}, u32[]{:S(2)}, u32[]{:S(2)}) async-start(bf16[32,35,200]{2,1,0:T(8,128)(2,1)} %bitcast.76.refs_1_), calls=%async_computation.4 | async-start | bytes 1310720 | tf_op jit(solution)/shard_map/all_to_all | solution.py:1605
  1008.7 54.8 %reduce-scatter.21.cloned.1.call-start = ((), (), s32[]{:S(2)}) async-start(), calls=%async_computation.21 | async-start | bytes 2580480 | tf_op jit(solution)/shard_map/reduce_scatter | solution.py:1570
  (184 other events, 2268.2 us)
Sparse Core Ops, SparseCore 0:
  25.3 64.4 all-gather.12
  100.7 32.3 all-gather.26
  134.7 44.9 all-gather.22
  181.1 36.9 all-gather.14
  220.1 47.5 all-gather.24
  269.7 50.9 all-gather.20
  322.8 50.8 all-gather.18
  376.2 57.5 all-gather.16
  573.2 52.9 reduce-scatter.24
  628.3 51.2 reduce-scatter.26
  790.5 40.1 reduce-scatter.16
  833.0 44.7 reduce-scatter.28
  880.1 37.7 reduce-scatter.18
  925.9 45.5 reduce-scatter.14
  973.7 39.4 reduce-scatter.22
  1019.9 43.5 reduce-scatter.20
